TPU v7x, 32 devices: a whole 2x2x4 slice. The times are simulated.
32 devices in a mesh: seq: 8 (over y, x, core), head: 4 (over z).
Axes of the slice: x: 2, y: 2, z: 4, core: 2. Of those that a mesh axis runs over, the one named last changes fastest.
Arguments:
- queries: bfloat16 [2048, 5120], P(('seq', 'head')), may hold values from -12 to 12
- keys: bfloat16 [2048, 5120], P(('seq', 'head')), may hold values from -12 to 12
- values: bfloat16 [2048, 5120], P(('seq', 'head')), may hold values from -6 to 6
- out_grad: bfloat16 [2048, 5120], P(('seq', 'head')), may hold values from -6 to 6
- chain_lengths: int32 [16], replicated, may hold values from 1 to 512, 2048 in all
- block_pairs: int32 [16, 4], replicated, may hold values from -1 to 15, as said below
Outputs:
- attn_out: bfloat16 [2048, 5120], P(('seq', 'head'))
- query_grad: bfloat16 [2048, 5120], P(('seq', 'head'))
- key_grad: bfloat16 [2048, 5120], P(('seq', 'head'))
- value_grad: bfloat16 [2048, 5120], P(('seq', 'head'))
Inputs may be any that keep to these rules, and one draw needn't show every extreme that they name: `block_pairs`: row q lists the key blocks that query block q attends to. Slot 0 holds q itself; the other live entries are distinct blocks of the same or an adjacent sequence shard of 256 tokens, in no particular order; empty slots hold -1 and follow the live ones. Every row has 2 or more live entries, and in every draw some row has 4.
All inputs are finite; a program needn't handle non-finite values.
Results may differ from a plain program's by a relative error of at most 0.023.
Values may be sent and summed in bfloat16 or wider, within the bound.
No kernel may reach another device: no remote copies, remote signals or barrier semaphores. Data moves between devices by JAX's collectives and lax.ppermute only.
A program may use at most 128 MiB of HBM per device.

v0:
```python
import functools
import math

import jax
import jax.numpy as jnp
from jax import lax
from jax.experimental import pallas as pl
from jax.experimental.pallas import tpu as pltpu
from jax.sharding import PartitionSpec as P

HEAD_SIZE = 128
BLOCK_TOKENS = 128
HALF = HEAD_SIZE // 2
SCALE = 1.0 / math.sqrt(HEAD_SIZE)
VMEM_LIMIT = 32 * 1024 * 1024
WIDE_LIMIT = 60 * 1024 * 1024

masked_score = -1e30
rotary_base = 10000.0

SMEM_SPEC = pl.BlockSpec(memory_space=pltpu.SMEM)


def cost(flops, moved, exps=0):
    return pl.CostEstimate(flops=flops, bytes_accessed=moved, transcendentals=exps)


def params(limit=VMEM_LIMIT):
    return pltpu.CompilerParams(vmem_limit_bytes=limit)


def behind(kernel, count):
    def run(*refs):
        kernel(*refs[count:])

    return run if count else kernel


ANY_SPEC = pl.BlockSpec(memory_space=pl.ANY)
HBM_SPEC = pl.BlockSpec(memory_space=pltpu.HBM)
VMEM_SPEC = pl.BlockSpec(memory_space=pltpu.VMEM)


def chain_angles(lengths, first_row, shape, tokens):
    row = first_row + lax.broadcasted_iota(jnp.int32, shape, tokens)

    def look(c, carry):
        start, begin = carry
        return start + lengths[c], jnp.maximum(begin, jnp.where(row >= start, start, 0))

    _, begin = lax.fori_loop(
        0, lengths.shape[0], look, (jnp.int32(0), jnp.zeros(shape, jnp.int32))
    )
    entry = lax.broadcasted_iota(jnp.int32, shape, 1 - tokens)
    column = jnp.where(entry < HALF, entry, entry - HALF).astype(jnp.float32)
    frequency = jnp.exp(column * (-2.0 * math.log(rotary_base) / HEAD_SIZE))
    return (row - begin).astype(jnp.float32) * frequency, entry


def fill_tables(lengths, first_row, cosine, sine, scale=1.0):
    angle, entry = chain_angles(lengths, first_row, cosine.shape, 0)
    turn = jnp.sin(angle) * scale
    cosine[...] = jnp.cos(angle) * scale
    sine[...] = jnp.where(entry < HALF, -turn, turn)


def rotate(x, cosine, sine):
    return x * cosine + pltpu.roll(x, HALF, 1) * sine


def unrotate(g, cosine, sine):
    return g * cosine - pltpu.roll(g, HALF, 1) * sine


def views(meta, refs):
    if len(refs) == 1:
        return [(refs[0].at[i], i) for i in range(refs[0].shape[0])]
    return [(ref, jnp.bitwise_xor(meta[0], k)) for k, ref in enumerate(refs)]


def start_of(index, size):
    return pl.ds(index * size if isinstance(index, int) else pl.multiple_of(index * size, size), size)


def set_shapes(joined, n, shape, dtype=jnp.bfloat16):
    if joined:
        return [jax.ShapeDtypeStruct((n,) + shape, dtype)]
    return [jax.ShapeDtypeStruct(shape, dtype)] * n


def set_specs(joined, n, shape, index_map):
    if joined:
        return [pl.BlockSpec((n,) + shape, lambda *i: (0,) + index_map(*i))]
    return [pl.BlockSpec(shape, index_map)] * n


def dot(a, b, contract):
    return lax.dot_general(a, b, (contract, ((), ())), preferred_element_type=jnp.float32)


def cut_kernel(n, meta, lengths, turned, plain, *refs):
    pieces, (held, cosine, sine, sems) = refs[-4 - n : -4], refs[-4:]
    rows, width = turned.shape[0], held.shape[2]
    copies = []
    for step, piece in enumerate(pieces):
        lanes = start_of(jnp.bitwise_xor(meta[0], step), width)
        copies.append(
            (
                pltpu.make_async_copy(turned.at[:, lanes], held.at[step], sems.at[step, 0]),
                pltpu.make_async_copy(plain.at[:, lanes], piece.at[1], sems.at[step, 1]),
            )
        )
    for t in range(2):
        for step in range(n):
            copies[step][t].start()
    fill_tables(lengths, meta[1] * (rows * n) + meta[0] * rows, cosine, sine)
    for step, piece in enumerate(pieces):
        copies[step][0].wait()
        for h in range(0, width, HEAD_SIZE):
            lanes = slice(h, h + HEAD_SIZE)
            x = held[step, :, lanes].astype(jnp.float32)
            piece[0, :, lanes] = rotate(x, cosine[...], sine[...]).astype(jnp.bfloat16)
    for step in range(n):
        copies[step][1].wait()


def cut(meta, lengths, turned, plain, n, after=()):
    rows, width = turned.shape[0], turned.shape[1] // n
    return pl.pallas_call(
        functools.partial(cut_kernel, n),
        out_shape=[jax.ShapeDtypeStruct((2, rows, width), jnp.bfloat16)] * n,
        in_specs=[SMEM_SPEC] * 2 + [HBM_SPEC] * 2 + [ANY_SPEC] * len(after),
        out_specs=[VMEM_SPEC] * n,
        scratch_shapes=[
            pltpu.VMEM((n, rows, width), jnp.bfloat16),
            pltpu.VMEM((rows, HEAD_SIZE), jnp.float32),
            pltpu.VMEM((rows, HEAD_SIZE), jnp.float32),
            pltpu.SemaphoreType.DMA((n, 2)),
        ],
        compiler_params=params(WIDE_LIMIT),
        cost_estimate=cost(0, 8 * n * rows * width),
        name="cut",
    )(meta, lengths, turned, plain, *after)


def tables_kernel(meta, lengths, cosine, sine, half_cosine, half_sine):
    first = meta[1] * cosine.shape[0]
    fill_tables(lengths, first, cosine, sine, SCALE)
    angle, _ = chain_angles(lengths, first, half_cosine.shape, 1)
    half_cosine[...] = jnp.cos(angle) * SCALE
    half_sine[...] = jnp.sin(angle) * SCALE


def tables(meta, lengths, length):
    return pl.pallas_call(
        tables_kernel,
        out_shape=[jax.ShapeDtypeStruct((length, HEAD_SIZE), jnp.float32)] * 2
        + [jax.ShapeDtypeStruct((HALF, length), jnp.float32)] * 2,
        in_specs=[SMEM_SPEC] * 2,
        compiler_params=params(),
        cost_estimate=cost(0, 8 * length * HEAD_SIZE),
        name="tables",
    )(meta, lengths)


def order_kernel(meta, *refs):
    out = refs[-1]
    for piece, index in views(meta, refs[:-1]):
        out[:, start_of(index, piece.shape[1]), :] = piece[...]


def order(meta, pieces, n, after=()):
    _, rows, width = pieces[0].shape[-3:]
    return pl.pallas_call(
        behind(order_kernel, len(after)),
        grid=(1,),
        out_shape=jax.ShapeDtypeStruct((2, n * rows, width), pieces[0].dtype),
        in_specs=[ANY_SPEC] * len(after)
        + [SMEM_SPEC]
        + set_specs(len(pieces) == 1, n, (2, rows, width), lambda i: (0, 0, 0)),
        out_specs=pl.BlockSpec((2, n * rows, width), lambda i: (0, 0, 0)),
        compiler_params=params(),
        cost_estimate=cost(0, 8 * n * rows * width),
        name="order",
    )(*after, meta, *pieces)


def attend_kernel(count, heads, meta, listed, half_cosine, half_sine, low, mid, high, *refs):
    inputs, results = views(meta, refs[:count]), views(meta, refs[count:-7])
    lower, upper, own, query_s, grad_s, out_s, back_s = refs[-7:]
    length = mid.shape[1]
    nblk = length // BLOCK_TOKENS
    for piece, index in inputs:
        place = start_of(index, piece.shape[1])
        query_s[place, :] = piece[0]
        grad_s[place, :] = piece[1]
    first = meta[1] * nblk
    query_block = lax.broadcasted_iota(jnp.int32, (1, length), 1) // BLOCK_TOKENS
    addends = []
    for key_block in range(3 * nblk):
        addend = jnp.zeros((1, length), jnp.float32)
        for block in range(nblk):
            times = jnp.int32(0)
            for p in range(listed.shape[1]):
                same = listed[first + block, p] == first + key_block - nblk
                times += jnp.where(same & (listed[first + block, p] >= 0), 1, 0)
            addend = jnp.where(query_block == block, times.astype(jnp.float32), addend)
        addends.append(jnp.where(addend > 0, jnp.log2(jnp.maximum(addend, 1.0)), masked_score))
    for h in range(heads):
        lanes = slice(h * HEAD_SIZE, (h + 1) * HEAD_SIZE)
        query, grad = query_s[:, lanes], grad_s[:, lanes]
        scores = []
        for i, part in enumerate((low, mid, high)):
            score = dot(part[0, :, lanes], query, ((1,), (1,))) * (SCALE * math.log2(math.e))
            for b in range(nblk):
                block = score[b * BLOCK_TOKENS : (b + 1) * BLOCK_TOKENS]
                scores.append(block + addends[i * nblk + b])
        top = functools.reduce(jnp.maximum, [jnp.max(s, axis=0, keepdims=True) for s in scores])
        raised = [jnp.exp2(s - top) for s in scores]
        total = sum(jnp.sum(r, axis=0, keepdims=True) for r in raised)
        scaling = 1.0 / total
        delta = jnp.zeros((1, length), jnp.float32)
        out = jnp.zeros((HEAD_SIZE, length), jnp.float32)
        chances, grad_chances = [], []
        for i, (part, sums) in enumerate(((low, lower), (mid, own), (high, upper))):
            chance = jnp.concatenate(raised[i * nblk : (i + 1) * nblk], axis=0) * scaling
            weights = chance.astype(jnp.bfloat16)
            sums[1, :, lanes] = dot(weights, grad, ((1,), (0,))).astype(sums.dtype)
            out += dot(part[1, :, lanes], weights, ((0,), (0,)))
            grad_chance = dot(part[1, :, lanes], grad, ((1,), (1,)))
            delta += jnp.sum(chance * grad_chance, axis=0, keepdims=True)
            chances.append(chance)
            grad_chances.append(grad_chance)
        back = jnp.zeros((HEAD_SIZE, length), jnp.float32)
        for i, (part, sums) in enumerate(((low, lower), (mid, own), (high, upper))):
            grad_score = (chances[i] * (grad_chances[i] - delta)).astype(jnp.bfloat16)
            sums[0, :, lanes] = dot(grad_score, query, ((1,), (0,))).astype(sums.dtype)
            back += dot(part[0, :, lanes], grad_score, ((0,), (0,)))
        near, far = back[:HALF], back[HALF:]
        back = jnp.concatenate(
            [
                near * half_cosine[...] + far * half_sine[...],
                far * half_cosine[...] - near * half_sine[...],
            ],
            axis=0,
        )
        out_s[:, lanes] = out.T.astype(jnp.bfloat16)
        back_s[:, lanes] = back.T.astype(jnp.bfloat16)
    for result, index in results:
        place = start_of(index, result.shape[1])
        result[0] = out_s[place, :]
        result[1] = back_s[place, :]


def attend(meta, listed, half_cosine, half_sine, low, mid, high, inputs, n, joined, heads, after=()):
    _, length, width = mid.shape
    rows, lanes = length // n, heads * HEAD_SIZE
    window = pl.BlockSpec((2, length, lanes), lambda i: (0, 0, i))
    sources = set_specs(len(inputs) == 1, n, (2, rows, lanes), lambda i: (0, 0, i))
    targets = set_specs(joined, n, (2, rows, lanes), lambda i: (0, 0, i))
    table = pl.BlockSpec(half_cosine.shape, lambda i: (0, 0))
    results = pl.pallas_call(
        behind(functools.partial(attend_kernel, len(inputs), heads), len(after)),
        grid=(width // lanes,),
        out_shape=set_shapes(joined, n, (2, rows, width))
        + [jax.ShapeDtypeStruct(mid.shape, jnp.bfloat16)] * 2
        + [jax.ShapeDtypeStruct(mid.shape, jnp.float32)],
        in_specs=[ANY_SPEC] * len(after)
        + [SMEM_SPEC, SMEM_SPEC, table, table]
        + [window] * 3
        + sources,
        out_specs=targets + [window] * 3,
        scratch_shapes=[pltpu.VMEM((length, lanes), jnp.bfloat16)] * 4,
        compiler_params=params(),
        cost_estimate=cost(36 * length * length * width, 40 * length * width),
        name="attend",
    )(*after, meta, listed, half_cosine, half_sine, low, mid, high, *inputs)
    return results[:-3], *results[-3:]


def combine_kernel(meta, cosine, sine, own, from_upper, from_lower, *pieces):
    for piece, index in views(meta, pieces):
        place = start_of(index, piece.shape[1])
        for h in range(0, own.shape[2], HEAD_SIZE):
            lanes = slice(h, h + HEAD_SIZE)
            for t in range(2):
                total = (
                    own[t, place, lanes]
                    + from_upper[t, place, lanes].astype(jnp.float32)
                    + from_lower[t, place, lanes].astype(jnp.float32)
                )
                if t == 0:
                    total = unrotate(total, cosine[place, :], sine[place, :])
                piece[t, :, lanes] = total.astype(jnp.bfloat16)


def combine(meta, cosine, sine, own, from_upper, from_lower, n):
    _, length, width = own.shape
    return pl.pallas_call(
        combine_kernel,
        out_shape=[jax.ShapeDtypeStruct((2, length // n, width), jnp.bfloat16)] * n,
        in_specs=[SMEM_SPEC] + [VMEM_SPEC] * 5,
        out_specs=[VMEM_SPEC] * n,
        compiler_params=params(),
        cost_estimate=cost(0, 20 * length * width),
        name="combine",
    )(meta, cosine, sine, own, from_upper, from_lower)


def join_kernel(n, meta, *refs):
    pieces, outs, sems = refs[:n], refs[n:-1], refs[-1]
    copies = []
    for step, piece in enumerate(pieces):
        lanes = start_of(jnp.bitwise_xor(meta[0], step), piece.shape[2])
        for t, out in enumerate(outs):
            copies.append(pltpu.make_async_copy(piece.at[t], out.at[:, lanes], sems.at[step, t]))
    for copy in copies:
        copy.start()
    for copy in copies:
        copy.wait()


def join(meta, pieces):
    n = len(pieces)
    count, rows, width = pieces[0].shape
    return pl.pallas_call(
        functools.partial(join_kernel, n),
        out_shape=[jax.ShapeDtypeStruct((rows, n * width), jnp.bfloat16)] * count,
        in_specs=[SMEM_SPEC] + [ANY_SPEC] * n,
        out_specs=[HBM_SPEC] * count,
        scratch_shapes=[pltpu.SemaphoreType.DMA((n, count))],
        compiler_params=params(),
        cost_estimate=cost(0, 4 * n * count * rows * width),
        name="join",
    )(meta, *pieces)


def swap(pieces):
    if len(pieces) == 1:
        return [lax.all_to_all(pieces[0], "head", 0, 0, tiled=True)]
    n = len(pieces)
    return [pieces[0]] + [
        lax.ppermute(pieces[k], "head", [(i, i ^ k) for i in range(n)]) for k in range(1, n)
    ]


def shift(block, distance):
    devices = range(lax.axis_size("seq"))
    return lax.ppermute(block, "seq", [(i, i + distance) for i in devices if i + distance in devices])


def on_device(queries, keys, values, out_grad, chain_lengths, block_pairs):
    n = lax.axis_size("head")
    length = queries.shape[0] * n
    meta = jnp.stack([lax.axis_index("head"), lax.axis_index("seq")]).astype(jnp.int32)
    cosine, sine, half_cosine, half_sine = tables(meta, chain_lengths, length)

    key_value = swap(cut(meta, chain_lengths, keys, values, n))
    later = cut(meta, chain_lengths, queries, out_grad, n, [key_value[1], cosine])
    inputs = swap(later)
    mid = order(meta, key_value, n, [later[0]])
    low, high = shift(mid, 1), shift(mid, -1)
    results, lower, upper, own = attend(
        meta, block_pairs, half_cosine, half_sine, low, mid, high, inputs, n, False, 5
    )
    attn_out, query_grad = join(meta, swap(results))
    from_upper, from_lower = shift(lower, -1), shift(upper, 1)
    back = swap(combine(meta, cosine, sine, own, from_upper, from_lower, n))
    key_grad, value_grad = join(meta, back)
    return attn_out, query_grad, key_grad, value_grad


def solution(mesh):
    split = P(("seq", "head"), None)
    return jax.shard_map(
        on_device,
        mesh=mesh,
        in_specs=(split, split, split, split, P(), P()),
        out_specs=(split, split, split, split),
        check_vma=False,
    )
```

profile of v0, /device:TPU:11, one launch (start us, length us, event | category | flops | bytes accessed | tf_op | source)
XLA Modules:
  0.0 158.8 jit_solution(17199682248785278696)
XLA Ops:
  0.6 0.0 copy-start.9
  0.6 0.6 pad_add_fusion.meta.refs_1_
  1.2 3.3 %cut.2 = (bf16[2,64,1280]{2,1,0:T(8,128)(2,1)}, bf16[2,64,1280]{2,1,0:T(8,128)(2,1)}, bf16[2,64,1280]{2,1,0:T(8,128)(2,1)}, bf16[2,64,1280]{2,1,0:T(8,128)(2,1)}) custom-call(s32[2]{0:T(128)} %pad_add_fusion.meta.refs_1_, s32[16]{0:T(128)} %lengths.5, bf16[64,5120]{1,0:T(8,128)(2,1)} %turned.2, bf16[64,5120]{1,0:T(8,128)(2,1)} %plain.2), custom_call_target="tpu_custom_call" | custom-call | bytes 2621440 | tf_op jit(solution)/shard_map/cut/pallas_call | solution.py:129
  4.6 0.0 copy-start.6
  4.6 0.2 collective-permute-start
  4.8 2.3 %collective-permute-start.1 = (bf16[2,64,1280]{2,1,0:T(8,128)(2,1)}, bf16[2,64,1280]{2,1,0:T(8,128)(2,1)S(1)}, u32[]{:S(2)}, u32[]{:S(2)}) collective-permute-start(bf16[2,64,1280]{2,1,0:T(8,128)(2,1)} %get-tuple-element.37), channel_id=1, source_target_pairs={{0,2},{1,3},{2,0},{3,1},{4,6},{5,7},{6,4},{7,5},{8,10},{9,11},{10,... | collective-permute-start | bytes 983048 | tf_op jit(solution)/shard_map/ppermute | solution.py:343
  7.1 0.2 collective-permute-start.2
  7.3 1.8 %tables.1 = (f32[256,128]{1,0:T(8,128)S(1)}, f32[256,128]{1,0:T(8,128)S(1)}, f32[64,256]{1,0:T(8,128)S(1)}, f32[64,256]{1,0:T(8,128)S(1)}) custom-call(s32[2]{0:T(128)S(1)} %copy-done.7, s32[16]{0:T(128)S(1)} %copy-done.9), custom_call_target="tpu_custom_call" | custom-call | bytes 262144 | tf_op jit(solution)/shard_map/tables/pallas_call | solution.py:155
  9.1 0.6 copy-done.2
  9.8 8.0 %collective-permute-done.refs_0_.refs_3_ = bf16[2,64,1280]{2,1,0:T(8,128)(2,1)S(1)} collective-permute-done((bf16[2,64,1280]{2,1,0:T(8,128)(2,1)}, bf16[2,64,1280]{2,1,0:T(8,128)(2,1)S(1)}, u32[]{:S(2)}, u32[]{:S(2)}) %collective-permute-start) | collective-permute-done | bytes 327712 | tf_op jit(solution)/shard_map/ppermute | solution.py:343
  17.7 0.7 copy-done
  18.5 3.2 %cut.3 = (bf16[2,64,1280]{2,1,0:T(8,128)(2,1)}, bf16[2,64,1280]{2,1,0:T(8,128)(2,1)}, bf16[2,64,1280]{2,1,0:T(8,128)(2,1)}, bf16[2,64,1280]{2,1,0:T(8,128)(2,1)}) custom-call(s32[2]{0:T(128)} %pad_add_fusion.meta.refs_1_, s32[16]{0:T(128)} %lengths.5, bf16[64,5120]{1,0:T(8,128)(2,1)} %turned.3, bf16[64,5120]{1,0:T(8,128)(2,1)} %plain.3, ...), custom_call_target="tpu_custom_call" | custom-call | bytes 2621440 | tf_op jit(solution)/shard_map/cut/pallas_call | solution.py:129
  21.7 0.0 collective-permute-done.1.refs_4_
  21.7 13.8 %collective-permute-done.2.refs_5_ = bf16[2,64,1280]{2,1,0:T(8,128)(2,1)S(1)} collective-permute-done((bf16[2,64,1280]{2,1,0:T(8,128)(2,1)}, bf16[2,64,1280]{2,1,0:T(8,128)(2,1)S(1)}, u32[]{:S(2)}, u32[]{:S(2)}) %collective-permute-start.2) | collective-permute-done | bytes 327712 | tf_op jit(solution)/shard_map/ppermute | solution.py:343
  35.4 1.0 copy-done.1
  36.4 1.0 copy-done.4
  37.4 0.6 order.1.mid
  38.0 3.7 %collective-permute-start.4 = (bf16[2,256,1280]{2,1,0:T(8,128)(2,1)S(1)}, bf16[2,256,1280]{2,1,0:T(8,128)(2,1)}, u32[]{:S(2)}, u32[]{:S(2)}) collective-permute-start(bf16[2,256,1280]{2,1,0:T(8,128)(2,1)S(1)} %order.1.mid), channel_id=1, source_target_pairs={{4,0},{8,4},{12,8},{16,12},{20,16},{24,20},{28,24},{5,1},{9,5},{13... | collective-permute-start | bytes 3932168 | tf_op jit(solution)/shard_map/ppermute | solution.py:349
  41.8 3.0 %collective-permute-start.3 = (bf16[2,256,1280]{2,1,0:T(8,128)(2,1)S(1)}, bf16[2,256,1280]{2,1,0:T(8,128)(2,1)}, u32[]{:S(2)}, u32[]{:S(2)}) collective-permute-start(bf16[2,256,1280]{2,1,0:T(8,128)(2,1)S(1)} %order.1.mid), channel_id=1, source_target_pairs={{0,4},{4,8},{8,12},{12,16},{16,20},{20,24},{24,28},{1,5},{5,9},{9,... | collective-permute-start | bytes 3932168 | tf_op jit(solution)/shard_map/ppermute | solution.py:349
  44.8 0.1 collective-permute-start.5
  44.9 2.5 %collective-permute-start.6 = (bf16[2,64,1280]{2,1,0:T(8,128)(2,1)}, bf16[2,64,1280]{2,1,0:T(8,128)(2,1)S(1)}, u32[]{:S(2)}, u32[]{:S(2)}) collective-permute-start(bf16[2,64,1280]{2,1,0:T(8,128)(2,1)} %get-tuple-element.40), channel_id=1, source_target_pairs={{0,2},{1,3},{2,0},{3,1},{4,6},{5,7},{6,4},{7,5},{8,10},{9,11},{10,... | collective-permute-start | bytes 983048 | tf_op jit(solution)/shard_map/ppermute | solution.py:343
  47.3 0.2 collective-permute-start.7
  47.5 0.1 copy.10.listed
  47.6 11.5 %collective-permute-done.5.refs_1_ = bf16[2,64,1280]{2,1,0:T(8,128)(2,1)S(1)} collective-permute-done((bf16[2,64,1280]{2,1,0:T(8,128)(2,1)}, bf16[2,64,1280]{2,1,0:T(8,128)(2,1)S(1)}, u32[]{:S(2)}, u32[]{:S(2)}) %collective-permute-start.5) | collective-permute-done | bytes 327712 | tf_op jit(solution)/shard_map/ppermute | solution.py:343
  59.1 10.1 %collective-permute-done.6.refs_2_ = bf16[2,64,1280]{2,1,0:T(8,128)(2,1)S(1)} collective-permute-done((bf16[2,64,1280]{2,1,0:T(8,128)(2,1)}, bf16[2,64,1280]{2,1,0:T(8,128)(2,1)S(1)}, u32[]{:S(2)}, u32[]{:S(2)}) %collective-permute-start.6) | collective-permute-done | bytes 327712 | tf_op jit(solution)/shard_map/ppermute | solution.py:343
  69.1 7.8 %collective-permute-done.7.refs_3_ = bf16[2,64,1280]{2,1,0:T(8,128)(2,1)S(1)} collective-permute-done((bf16[2,64,1280]{2,1,0:T(8,128)(2,1)}, bf16[2,64,1280]{2,1,0:T(8,128)(2,1)S(1)}, u32[]{:S(2)}, u32[]{:S(2)}) %collective-permute-start.7) | collective-permute-done | bytes 327712 | tf_op jit(solution)/shard_map/ppermute | solution.py:343
  77.0 0.7 copy-done.10
  77.7 0.0 collective-permute-done.3.low
  77.7 1.0 copy-done.11
  78.7 12.9 %attend.1 = (bf16[2,64,1280]{2,1,0:T(8,128)(2,1)S(1)}, bf16[2,64,1280]{2,1,0:T(8,128)(2,1)S(1)}, bf16[2,64,1280]{2,1,0:T(8,128)(2,1)S(1)}, bf16[2,64,1280]{2,1,0...) custom-call(s32[2]{0:T(128)S(1)} %copy-done.8, ...), custom_call_target="tpu_custom_call" | custom-call | flops 3019898880 | bytes 13107200 | tf_op jit(solution)/shard_map/attend/pallas_call | solution.py:262
  91.6 2.4 %collective-permute-start.11 = (bf16[2,256,1280]{2,1,0:T(8,128)(2,1)S(1)}, bf16[2,256,1280]{2,1,0:T(8,128)(2,1)S(1)}, u32[]{:S(2)}, u32[]{:S(2)}) collective-permute-start(bf16[2,256,1280]{2,1,0:T(8,128)(2,1)S(1)} %get-tuple-element.50), channel_id=1, source_target_pairs={{4,0},{8,4},{12,8},{16,12},{20,16},{24,20},{28,24},{5,1},{9,5},{13... | collective-permute-start | bytes 3932168 | tf_op jit(solution)/shard_map/ppermute | solution.py:349
  94.1 4.0 %collective-permute-start.12 = (bf16[2,256,1280]{2,1,0:T(8,128)(2,1)S(1)}, bf16[2,256,1280]{2,1,0:T(8,128)(2,1)S(1)}, u32[]{:S(2)}, u32[]{:S(2)}) collective-permute-start(bf16[2,256,1280]{2,1,0:T(8,128)(2,1)S(1)} %get-tuple-element.51), channel_id=1, source_target_pairs={{0,4},{4,8},{8,12},{12,16},{16,20},{20,24},{24,28},{1,5},{5,9},{9,... | collective-permute-start | bytes 3932168 | tf_op jit(solution)/shard_map/ppermute | solution.py:349
  98.1 0.1 collective-permute-start.8
  98.2 2.5 %collective-permute-start.9 = (bf16[2,64,1280]{2,1,0:T(8,128)(2,1)S(1)}, bf16[2,64,1280]{2,1,0:T(8,128)(2,1)S(1)}, u32[]{:S(2)}, u32[]{:S(2)}) collective-permute-start(bf16[2,64,1280]{2,1,0:T(8,128)(2,1)S(1)} %get-tuple-element.44), channel_id=1, source_target_pairs={{0,2},{1,3},{2,0},{3,1},{4,6},{5,7},{6,4},{7,5},{8,10},{9,11},{10,... | collective-permute-start | bytes 983048 | tf_op jit(solution)/shard_map/ppermute | solution.py:343
  100.6 0.2 collective-permute-start.10
  100.8 22.7 %collective-permute-done.11.from_upper = bf16[2,256,1280]{2,1,0:T(8,128)(2,1)S(1)} collective-permute-done((bf16[2,256,1280]{2,1,0:T(8,128)(2,1)S(1)}, bf16[2,256,1280]{2,1,0:T(8,128)(2,1)S(1)}, u32[]{:S(2)}, u32[]{:S(2)}) %collective-permute-start.11) | collective-permute-done | bytes 1310752 | tf_op jit(solution)/shard_map/ppermute | solution.py:349
  123.5 0.0 collective-permute-done.12.from_lower
  123.5 1.2 combine.1
  124.7 0.1 collective-permute-start.13
  124.8 2.5 %collective-permute-start.14 = (bf16[2,64,1280]{2,1,0:T(8,128)(2,1)S(1)}, bf16[2,64,1280]{2,1,0:T(8,128)(2,1)S(1)}, u32[]{:S(2)}, u32[]{:S(2)}) collective-permute-start(bf16[2,64,1280]{2,1,0:T(8,128)(2,1)S(1)} %get-tuple-element.54), channel_id=1, source_target_pairs={{0,2},{1,3},{2,0},{3,1},{4,6},{5,7},{6,4},{7,5},{8,10},{9,11},{10,... | collective-permute-start | bytes 983048 | tf_op jit(solution)/shard_map/ppermute | solution.py:343
  127.3 0.0 collective-permute-done.8.refs_1_
  127.3 0.2 collective-permute-start.15
  127.5 4.8 %collective-permute-done.10.refs_3_ = bf16[2,64,1280]{2,1,0:T(8,128)(2,1)S(1)} collective-permute-done((bf16[2,64,1280]{2,1,0:T(8,128)(2,1)S(1)}, bf16[2,64,1280]{2,1,0:T(8,128)(2,1)S(1)}, u32[]{:S(2)}, u32[]{:S(2)}) %collective-permute-start.10) | collective-permute-done | bytes 327712 | tf_op jit(solution)/shard_map/ppermute | solution.py:343
  132.3 1.7 %join.2 = (bf16[64,5120]{1,0:T(8,128)(2,1)}, bf16[64,5120]{1,0:T(8,128)(2,1)}) custom-call(s32[2]{0:T(128)S(1)} %copy-done.8, bf16[2,64,1280]{2,1,0:T(8,128)(2,1)S(1)} %get-tuple-element.42.refs_0_, bf16[2,64,1280]{2,1,0:T(8,128)(2,1)S(1)} %collective-permute-done.8.refs_1_, bf16[2,64,1280]{2,1,0:T(8,128)(2,1)S(1)} %collective-permute-done.9.refs_2_, ...), custom_call_target="tpu_custom_call" | custom-call | bytes 2621440 | tf_op jit(solution)/shard_map/join/pallas_call | solution.py:326
  133.9 0.7 collective-permute-done.13.refs_1_
  134.6 15.7 %collective-permute-done.14.refs_2_ = bf16[2,64,1280]{2,1,0:T(8,128)(2,1)S(1)} collective-permute-done((bf16[2,64,1280]{2,1,0:T(8,128)(2,1)S(1)}, bf16[2,64,1280]{2,1,0:T(8,128)(2,1)S(1)}, u32[]{:S(2)}, u32[]{:S(2)}) %collective-permute-start.14) | collective-permute-done | bytes 327712 | tf_op jit(solution)/shard_map/ppermute | solution.py:343
  150.3 6.8 %collective-permute-done.15.refs_3_ = bf16[2,64,1280]{2,1,0:T(8,128)(2,1)S(1)} collective-permute-done((bf16[2,64,1280]{2,1,0:T(8,128)(2,1)S(1)}, bf16[2,64,1280]{2,1,0:T(8,128)(2,1)S(1)}, u32[]{:S(2)}, u32[]{:S(2)}) %collective-permute-start.15) | collective-permute-done | bytes 327712 | tf_op jit(solution)/shard_map/ppermute | solution.py:343
  157.1 1.7 %join.3 = (bf16[64,5120]{1,0:T(8,128)(2,1)}, bf16[64,5120]{1,0:T(8,128)(2,1)}) custom-call(s32[2]{0:T(128)S(1)} %copy-done.8, bf16[2,64,1280]{2,1,0:T(8,128)(2,1)S(1)} %get-tuple-element.52.refs_0_, bf16[2,64,1280]{2,1,0:T(8,128)(2,1)S(1)} %collective-permute-done.13.refs_1_, bf16[2,64,1280]{2,1,0:T(8,128)(2,1)S(1)} %collective-permute-done.14.refs_2_, ...), custom_call_target="tpu_custom_call" | custom-call | bytes 2621440 | tf_op jit(solution)/shard_map/join/pallas_call | solution.py:326
  (20 shorter events, 0.0 us)
Async XLA Ops:
  0.6 6.7 %copy-start.9 = (s32[16]{0:T(128)S(1)}, s32[16]{0:T(128)}, u32[]{:S(2)}) copy-start(s32[16]{0:T(128)} %lengths.5) | copy-start | bytes 196
  1.2 6.1 %copy-start.7 = (s32[2]{0:T(128)S(1)}, s32[2]{0:T(128)}, u32[]{:S(2)}) copy-start(s32[2]{0:T(128)} %pad_add_fusion.meta.refs_1_) | copy-start | bytes 28
  1.2 34.2 %copy-start.8 = (s32[2]{0:T(128)S(1)}, s32[2]{0:T(128)}, u32[]{:S(2)}) copy-start(s32[2]{0:T(128)} %pad_add_fusion.meta.refs_1_) | copy-start | bytes 28
  4.6 30.9 %copy-start.6 = (bf16[2,64,1280]{2,1,0:T(8,128)(2,1)S(1)}, bf16[2,64,1280]{2,1,0:T(8,128)(2,1)}, u32[]{:S(2)}) copy-start(bf16[2,64,1280]{2,1,0:T(8,128)(2,1)} %get-tuple-element.36.refs_2_) | copy-start | bytes 983044
  4.6 13.2 %collective-permute-start = (bf16[2,64,1280]{2,1,0:T(8,128)(2,1)}, bf16[2,64,1280]{2,1,0:T(8,128)(2,1)S(1)}, u32[]{:S(2)}, u32[]{:S(2)}) collective-permute-start(bf16[2,64,1280]{2,1,0:T(8,128)(2,1)} %get-tuple-element.33), channel_id=1, source_target_pairs={{0,1},{1,0},{2,3},{3,2},{4,5},{5,4},{6,7},{7,6},{8,9},{9,8},{10,11... | collective-permute-start | bytes 983048 | tf_op jit(solution)/shard_map/ppermute | solution.py:343
  4.8 16.9 %collective-permute-start.1 = (bf16[2,64,1280]{2,1,0:T(8,128)(2,1)}, bf16[2,64,1280]{2,1,0:T(8,128)(2,1)S(1)}, u32[]{:S(2)}, u32[]{:S(2)}) collective-permute-start(bf16[2,64,1280]{2,1,0:T(8,128)(2,1)} %get-tuple-element.37), channel_id=1, source_target_pairs={{0,2},{1,3},{2,0},{3,1},{4,6},{5,7},{6,4},{7,5},{8,10},{9,11},{10,... | collective-permute-start | bytes 983048 | tf_op jit(solution)/shard_map/ppermute | solution.py:343
  7.1 28.3 %collective-permute-start.2 = (bf16[2,64,1280]{2,1,0:T(8,128)(2,1)}, bf16[2,64,1280]{2,1,0:T(8,128)(2,1)S(1)}, u32[]{:S(2)}, u32[]{:S(2)}) collective-permute-start(bf16[2,64,1280]{2,1,0:T(8,128)(2,1)} %get-tuple-element.38), channel_id=1, source_target_pairs={{0,3},{1,2},{2,1},{3,0},{4,7},{5,6},{6,5},{7,4},{8,11},{9,10},{10,... | collective-permute-start | bytes 983048 | tf_op jit(solution)/shard_map/ppermute | solution.py:343
  9.1 0.7 copy-start.2
  17.7 0.7 copy-start
  35.4 1.0 copy-start.1
  36.4 1.0 copy-start.4
  37.4 10.1 %copy-start.12 = (s32[16,4]{0,1:T(4,128)S(1)}, s32[16,4]{0,1:T(4,128)}, u32[]{:S(2)}) copy-start(s32[16,4]{0,1:T(4,128)} %param.11) | copy-start | bytes 772
  37.4 40.3 %copy-start.5 = (bf16[2,64,1280]{2,1,0:T(8,128)(2,1)S(1)}, bf16[2,64,1280]{2,1,0:T(8,128)(2,1)}, u32[]{:S(2)}) copy-start(bf16[2,64,1280]{2,1,0:T(8,128)(2,1)} %get-tuple-element.35.refs_0_) | copy-start | bytes 983044
  38.0 39.7 %collective-permute-start.4 = (bf16[2,256,1280]{2,1,0:T(8,128)(2,1)S(1)}, bf16[2,256,1280]{2,1,0:T(8,128)(2,1)}, u32[]{:S(2)}, u32[]{:S(2)}) collective-permute-start(bf16[2,256,1280]{2,1,0:T(8,128)(2,1)S(1)} %order.1.mid), channel_id=1, source_target_pairs={{4,0},{8,4},{12,8},{16,12},{20,16},{24,20},{28,24},{5,1},{9,5},{13... | collective-permute-start | bytes 3932168 | tf_op jit(solution)/shard_map/ppermute | solution.py:349
  41.8 35.9 %collective-permute-start.3 = (bf16[2,256,1280]{2,1,0:T(8,128)(2,1)S(1)}, bf16[2,256,1280]{2,1,0:T(8,128)(2,1)}, u32[]{:S(2)}, u32[]{:S(2)}) collective-permute-start(bf16[2,256,1280]{2,1,0:T(8,128)(2,1)S(1)} %order.1.mid), channel_id=1, source_target_pairs={{0,4},{4,8},{8,12},{12,16},{16,20},{20,24},{24,28},{1,5},{5,9},{9,... | collective-permute-start | bytes 3932168 | tf_op jit(solution)/shard_map/ppermute | solution.py:349
  44.8 14.3 %collective-permute-start.5 = (bf16[2,64,1280]{2,1,0:T(8,128)(2,1)}, bf16[2,64,1280]{2,1,0:T(8,128)(2,1)S(1)}, u32[]{:S(2)}, u32[]{:S(2)}) collective-permute-start(bf16[2,64,1280]{2,1,0:T(8,128)(2,1)} %get-tuple-element.39), channel_id=1, source_target_pairs={{0,1},{1,0},{2,3},{3,2},{4,5},{5,4},{6,7},{7,6},{8,9},{9,8},{10,11... | collective-permute-start | bytes 983048 | tf_op jit(solution)/shard_map/ppermute | solution.py:343
  44.9 24.3 %collective-permute-start.6 = (bf16[2,64,1280]{2,1,0:T(8,128)(2,1)}, bf16[2,64,1280]{2,1,0:T(8,128)(2,1)S(1)}, u32[]{:S(2)}, u32[]{:S(2)}) collective-permute-start(bf16[2,64,1280]{2,1,0:T(8,128)(2,1)} %get-tuple-element.40), channel_id=1, source_target_pairs={{0,2},{1,3},{2,0},{3,1},{4,6},{5,7},{6,4},{7,5},{8,10},{9,11},{10,... | collective-permute-start | bytes 983048 | tf_op jit(solution)/shard_map/ppermute | solution.py:343
  47.3 29.6 %collective-permute-start.7 = (bf16[2,64,1280]{2,1,0:T(8,128)(2,1)}, bf16[2,64,1280]{2,1,0:T(8,128)(2,1)S(1)}, u32[]{:S(2)}, u32[]{:S(2)}) collective-permute-start(bf16[2,64,1280]{2,1,0:T(8,128)(2,1)} %get-tuple-element.41), channel_id=1, source_target_pairs={{0,3},{1,2},{2,1},{3,0},{4,7},{5,6},{6,5},{7,4},{8,11},{9,10},{10,... | collective-permute-start | bytes 983048 | tf_op jit(solution)/shard_map/ppermute | solution.py:343
  77.0 0.7 copy-start.10
  77.7 1.0 copy-start.11
  78.7 44.8 %copy-start.3 = (f32[256,128]{1,0:T(8,128)S(1)}, f32[256,128]{1,0:T(8,128)}, u32[]{:S(2)}) copy-start(f32[256,128]{1,0:T(8,128)} %copy-done.2) | copy-start | bytes 393220
  91.6 31.9 %collective-permute-start.11 = (bf16[2,256,1280]{2,1,0:T(8,128)(2,1)S(1)}, bf16[2,256,1280]{2,1,0:T(8,128)(2,1)S(1)}, u32[]{:S(2)}, u32[]{:S(2)}) collective-permute-start(bf16[2,256,1280]{2,1,0:T(8,128)(2,1)S(1)} %get-tuple-element.50), channel_id=1, source_target_pairs={{4,0},{8,4},{12,8},{16,12},{20,16},{24,20},{28,24},{5,1},{9,5},{13... | collective-permute-start | bytes 3932168 | tf_op jit(solution)/shard_map/ppermute | solution.py:349
  94.1 29.4 %collective-permute-start.12 = (bf16[2,256,1280]{2,1,0:T(8,128)(2,1)S(1)}, bf16[2,256,1280]{2,1,0:T(8,128)(2,1)S(1)}, u32[]{:S(2)}, u32[]{:S(2)}) collective-permute-start(bf16[2,256,1280]{2,1,0:T(8,128)(2,1)S(1)} %get-tuple-element.51), channel_id=1, source_target_pairs={{0,4},{4,8},{8,12},{12,16},{16,20},{20,24},{24,28},{1,5},{5,9},{9,... | collective-permute-start | bytes 3932168 | tf_op jit(solution)/shard_map/ppermute | solution.py:349
  98.1 29.2 %collective-permute-start.8 = (bf16[2,64,1280]{2,1,0:T(8,128)(2,1)S(1)}, bf16[2,64,1280]{2,1,0:T(8,128)(2,1)S(1)}, u32[]{:S(2)}, u32[]{:S(2)}) collective-permute-start(bf16[2,64,1280]{2,1,0:T(8,128)(2,1)S(1)} %get-tuple-element.43), channel_id=1, source_target_pairs={{0,1},{1,0},{2,3},{3,2},{4,5},{5,4},{6,7},{7,6},{8,9},{9,8},{10,11... | collective-permute-start | bytes 983048 | tf_op jit(solution)/shard_map/ppermute | solution.py:343
  98.2 29.3 %collective-permute-start.9 = (bf16[2,64,1280]{2,1,0:T(8,128)(2,1)S(1)}, bf16[2,64,1280]{2,1,0:T(8,128)(2,1)S(1)}, u32[]{:S(2)}, u32[]{:S(2)}) collective-permute-start(bf16[2,64,1280]{2,1,0:T(8,128)(2,1)S(1)} %get-tuple-element.44), channel_id=1, source_target_pairs={{0,2},{1,3},{2,0},{3,1},{4,6},{5,7},{6,4},{7,5},{8,10},{9,11},{10,... | collective-permute-start | bytes 983048 | tf_op jit(solution)/shard_map/ppermute | solution.py:343
  100.6 31.6 %collective-permute-start.10 = (bf16[2,64,1280]{2,1,0:T(8,128)(2,1)S(1)}, bf16[2,64,1280]{2,1,0:T(8,128)(2,1)S(1)}, u32[]{:S(2)}, u32[]{:S(2)}) collective-permute-start(bf16[2,64,1280]{2,1,0:T(8,128)(2,1)S(1)} %get-tuple-element.45), channel_id=1, source_target_pairs={{0,3},{1,2},{2,1},{3,0},{4,7},{5,6},{6,5},{7,4},{8,11},{9,10},{10,... | collective-permute-start | bytes 983048 | tf_op jit(solution)/shard_map/ppermute | solution.py:343
  124.7 9.9 %collective-permute-start.13 = (bf16[2,64,1280]{2,1,0:T(8,128)(2,1)S(1)}, bf16[2,64,1280]{2,1,0:T(8,128)(2,1)S(1)}, u32[]{:S(2)}, u32[]{:S(2)}) collective-permute-start(bf16[2,64,1280]{2,1,0:T(8,128)(2,1)S(1)} %get-tuple-element.53), channel_id=1, source_target_pairs={{0,1},{1,0},{2,3},{3,2},{4,5},{5,4},{6,7},{7,6},{8,9},{9,8},{10,11... | collective-permute-start | bytes 983048 | tf_op jit(solution)/shard_map/ppermute | solution.py:343
  124.8 25.5 %collective-permute-start.14 = (bf16[2,64,1280]{2,1,0:T(8,128)(2,1)S(1)}, bf16[2,64,1280]{2,1,0:T(8,128)(2,1)S(1)}, u32[]{:S(2)}, u32[]{:S(2)}) collective-permute-start(bf16[2,64,1280]{2,1,0:T(8,128)(2,1)S(1)} %get-tuple-element.54), channel_id=1, source_target_pairs={{0,2},{1,3},{2,0},{3,1},{4,6},{5,7},{6,4},{7,5},{8,10},{9,11},{10,... | collective-permute-start | bytes 983048 | tf_op jit(solution)/shard_map/ppermute | solution.py:343
  127.3 29.8 %collective-permute-start.15 = (bf16[2,64,1280]{2,1,0:T(8,128)(2,1)S(1)}, bf16[2,64,1280]{2,1,0:T(8,128)(2,1)S(1)}, u32[]{:S(2)}, u32[]{:S(2)}) collective-permute-start(bf16[2,64,1280]{2,1,0:T(8,128)(2,1)S(1)} %get-tuple-element.55), channel_id=1, source_target_pairs={{0,3},{1,2},{2,1},{3,0},{4,7},{5,6},{6,5},{7,4},{8,11},{9,10},{10,... | collective-permute-start | bytes 983048 | tf_op jit(solution)/shard_map/ppermute | solution.py:343
where the time goes:
time: 159 us
  waiting for transfers between devices  102 us (64%)
  Pallas kernels  26.5 us (17%)
  starting transfers between devices  24 us (15%)
  local copies, waits for them, and re-layouts  5.12 us (3%)
    ppermute x12, waiting for transfers between devices, swap(): lax.ppermute(pieces[k], 'head', [(i, i ^ k) for i in range(n)])  79.1 us
    ppermute x4, waiting for transfers between devices, shift(): lax.ppermute(block, 'seq', [(i, i + distance) for i in devices if i + dis...  22.7 us
    ppermute x4, starting transfers between devices, shift(): lax.ppermute(block, 'seq', [(i, i + distance) for i in devices if i + dis...  13.2 us
    pallas_call x1, Pallas kernels, attend(): pl.pallas_call(behind(functools.partial(attend_kernel, len(inputs), heads...  12.9 us
    ppermute x12, starting transfers between devices, swap(): lax.ppermute(pieces[k], 'head', [(i, i ^ k) for i in range(n)])  10.8 us
    pallas_call x2, Pallas kernels, cut(): pl.pallas_call(functools.partial(cut_kernel, n), out_shape=[jax.ShapeDtyp...  6.5 us
    unnamed x27, local copies, waits for them, and re-layouts  5.12 us
    pallas_call x2, Pallas kernels, join(): pl.pallas_call(functools.partial(join_kernel, n), out_shape=[jax.ShapeDty...  3.31 us
  transfers between devices with their start and end apart: 16, of which 10 were waited for; matrix products, arithmetic and copies ran while one was open for 0% of the time, Pallas kernels for 5%

commit v1 on v0

--- a/solution.py
+++ b/solution.py
@@ -14,6 +14,7 @@
 SCALE = 1.0 / math.sqrt(HEAD_SIZE)
 VMEM_LIMIT = 32 * 1024 * 1024
 WIDE_LIMIT = 60 * 1024 * 1024
+PARTS = 1
 
 masked_score = -1e30
 rotary_base = 10000.0
@@ -57,10 +58,10 @@
     return (row - begin).astype(jnp.float32) * frequency, entry
 
 
-def fill_tables(lengths, first_row, cosine, sine, scale=1.0):
+def fill_tables(lengths, first_row, cosine, sine):
     angle, entry = chain_angles(lengths, first_row, cosine.shape, 0)
-    turn = jnp.sin(angle) * scale
-    cosine[...] = jnp.cos(angle) * scale
+    turn = jnp.sin(angle)
+    cosine[...] = jnp.cos(angle)
     sine[...] = jnp.where(entry < HALF, -turn, turn)
 
 
@@ -98,12 +99,13 @@
     return lax.dot_general(a, b, (contract, ((), ())), preferred_element_type=jnp.float32)
 
 
-def cut_kernel(n, meta, lengths, turned, plain, *refs):
+def cut_kernel(n, offset, meta, lengths, turned, plain, *refs):
     pieces, (held, cosine, sine, sems) = refs[-4 - n : -4], refs[-4:]
     rows, width = turned.shape[0], held.shape[2]
     copies = []
     for step, piece in enumerate(pieces):
-        lanes = start_of(jnp.bitwise_xor(meta[0], step), width)
+        base = jnp.bitwise_xor(meta[0], step) * (turned.shape[1] // n) + offset
+        lanes = pl.ds(pl.multiple_of(base, HEAD_SIZE), width)
         copies.append(
             (
                 pltpu.make_async_copy(turned.at[:, lanes], held.at[step], sems.at[step, 0]),
@@ -124,10 +126,10 @@
         copies[step][1].wait()
 
 
-def cut(meta, lengths, turned, plain, n, after=()):
-    rows, width = turned.shape[0], turned.shape[1] // n
+def cut(meta, lengths, turned, plain, n, limit, part=0, parts=1, after=()):
+    rows, width = turned.shape[0], turned.shape[1] // (n * parts)
     return pl.pallas_call(
-        functools.partial(cut_kernel, n),
+        functools.partial(cut_kernel, n, part * width),
         out_shape=[jax.ShapeDtypeStruct((2, rows, width), jnp.bfloat16)] * n,
         in_specs=[SMEM_SPEC] * 2 + [HBM_SPEC] * 2 + [ANY_SPEC] * len(after),
         out_specs=[VMEM_SPEC] * n,
@@ -137,7 +139,7 @@
             pltpu.VMEM((rows, HEAD_SIZE), jnp.float32),
             pltpu.SemaphoreType.DMA((n, 2)),
         ],
-        compiler_params=params(WIDE_LIMIT),
+        compiler_params=params(limit),
         cost_estimate=cost(0, 8 * n * rows * width),
         name="cut",
     )(meta, lengths, turned, plain, *after)
@@ -145,49 +147,55 @@
 
 def tables_kernel(meta, lengths, cosine, sine, half_cosine, half_sine):
     first = meta[1] * cosine.shape[0]
-    fill_tables(lengths, first, cosine, sine, SCALE)
+    fill_tables(lengths, first, cosine, sine)
     angle, _ = chain_angles(lengths, first, half_cosine.shape, 1)
-    half_cosine[...] = jnp.cos(angle) * SCALE
-    half_sine[...] = jnp.sin(angle) * SCALE
-
-
-def tables(meta, lengths, length):
+    half_cosine[...] = jnp.cos(angle)
+    half_sine[...] = jnp.sin(angle)
+
+
+def tables(meta, lengths, length, after):
     return pl.pallas_call(
-        tables_kernel,
+        behind(tables_kernel, len(after)),
         out_shape=[jax.ShapeDtypeStruct((length, HEAD_SIZE), jnp.float32)] * 2
         + [jax.ShapeDtypeStruct((HALF, length), jnp.float32)] * 2,
-        in_specs=[SMEM_SPEC] * 2,
+        in_specs=[ANY_SPEC] * len(after) + [SMEM_SPEC] * 2,
         compiler_params=params(),
         cost_estimate=cost(0, 8 * length * HEAD_SIZE),
         name="tables",
-    )(meta, lengths)
-
-
-def order_kernel(meta, *refs):
-    out = refs[-1]
-    for piece, index in views(meta, refs[:-1]):
-        out[:, start_of(index, piece.shape[1]), :] = piece[...]
-
-
-def order(meta, pieces, n, after=()):
-    _, rows, width = pieces[0].shape[-3:]
+    )(*after, meta, lengths)
+
+
+def order_kernel(n, meta, *refs):
+    outs = refs[n:]
+    width = outs[0].shape[2]
+    for piece, index in views(meta, refs[:n]):
+        for part, out in enumerate(outs):
+            out[:, start_of(index, piece.shape[1]), :] = piece[:, :, part * width : (part + 1) * width]
+
+
+def order(meta, pieces, parts, after=()):
+    _, rows, width = pieces[0].shape
+    n = len(pieces)
+    shape = jax.ShapeDtypeStruct((2, n * rows, width // parts), jnp.bfloat16)
     return pl.pallas_call(
-        behind(order_kernel, len(after)),
-        grid=(1,),
-        out_shape=jax.ShapeDtypeStruct((2, n * rows, width), pieces[0].dtype),
-        in_specs=[ANY_SPEC] * len(after)
-        + [SMEM_SPEC]
-        + set_specs(len(pieces) == 1, n, (2, rows, width), lambda i: (0, 0, 0)),
-        out_specs=pl.BlockSpec((2, n * rows, width), lambda i: (0, 0, 0)),
+        behind(functools.partial(order_kernel, n), len(after)),
+        out_shape=[shape] * parts,
+        in_specs=[ANY_SPEC] * len(after) + [SMEM_SPEC] + [VMEM_SPEC] * n,
+        out_specs=[VMEM_SPEC] * parts,
         compiler_params=params(),
         cost_estimate=cost(0, 8 * n * rows * width),
         name="order",
     )(*after, meta, *pieces)
 
 
-def attend_kernel(count, heads, meta, listed, half_cosine, half_sine, low, mid, high, *refs):
+def window_shards(shard):
+    odd = lax.rem(shard, 2)
+    return shard, shard + 1 - 2 * odd, shard - 1 + 2 * odd
+
+
+def attend_kernel(count, heads, meta, listed, half_cosine, half_sine, mid, near, far, *refs):
     inputs, results = views(meta, refs[:count]), views(meta, refs[count:-7])
-    lower, upper, own, query_s, grad_s, out_s, back_s = refs[-7:]
+    own, near_sum, far_sum, query_s, grad_s, out_s, back_s = refs[-7:]
     length = mid.shape[1]
     nblk = length // BLOCK_TOKENS
     for piece, index in inputs:
@@ -197,20 +205,22 @@
     first = meta[1] * nblk
     query_block = lax.broadcasted_iota(jnp.int32, (1, length), 1) // BLOCK_TOKENS
     addends = []
-    for key_block in range(3 * nblk):
-        addend = jnp.zeros((1, length), jnp.float32)
-        for block in range(nblk):
-            times = jnp.int32(0)
-            for p in range(listed.shape[1]):
-                same = listed[first + block, p] == first + key_block - nblk
-                times += jnp.where(same & (listed[first + block, p] >= 0), 1, 0)
-            addend = jnp.where(query_block == block, times.astype(jnp.float32), addend)
-        addends.append(jnp.where(addend > 0, jnp.log2(jnp.maximum(addend, 1.0)), masked_score))
+    for shard in window_shards(meta[1]):
+        for key_block in range(nblk):
+            addend = jnp.zeros((1, length), jnp.float32)
+            for block in range(nblk):
+                times = jnp.int32(0)
+                for p in range(listed.shape[1]):
+                    entry = listed[first + block, p]
+                    times += jnp.where((entry >= 0) & (entry == shard * nblk + key_block), 1, 0)
+                addend = jnp.where(query_block == block, times.astype(jnp.float32), addend)
+            addends.append(jnp.where(addend > 0, jnp.log2(jnp.maximum(addend, 1.0)), masked_score))
+    window = ((mid, own), (near, near_sum), (far, far_sum))
     for h in range(heads):
         lanes = slice(h * HEAD_SIZE, (h + 1) * HEAD_SIZE)
         query, grad = query_s[:, lanes], grad_s[:, lanes]
         scores = []
-        for i, part in enumerate((low, mid, high)):
+        for i, part in enumerate((mid, near, far)):
             score = dot(part[0, :, lanes], query, ((1,), (1,))) * (SCALE * math.log2(math.e))
             for b in range(nblk):
                 block = score[b * BLOCK_TOKENS : (b + 1) * BLOCK_TOKENS]
@@ -222,7 +232,7 @@
         delta = jnp.zeros((1, length), jnp.float32)
         out = jnp.zeros((HEAD_SIZE, length), jnp.float32)
         chances, grad_chances = [], []
-        for i, (part, sums) in enumerate(((low, lower), (mid, own), (high, upper))):
+        for i, (part, sums) in enumerate(window):
             chance = jnp.concatenate(raised[i * nblk : (i + 1) * nblk], axis=0) * scaling
             weights = chance.astype(jnp.bfloat16)
             sums[1, :, lanes] = dot(weights, grad, ((1,), (0,))).astype(sums.dtype)
@@ -232,15 +242,15 @@
             chances.append(chance)
             grad_chances.append(grad_chance)
         back = jnp.zeros((HEAD_SIZE, length), jnp.float32)
-        for i, (part, sums) in enumerate(((low, lower), (mid, own), (high, upper))):
-            grad_score = (chances[i] * (grad_chances[i] - delta)).astype(jnp.bfloat16)
+        for i, (part, sums) in enumerate(window):
+            grad_score = (chances[i] * (grad_chances[i] - delta) * SCALE).astype(jnp.bfloat16)
             sums[0, :, lanes] = dot(grad_score, query, ((1,), (0,))).astype(sums.dtype)
             back += dot(part[0, :, lanes], grad_score, ((0,), (0,)))
-        near, far = back[:HALF], back[HALF:]
+        low, high = back[:HALF], back[HALF:]
         back = jnp.concatenate(
             [
-                near * half_cosine[...] + far * half_sine[...],
-                far * half_cosine[...] - near * half_sine[...],
+                low * half_cosine[...] + high * half_sine[...],
+                high * half_cosine[...] - low * half_sine[...],
             ],
             axis=0,
         )
@@ -252,33 +262,36 @@
         result[1] = back_s[place, :]
 
 
-def attend(meta, listed, half_cosine, half_sine, low, mid, high, inputs, n, joined, heads, after=()):
+def attend(meta, listed, half_cosine, half_sine, mid, near, far, inputs, part, parts, before):
+    n = len(inputs)
     _, length, width = mid.shape
-    rows, lanes = length // n, heads * HEAD_SIZE
-    window = pl.BlockSpec((2, length, lanes), lambda i: (0, 0, i))
-    sources = set_specs(len(inputs) == 1, n, (2, rows, lanes), lambda i: (0, 0, i))
-    targets = set_specs(joined, n, (2, rows, lanes), lambda i: (0, 0, i))
+    rows, whole = length // n, width * parts
+    window = pl.BlockSpec(mid.shape, lambda i: (0, 0, 0))
+    sums = pl.BlockSpec(mid.shape, lambda i: (0, 0, part))
+    source = pl.BlockSpec((2, rows, width), lambda i: (0, 0, 0))
+    target = pl.BlockSpec((2, rows, width), lambda i: (0, 0, part))
     table = pl.BlockSpec(half_cosine.shape, lambda i: (0, 0))
     results = pl.pallas_call(
-        behind(functools.partial(attend_kernel, len(inputs), heads), len(after)),
-        grid=(width // lanes,),
-        out_shape=set_shapes(joined, n, (2, rows, width))
-        + [jax.ShapeDtypeStruct(mid.shape, jnp.bfloat16)] * 2
-        + [jax.ShapeDtypeStruct(mid.shape, jnp.float32)],
-        in_specs=[ANY_SPEC] * len(after)
+        behind(functools.partial(attend_kernel, n, width // HEAD_SIZE), len(before)),
+        grid=(1,),
+        out_shape=[jax.ShapeDtypeStruct((2, rows, whole), jnp.bfloat16)] * n
+        + [jax.ShapeDtypeStruct((2, length, whole), jnp.float32)]
+        + [jax.ShapeDtypeStruct((2, length, whole), jnp.bfloat16)] * 2,
+        in_specs=[ANY_SPEC] * len(before)
         + [SMEM_SPEC, SMEM_SPEC, table, table]
         + [window] * 3
-        + sources,
-        out_specs=targets + [window] * 3,
-        scratch_shapes=[pltpu.VMEM((length, lanes), jnp.bfloat16)] * 4,
+        + [source] * n,
+        out_specs=[target] * n + [sums] * 3,
+        scratch_shapes=[pltpu.VMEM((length, width), jnp.bfloat16)] * 4,
+        input_output_aliases={t: t for t in range(len(before))},
         compiler_params=params(),
         cost_estimate=cost(36 * length * length * width, 40 * length * width),
         name="attend",
-    )(*after, meta, listed, half_cosine, half_sine, low, mid, high, *inputs)
-    return results[:-3], *results[-3:]
-
-
-def combine_kernel(meta, cosine, sine, own, from_upper, from_lower, *pieces):
+    )(*before, meta, listed, half_cosine, half_sine, mid, near, far, *inputs)
+    return results
+
+
+def combine_kernel(meta, cosine, sine, own, from_near, from_far, *pieces):
     for piece, index in views(meta, pieces):
         place = start_of(index, piece.shape[1])
         for h in range(0, own.shape[2], HEAD_SIZE):
@@ -286,15 +299,15 @@
             for t in range(2):
                 total = (
                     own[t, place, lanes]
-                    + from_upper[t, place, lanes].astype(jnp.float32)
-                    + from_lower[t, place, lanes].astype(jnp.float32)
+                    + from_near[t, place, lanes].astype(jnp.float32)
+                    + from_far[t, place, lanes].astype(jnp.float32)
                 )
                 if t == 0:
                     total = unrotate(total, cosine[place, :], sine[place, :])
                 piece[t, :, lanes] = total.astype(jnp.bfloat16)
 
 
-def combine(meta, cosine, sine, own, from_upper, from_lower, n):
+def combine(meta, cosine, sine, own, from_near, from_far, n):
     _, length, width = own.shape
     return pl.pallas_call(
         combine_kernel,
@@ -304,7 +317,7 @@
         compiler_params=params(),
         cost_estimate=cost(0, 20 * length * width),
         name="combine",
-    )(meta, cosine, sine, own, from_upper, from_lower)
+    )(meta, cosine, sine, own, from_near, from_far)
 
 
 def join_kernel(n, meta, *refs):
@@ -344,28 +357,45 @@
     ]
 
 
-def shift(block, distance):
-    devices = range(lax.axis_size("seq"))
-    return lax.ppermute(block, "seq", [(i, i + distance) for i in devices if i + distance in devices])
+def trade(block, first):
+    route = []
+    for i in range(first, lax.axis_size("seq") - 1, 2):
+        route += [(i, i + 1), (i + 1, i)]
+    return lax.ppermute(block, "seq", route)
 
 
 def on_device(queries, keys, values, out_grad, chain_lengths, block_pairs):
     n = lax.axis_size("head")
     length = queries.shape[0] * n
     meta = jnp.stack([lax.axis_index("head"), lax.axis_index("seq")]).astype(jnp.int32)
-    cosine, sine, half_cosine, half_sine = tables(meta, chain_lengths, length)
-
-    key_value = swap(cut(meta, chain_lengths, keys, values, n))
-    later = cut(meta, chain_lengths, queries, out_grad, n, [key_value[1], cosine])
-    inputs = swap(later)
-    mid = order(meta, key_value, n, [later[0]])
-    low, high = shift(mid, 1), shift(mid, -1)
-    results, lower, upper, own = attend(
-        meta, block_pairs, half_cosine, half_sine, low, mid, high, inputs, n, False, 5
-    )
+    key_value = swap(cut(meta, chain_lengths, keys, values, n, WIDE_LIMIT))
+    laters = [
+        cut(meta, chain_lengths, queries, out_grad, n, VMEM_LIMIT, part, PARTS, [key_value[1]])
+        for part in range(PARTS)
+    ]
+    inputs = [swap(later) for later in laters]
+    mids = order(meta, key_value, PARTS, [later[0] for later in laters])
+    nears, fars = [trade(mid, 0) for mid in mids], [trade(mid, 1) for mid in mids]
+    cosine, sine, half_cosine, half_sine = tables(meta, chain_lengths, length, [inputs[0][1]])
+    sums = []
+    for part in range(PARTS):
+        sums = attend(
+            meta,
+            block_pairs,
+            half_cosine,
+            half_sine,
+            mids[part],
+            nears[part],
+            fars[part],
+            inputs[part],
+            part,
+            PARTS,
+            sums,
+        )
+    results, (own, near_sum, far_sum) = sums[:n], sums[n:]
     attn_out, query_grad = join(meta, swap(results))
-    from_upper, from_lower = shift(lower, -1), shift(upper, 1)
-    back = swap(combine(meta, cosine, sine, own, from_upper, from_lower, n))
+    from_near, from_far = trade(near_sum, 0), trade(far_sum, 1)
+    back = swap(combine(meta, cosine, sine, own, from_near, from_far, n))
     key_grad, value_grad = join(meta, back)
     return attn_out, query_grad, key_grad, value_grad
 

time: 159 us -> 154 us (0.969)
  local copies, waits for them, and re-layouts: 5.12 us -> 0.11 us
  waiting for transfers between devices: 102 us -> 106 us
  starting transfers between devices: 24 us -> 20.4 us
    unnamed x27 -> x13, local copies, waits for them, and re-layouts: 5.12 us -> 0.11 us
    ppermute x4, waiting for transfers between devices: 22.7 us -> 26.4 us  [trade(): return lax.ppermute(block, 'seq', route)]
    ppermute x4, starting transfers between devices: 13.2 us -> 9.51 us  [trade(): return lax.ppermute(block, 'seq', route)]
where the time goes in v1:
time: 154 us; the launch traced here: 153 us
  waiting for transfers between devices  106 us (69%)
  Pallas kernels  25.1 us (16%)
  starting transfers between devices  20.4 us (13%)
    ppermute x12, waiting for transfers between devices, swap(): lax.ppermute(pieces[k], 'head', [(i, i ^ k) for i in range(n)])  79.9 us
    ppermute x4, waiting for transfers between devices, trade(): return lax.ppermute(block, 'seq', route)  26.4 us
    pallas_call x1, Pallas kernels, attend(): pl.pallas_call(behind(functools.partial(attend_kernel, n, width // HEAD_S...  12.3 us
    ppermute x12, starting transfers between devices, swap(): lax.ppermute(pieces[k], 'head', [(i, i ^ k) for i in range(n)])  10.8 us
    ppermute x4, starting transfers between devices, trade(): return lax.ppermute(block, 'seq', route)  9.51 us
    pallas_call x2, Pallas kernels, cut(): pl.pallas_call(functools.partial(cut_kernel, n, part * width), out_shape=...  5.79 us
    pallas_call x2, Pallas kernels, join(): pl.pallas_call(functools.partial(join_kernel, n), out_shape=[jax.ShapeDty...  3.32 us
  transfers between devices with their start and end apart: 16, of which 10 were waited for; matrix products, arithmetic and copies ran while one was open for 0% of the time, Pallas kernels for 5%

profile of v1, /device:TPU:11, one launch (start us, length us, event | category | flops | bytes accessed | tf_op | source)
XLA Modules:
  0.0 153.3 jit_solution(1463289578439671613)
XLA Ops:
  0.6 0.0 copy-start.4
  0.6 0.0 copy-start.1
  0.7 0.0 copy-start
  0.7 0.7 pad_add_fusion.meta.refs_1_
  1.3 3.2 %cut.2 = (bf16[2,64,1280]{2,1,0:T(8,128)(2,1)}, bf16[2,64,1280]{2,1,0:T(8,128)(2,1)}, bf16[2,64,1280]{2,1,0:T(8,128)(2,1)}, bf16[2,64,1280]{2,1,0:T(8,128)(2,1)}) custom-call(s32[2]{0:T(128)} %pad_add_fusion.meta.refs_1_, s32[16]{0:T(128)} %refs_2_.1, bf16[64,5120]{1,0:T(8,128)(2,1)} %turned.2, bf16[64,5120]{1,0:T(8,128)(2,1)} %plain.2), custom_call_target="tpu_custom_call" | custom-call | bytes 2621440 | tf_op jit(solution)/shard_map/cut/pallas_call | solution.py:131
  4.6 0.0 copy-start.2
  4.6 0.2 collective-permute-start
  4.8 2.3 %collective-permute-start.2 = (bf16[2,64,1280]{2,1,0:T(8,128)(2,1)}, bf16[2,64,1280]{2,1,0:T(8,128)(2,1)S(1)}, u32[]{:S(2)}, u32[]{:S(2)}) collective-permute-start(bf16[2,64,1280]{2,1,0:T(8,128)(2,1)} %get-tuple-element.37), channel_id=1, source_target_pairs={{0,2},{1,3},{2,0},{3,1},{4,6},{5,7},{6,4},{7,5},{8,10},{9,11},{10,... | collective-permute-start | bytes 983048 | tf_op jit(solution)/shard_map/ppermute | solution.py:356
  7.1 0.2 collective-permute-start.3
  7.3 10.5 %collective-permute-done.refs_0_.refs_3_ = bf16[2,64,1280]{2,1,0:T(8,128)(2,1)S(1)} collective-permute-done((bf16[2,64,1280]{2,1,0:T(8,128)(2,1)}, bf16[2,64,1280]{2,1,0:T(8,128)(2,1)S(1)}, u32[]{:S(2)}, u32[]{:S(2)}) %collective-permute-start) | collective-permute-done | bytes 327712 | tf_op jit(solution)/shard_map/ppermute | solution.py:356
  17.8 0.0 copy-done.4
  17.8 0.0 copy-done.1
  17.8 2.5 %cut.3 = (bf16[2,64,1280]{2,1,0:T(8,128)(2,1)S(1)}, bf16[2,64,1280]{2,1,0:T(8,128)(2,1)}, bf16[2,64,1280]{2,1,0:T(8,128)(2,1)}, bf16[2,64,1280]{2,1,0:T(8,128)(2,1)}) custom-call(s32[2]{0:T(128)S(1)} %copy-done.3, s32[16]{0:T(128)S(1)} %copy-done.4, bf16[64,5120]{1,0:T(8,128)(2,1)S(1)} %copy-done, bf16[64,5120]{1,0:T(8,128)(2,1)S(1)} %copy-done.1, ...), custom_call_target="tpu_custom_call" | custom-call | bytes 2621440 | tf_op jit(solution)/shard_map/cut/pallas_call | solution.py:131
  20.3 1.2 collective-permute-done.2.refs_4_
  21.5 13.9 %collective-permute-done.3.refs_5_ = bf16[2,64,1280]{2,1,0:T(8,128)(2,1)S(1)} collective-permute-done((bf16[2,64,1280]{2,1,0:T(8,128)(2,1)}, bf16[2,64,1280]{2,1,0:T(8,128)(2,1)S(1)}, u32[]{:S(2)}, u32[]{:S(2)}) %collective-permute-start.3) | collective-permute-done | bytes 327712 | tf_op jit(solution)/shard_map/ppermute | solution.py:356
  35.5 0.6 order.1.mid
  36.1 4.8 %collective-permute-start.5 = (bf16[2,256,1280]{2,1,0:T(8,128)(2,1)S(1)}, bf16[2,256,1280]{2,1,0:T(8,128)(2,1)S(1)}, u32[]{:S(2)}, u32[]{:S(2)}) collective-permute-start(bf16[2,256,1280]{2,1,0:T(8,128)(2,1)S(1)} %order.1.mid), channel_id=1, source_target_pairs={{4,8},{8,4},{12,16},{16,12},{20,24},{24,20},{5,9},{9,5},{13,17},{1... | collective-permute-start | bytes 3932168 | tf_op jit(solution)/shard_map/ppermute | solution.py:364
  41.0 0.1 collective-permute-start.4
  41.0 0.1 collective-permute-start.1
  41.1 2.5 %collective-permute-start.6 = (bf16[2,64,1280]{2,1,0:T(8,128)(2,1)}, bf16[2,64,1280]{2,1,0:T(8,128)(2,1)}, u32[]{:S(2)}, u32[]{:S(2)}) collective-permute-start(bf16[2,64,1280]{2,1,0:T(8,128)(2,1)} %get-tuple-element.39), channel_id=1, source_target_pairs={{0,2},{1,3},{2,0},{3,1},{4,6},{5,7},{6,4},{7,5},{8,10},{9,11},{10,... | collective-permute-start | bytes 983048 | tf_op jit(solution)/shard_map/ppermute | solution.py:356
  43.6 0.2 collective-permute-start.7
  43.8 0.1 copy.10.listed
  43.8 11.0 %collective-permute-done.1.refs_0_.refs_1_ = bf16[2,64,1280]{2,1,0:T(8,128)(2,1)S(1)} collective-permute-done((bf16[2,64,1280]{2,1,0:T(8,128)(2,1)}, bf16[2,64,1280]{2,1,0:T(8,128)(2,1)S(1)}, u32[]{:S(2)}, u32[]{:S(2)}) %collective-permute-start.1) | collective-permute-done | bytes 327712 | tf_op jit(solution)/shard_map/ppermute | solution.py:356
  54.8 1.8 %tables.1 = (f32[256,128]{1,0:T(8,128)S(1)}, f32[256,128]{1,0:T(8,128)S(1)}, f32[64,256]{1,0:T(8,128)S(1)}, f32[64,256]{1,0:T(8,128)S(1)}) custom-call(bf16[2,64,1280]{2,1,0:T(8,128)(2,1)S(1)} %collective-permute-done.1.refs_0_.refs_1_, s32[2]{0:T(128)S(1)} %copy-done.3, s32[16]{0:T(128)S(1)} %copy-done.4), custom_call_target="tpu_custom_call" | custom-call | bytes 262144 | tf_op jit(solution)/shard_map/tables/pallas_call | solution.py:157
  56.6 1.7 %collective-permute-done.6.refs_2_ = bf16[2,64,1280]{2,1,0:T(8,128)(2,1)} collective-permute-done((bf16[2,64,1280]{2,1,0:T(8,128)(2,1)}, bf16[2,64,1280]{2,1,0:T(8,128)(2,1)}, u32[]{:S(2)}, u32[]{:S(2)}) %collective-permute-start.6) | collective-permute-done | bytes 327712 | tf_op jit(solution)/shard_map/ppermute | solution.py:356
  58.3 14.0 %collective-permute-done.7.refs_3_ = bf16[2,64,1280]{2,1,0:T(8,128)(2,1)} collective-permute-done((bf16[2,64,1280]{2,1,0:T(8,128)(2,1)}, bf16[2,64,1280]{2,1,0:T(8,128)(2,1)}, u32[]{:S(2)}, u32[]{:S(2)}) %collective-permute-start.7) | collective-permute-done | bytes 327712 | tf_op jit(solution)/shard_map/ppermute | solution.py:356
  72.3 0.0 collective-permute-done.5.far
  72.3 0.0 collective-permute-done.4.near
  72.3 12.3 %attend.1 = (bf16[2,64,1280]{2,1,0:T(8,128)(2,1)S(1)}, bf16[2,64,1280]{2,1,0:T(8,128)(2,1)S(1)}, bf16[2,64,1280]{2,1,0:T(8,128)(2,1)S(1)}, bf16[2,64,1280]{2,1,0...) custom-call(s32[2]{0:T(128)S(1)} %copy-done.3, ...), custom_call_target="tpu_custom_call" | custom-call | flops 3019898880 | bytes 13107200 | tf_op jit(solution)/shard_map/attend/pallas_call | solution.py:274
  84.6 1.6 %collective-permute-start.11 = (bf16[2,256,1280]{2,1,0:T(8,128)(2,1)S(1)}, bf16[2,256,1280]{2,1,0:T(8,128)(2,1)S(1)}, u32[]{:S(2)}, u32[]{:S(2)}) collective-permute-start(bf16[2,256,1280]{2,1,0:T(8,128)(2,1)S(1)} %get-tuple-element.50), channel_id=1, source_target_pairs={{0,4},{4,0},{8,12},{12,8},{16,20},{20,16},{24,28},{28,24},{1,5},{5... | collective-permute-start | bytes 3932168 | tf_op jit(solution)/shard_map/ppermute | solution.py:364
  86.2 3.0 %collective-permute-start.12 = (bf16[2,256,1280]{2,1,0:T(8,128)(2,1)S(1)}, bf16[2,256,1280]{2,1,0:T(8,128)(2,1)S(1)}, u32[]{:S(2)}, u32[]{:S(2)}) collective-permute-start(bf16[2,256,1280]{2,1,0:T(8,128)(2,1)S(1)} %get-tuple-element.51), channel_id=1, source_target_pairs={{4,8},{8,4},{12,16},{16,12},{20,24},{24,20},{5,9},{9,5},{13,17},{1... | collective-permute-start | bytes 3932168 | tf_op jit(solution)/shard_map/ppermute | solution.py:364
  89.2 0.1 collective-permute-start.8
  89.3 2.5 %collective-permute-start.9 = (bf16[2,64,1280]{2,1,0:T(8,128)(2,1)S(1)}, bf16[2,64,1280]{2,1,0:T(8,128)(2,1)S(1)}, u32[]{:S(2)}, u32[]{:S(2)}) collective-permute-start(bf16[2,64,1280]{2,1,0:T(8,128)(2,1)S(1)} %get-tuple-element.43), channel_id=1, source_target_pairs={{0,2},{1,3},{2,0},{3,1},{4,6},{5,7},{6,4},{7,5},{8,10},{9,11},{10,... | collective-permute-start | bytes 983048 | tf_op jit(solution)/shard_map/ppermute | solution.py:356
  91.8 0.2 collective-permute-start.10
  92.0 0.0 collective-permute-done.11.from_near
  92.0 26.4 %collective-permute-done.12.from_far = bf16[2,256,1280]{2,1,0:T(8,128)(2,1)S(1)} collective-permute-done((bf16[2,256,1280]{2,1,0:T(8,128)(2,1)S(1)}, bf16[2,256,1280]{2,1,0:T(8,128)(2,1)S(1)}, u32[]{:S(2)}, u32[]{:S(2)}) %collective-permute-start.12) | collective-permute-done | bytes 1310752 | tf_op jit(solution)/shard_map/ppermute | solution.py:364
  118.4 1.2 combine.1
  119.6 0.1 collective-permute-start.13
  119.7 2.5 %collective-permute-start.14 = (bf16[2,64,1280]{2,1,0:T(8,128)(2,1)S(1)}, bf16[2,64,1280]{2,1,0:T(8,128)(2,1)S(1)}, u32[]{:S(2)}, u32[]{:S(2)}) collective-permute-start(bf16[2,64,1280]{2,1,0:T(8,128)(2,1)S(1)} %get-tuple-element.54), channel_id=1, source_target_pairs={{0,2},{1,3},{2,0},{3,1},{4,6},{5,7},{6,4},{7,5},{8,10},{9,11},{10,... | collective-permute-start | bytes 983048 | tf_op jit(solution)/shard_map/ppermute | solution.py:356
  122.1 0.0 collective-permute-done.8.refs_1_
  122.2 0.2 collective-permute-start.15
  122.3 0.0 collective-permute-done.9.refs_2_
  122.3 0.0 collective-permute-done.10.refs_3_
  122.3 1.7 %join.2 = (bf16[64,5120]{1,0:T(8,128)(2,1)}, bf16[64,5120]{1,0:T(8,128)(2,1)}) custom-call(s32[2]{0:T(128)S(1)} %copy-done.3, bf16[2,64,1280]{2,1,0:T(8,128)(2,1)S(1)} %get-tuple-element.41.refs_0_, bf16[2,64,1280]{2,1,0:T(8,128)(2,1)S(1)} %collective-permute-done.8.refs_1_, bf16[2,64,1280]{2,1,0:T(8,128)(2,1)S(1)} %collective-permute-done.9.refs_2_, ...), custom_call_target="tpu_custom_call" | custom-call | bytes 2621440 | tf_op jit(solution)/shard_map/join/pallas_call | solution.py:339
  124.0 9.3 %collective-permute-done.13.refs_1_ = bf16[2,64,1280]{2,1,0:T(8,128)(2,1)S(1)} collective-permute-done((bf16[2,64,1280]{2,1,0:T(8,128)(2,1)S(1)}, bf16[2,64,1280]{2,1,0:T(8,128)(2,1)S(1)}, u32[]{:S(2)}, u32[]{:S(2)}) %collective-permute-start.13) | collective-permute-done | bytes 327712 | tf_op jit(solution)/shard_map/ppermute | solution.py:356
  133.3 10.5 %collective-permute-done.14.refs_2_ = bf16[2,64,1280]{2,1,0:T(8,128)(2,1)S(1)} collective-permute-done((bf16[2,64,1280]{2,1,0:T(8,128)(2,1)S(1)}, bf16[2,64,1280]{2,1,0:T(8,128)(2,1)S(1)}, u32[]{:S(2)}, u32[]{:S(2)}) %collective-permute-start.14) | collective-permute-done | bytes 327712 | tf_op jit(solution)/shard_map/ppermute | solution.py:356
  143.8 7.9 %collective-permute-done.15.refs_3_ = bf16[2,64,1280]{2,1,0:T(8,128)(2,1)S(1)} collective-permute-done((bf16[2,64,1280]{2,1,0:T(8,128)(2,1)S(1)}, bf16[2,64,1280]{2,1,0:T(8,128)(2,1)S(1)}, u32[]{:S(2)}, u32[]{:S(2)}) %collective-permute-start.15) | collective-permute-done | bytes 327712 | tf_op jit(solution)/shard_map/ppermute | solution.py:356
  151.7 1.7 %join.3 = (bf16[64,5120]{1,0:T(8,128)(2,1)}, bf16[64,5120]{1,0:T(8,128)(2,1)}) custom-call(s32[2]{0:T(128)S(1)} %copy-done.3, bf16[2,64,1280]{2,1,0:T(8,128)(2,1)S(1)} %get-tuple-element.52.refs_0_, bf16[2,64,1280]{2,1,0:T(8,128)(2,1)S(1)} %collective-permute-done.13.refs_1_, bf16[2,64,1280]{2,1,0:T(8,128)(2,1)S(1)} %collective-permute-done.14.refs_2_, ...), custom_call_target="tpu_custom_call" | custom-call | bytes 2621440 | tf_op jit(solution)/shard_map/join/pallas_call | solution.py:339
  (6 shorter events, 0.0 us)
Async XLA Ops:
  0.6 17.2 %copy-start.4 = (s32[16]{0:T(128)S(1)}, s32[16]{0:T(128)}, u32[]{:S(2)}) copy-start(s32[16]{0:T(128)} %refs_2_.1) | copy-start | bytes 196
  0.6 17.1 %copy-start.1 = (bf16[64,5120]{1,0:T(8,128)(2,1)S(1)}, bf16[64,5120]{1,0:T(8,128)(2,1)}, u32[]{:S(2)}) copy-start(bf16[64,5120]{1,0:T(8,128)(2,1)} %plain.3) | copy-start | bytes 1966084
  0.7 17.1 %copy-start = (bf16[64,5120]{1,0:T(8,128)(2,1)S(1)}, bf16[64,5120]{1,0:T(8,128)(2,1)}, u32[]{:S(2)}) copy-start(bf16[64,5120]{1,0:T(8,128)(2,1)} %turned.3) | copy-start | bytes 1966084
  1.3 16.5 %copy-start.3 = (s32[2]{0:T(128)S(1)}, s32[2]{0:T(128)}, u32[]{:S(2)}) copy-start(s32[2]{0:T(128)} %pad_add_fusion.meta.refs_1_) | copy-start | bytes 28
  4.6 30.9 %copy-start.2 = (bf16[2,64,1280]{2,1,0:T(8,128)(2,1)S(1)}, bf16[2,64,1280]{2,1,0:T(8,128)(2,1)}, u32[]{:S(2)}) copy-start(bf16[2,64,1280]{2,1,0:T(8,128)(2,1)} %get-tuple-element.36.refs_2_) | copy-start | bytes 983044
  4.6 13.2 %collective-permute-start = (bf16[2,64,1280]{2,1,0:T(8,128)(2,1)}, bf16[2,64,1280]{2,1,0:T(8,128)(2,1)S(1)}, u32[]{:S(2)}, u32[]{:S(2)}) collective-permute-start(bf16[2,64,1280]{2,1,0:T(8,128)(2,1)} %get-tuple-element.31), channel_id=1, source_target_pairs={{0,1},{1,0},{2,3},{3,2},{4,5},{5,4},{6,7},{7,6},{8,9},{9,8},{10,11... | collective-permute-start | bytes 983048 | tf_op jit(solution)/shard_map/ppermute | solution.py:356
  4.8 16.7 %collective-permute-start.2 = (bf16[2,64,1280]{2,1,0:T(8,128)(2,1)}, bf16[2,64,1280]{2,1,0:T(8,128)(2,1)S(1)}, u32[]{:S(2)}, u32[]{:S(2)}) collective-permute-start(bf16[2,64,1280]{2,1,0:T(8,128)(2,1)} %get-tuple-element.37), channel_id=1, source_target_pairs={{0,2},{1,3},{2,0},{3,1},{4,6},{5,7},{6,4},{7,5},{8,10},{9,11},{10,... | collective-permute-start | bytes 983048 | tf_op jit(solution)/shard_map/ppermute | solution.py:356
  7.1 28.3 %collective-permute-start.3 = (bf16[2,64,1280]{2,1,0:T(8,128)(2,1)}, bf16[2,64,1280]{2,1,0:T(8,128)(2,1)S(1)}, u32[]{:S(2)}, u32[]{:S(2)}) collective-permute-start(bf16[2,64,1280]{2,1,0:T(8,128)(2,1)} %get-tuple-element.38), channel_id=1, source_target_pairs={{0,3},{1,2},{2,1},{3,0},{4,7},{5,6},{6,5},{7,4},{8,11},{9,10},{10,... | collective-permute-start | bytes 983048 | tf_op jit(solution)/shard_map/ppermute | solution.py:356
  35.5 8.3 %copy-start.5 = (s32[16,4]{0,1:T(4,128)S(1)}, s32[16,4]{0,1:T(4,128)}, u32[]{:S(2)}) copy-start(s32[16,4]{0,1:T(4,128)} %param.11) | copy-start | bytes 772
  36.1 36.2 %collective-permute-start.5 = (bf16[2,256,1280]{2,1,0:T(8,128)(2,1)S(1)}, bf16[2,256,1280]{2,1,0:T(8,128)(2,1)S(1)}, u32[]{:S(2)}, u32[]{:S(2)}) collective-permute-start(bf16[2,256,1280]{2,1,0:T(8,128)(2,1)S(1)} %order.1.mid), channel_id=1, source_target_pairs={{4,8},{8,4},{12,16},{16,12},{20,24},{24,20},{5,9},{9,5},{13,17},{1... | collective-permute-start | bytes 3932168 | tf_op jit(solution)/shard_map/ppermute | solution.py:364
  41.0 31.3 %collective-permute-start.4 = (bf16[2,256,1280]{2,1,0:T(8,128)(2,1)S(1)}, bf16[2,256,1280]{2,1,0:T(8,128)(2,1)}, u32[]{:S(2)}, u32[]{:S(2)}) collective-permute-start(bf16[2,256,1280]{2,1,0:T(8,128)(2,1)S(1)} %order.1.mid), channel_id=1, source_target_pairs={{0,4},{4,0},{8,12},{12,8},{16,20},{20,16},{24,28},{28,24},{1,5},{5... | collective-permute-start | bytes 3932168 | tf_op jit(solution)/shard_map/ppermute | solution.py:364
  41.0 13.8 %collective-permute-start.1 = (bf16[2,64,1280]{2,1,0:T(8,128)(2,1)}, bf16[2,64,1280]{2,1,0:T(8,128)(2,1)S(1)}, u32[]{:S(2)}, u32[]{:S(2)}) collective-permute-start(bf16[2,64,1280]{2,1,0:T(8,128)(2,1)} %get-tuple-element.32), channel_id=1, source_target_pairs={{0,1},{1,0},{2,3},{3,2},{4,5},{5,4},{6,7},{7,6},{8,9},{9,8},{10,11... | collective-permute-start | bytes 983048 | tf_op jit(solution)/shard_map/ppermute | solution.py:356
  41.1 17.2 %collective-permute-start.6 = (bf16[2,64,1280]{2,1,0:T(8,128)(2,1)}, bf16[2,64,1280]{2,1,0:T(8,128)(2,1)}, u32[]{:S(2)}, u32[]{:S(2)}) collective-permute-start(bf16[2,64,1280]{2,1,0:T(8,128)(2,1)} %get-tuple-element.39), channel_id=1, source_target_pairs={{0,2},{1,3},{2,0},{3,1},{4,6},{5,7},{6,4},{7,5},{8,10},{9,11},{10,... | collective-permute-start | bytes 983048 | tf_op jit(solution)/shard_map/ppermute | solution.py:356
  43.6 28.7 %collective-permute-start.7 = (bf16[2,64,1280]{2,1,0:T(8,128)(2,1)}, bf16[2,64,1280]{2,1,0:T(8,128)(2,1)}, u32[]{:S(2)}, u32[]{:S(2)}) collective-permute-start(bf16[2,64,1280]{2,1,0:T(8,128)(2,1)} %get-tuple-element.40), channel_id=1, source_target_pairs={{0,3},{1,2},{2,1},{3,0},{4,7},{5,6},{6,5},{7,4},{8,11},{9,10},{10,... | collective-permute-start | bytes 983048 | tf_op jit(solution)/shard_map/ppermute | solution.py:356
  84.6 7.4 %collective-permute-start.11 = (bf16[2,256,1280]{2,1,0:T(8,128)(2,1)S(1)}, bf16[2,256,1280]{2,1,0:T(8,128)(2,1)S(1)}, u32[]{:S(2)}, u32[]{:S(2)}) collective-permute-start(bf16[2,256,1280]{2,1,0:T(8,128)(2,1)S(1)} %get-tuple-element.50), channel_id=1, source_target_pairs={{0,4},{4,0},{8,12},{12,8},{16,20},{20,16},{24,28},{28,24},{1,5},{5... | collective-permute-start | bytes 3932168 | tf_op jit(solution)/shard_map/ppermute | solution.py:364
  86.2 32.1 %collective-permute-start.12 = (bf16[2,256,1280]{2,1,0:T(8,128)(2,1)S(1)}, bf16[2,256,1280]{2,1,0:T(8,128)(2,1)S(1)}, u32[]{:S(2)}, u32[]{:S(2)}) collective-permute-start(bf16[2,256,1280]{2,1,0:T(8,128)(2,1)S(1)} %get-tuple-element.51), channel_id=1, source_target_pairs={{4,8},{8,4},{12,16},{16,12},{20,24},{24,20},{5,9},{9,5},{13,17},{1... | collective-permute-start | bytes 3932168 | tf_op jit(solution)/shard_map/ppermute | solution.py:364
  89.2 32.9 %collective-permute-start.8 = (bf16[2,64,1280]{2,1,0:T(8,128)(2,1)S(1)}, bf16[2,64,1280]{2,1,0:T(8,128)(2,1)S(1)}, u32[]{:S(2)}, u32[]{:S(2)}) collective-permute-start(bf16[2,64,1280]{2,1,0:T(8,128)(2,1)S(1)} %get-tuple-element.42), channel_id=1, source_target_pairs={{0,1},{1,0},{2,3},{3,2},{4,5},{5,4},{6,7},{7,6},{8,9},{9,8},{10,11... | collective-permute-start | bytes 983048 | tf_op jit(solution)/shard_map/ppermute | solution.py:356
  89.3 33.0 %collective-permute-start.9 = (bf16[2,64,1280]{2,1,0:T(8,128)(2,1)S(1)}, bf16[2,64,1280]{2,1,0:T(8,128)(2,1)S(1)}, u32[]{:S(2)}, u32[]{:S(2)}) collective-permute-start(bf16[2,64,1280]{2,1,0:T(8,128)(2,1)S(1)} %get-tuple-element.43), channel_id=1, source_target_pairs={{0,2},{1,3},{2,0},{3,1},{4,6},{5,7},{6,4},{7,5},{8,10},{9,11},{10,... | collective-permute-start | bytes 983048 | tf_op jit(solution)/shard_map/ppermute | solution.py:356
  91.8 30.6 %collective-permute-start.10 = (bf16[2,64,1280]{2,1,0:T(8,128)(2,1)S(1)}, bf16[2,64,1280]{2,1,0:T(8,128)(2,1)S(1)}, u32[]{:S(2)}, u32[]{:S(2)}) collective-permute-start(bf16[2,64,1280]{2,1,0:T(8,128)(2,1)S(1)} %get-tuple-element.44), channel_id=1, source_target_pairs={{0,3},{1,2},{2,1},{3,0},{4,7},{5,6},{6,5},{7,4},{8,11},{9,10},{10,... | collective-permute-start | bytes 983048 | tf_op jit(solution)/shard_map/ppermute | solution.py:356
  119.6 13.7 %collective-permute-start.13 = (bf16[2,64,1280]{2,1,0:T(8,128)(2,1)S(1)}, bf16[2,64,1280]{2,1,0:T(8,128)(2,1)S(1)}, u32[]{:S(2)}, u32[]{:S(2)}) collective-permute-start(bf16[2,64,1280]{2,1,0:T(8,128)(2,1)S(1)} %get-tuple-element.53), channel_id=1, source_target_pairs={{0,1},{1,0},{2,3},{3,2},{4,5},{5,4},{6,7},{7,6},{8,9},{9,8},{10,11... | collective-permute-start | bytes 983048 | tf_op jit(solution)/shard_map/ppermute | solution.py:356
  119.7 24.1 %collective-permute-start.14 = (bf16[2,64,1280]{2,1,0:T(8,128)(2,1)S(1)}, bf16[2,64,1280]{2,1,0:T(8,128)(2,1)S(1)}, u32[]{:S(2)}, u32[]{:S(2)}) collective-permute-start(bf16[2,64,1280]{2,1,0:T(8,128)(2,1)S(1)} %get-tuple-element.54), channel_id=1, source_target_pairs={{0,2},{1,3},{2,0},{3,1},{4,6},{5,7},{6,4},{7,5},{8,10},{9,11},{10,... | collective-permute-start | bytes 983048 | tf_op jit(solution)/shard_map/ppermute | solution.py:356
  122.2 29.5 %collective-permute-start.15 = (bf16[2,64,1280]{2,1,0:T(8,128)(2,1)S(1)}, bf16[2,64,1280]{2,1,0:T(8,128)(2,1)S(1)}, u32[]{:S(2)}, u32[]{:S(2)}) collective-permute-start(bf16[2,64,1280]{2,1,0:T(8,128)(2,1)S(1)} %get-tuple-element.55), channel_id=1, source_target_pairs={{0,3},{1,2},{2,1},{3,0},{4,7},{5,6},{6,5},{7,4},{8,11},{9,10},{10,... | collective-permute-start | bytes 983048 | tf_op jit(solution)/shard_map/ppermute | solution.py:356

commit v2 on v1

--- a/solution.py
+++ b/solution.py
@@ -14,7 +14,7 @@
 SCALE = 1.0 / math.sqrt(HEAD_SIZE)
 VMEM_LIMIT = 32 * 1024 * 1024
 WIDE_LIMIT = 60 * 1024 * 1024
-PARTS = 1
+HEADS_A_STEP = 10
 
 masked_score = -1e30
 rotary_base = 10000.0
@@ -99,13 +99,12 @@
     return lax.dot_general(a, b, (contract, ((), ())), preferred_element_type=jnp.float32)
 
 
-def cut_kernel(n, offset, meta, lengths, turned, plain, *refs):
+def cut_kernel(n, meta, lengths, turned, plain, *refs):
     pieces, (held, cosine, sine, sems) = refs[-4 - n : -4], refs[-4:]
     rows, width = turned.shape[0], held.shape[2]
     copies = []
     for step, piece in enumerate(pieces):
-        base = jnp.bitwise_xor(meta[0], step) * (turned.shape[1] // n) + offset
-        lanes = pl.ds(pl.multiple_of(base, HEAD_SIZE), width)
+        lanes = start_of(jnp.bitwise_xor(meta[0], step), width)
         copies.append(
             (
                 pltpu.make_async_copy(turned.at[:, lanes], held.at[step], sems.at[step, 0]),
@@ -126,10 +125,10 @@
         copies[step][1].wait()
 
 
-def cut(meta, lengths, turned, plain, n, limit, part=0, parts=1, after=()):
-    rows, width = turned.shape[0], turned.shape[1] // (n * parts)
-    return pl.pallas_call(
-        functools.partial(cut_kernel, n, part * width),
+def cut(meta, lengths, turned, plain, n, limit, after=()):
+    rows, width = turned.shape[0], turned.shape[1] // n
+    return pl.pallas_call(
+        functools.partial(cut_kernel, n),
         out_shape=[jax.ShapeDtypeStruct((2, rows, width), jnp.bfloat16)] * n,
         in_specs=[SMEM_SPEC] * 2 + [HBM_SPEC] * 2 + [ANY_SPEC] * len(after),
         out_specs=[VMEM_SPEC] * n,
@@ -165,23 +164,20 @@
     )(*after, meta, lengths)
 
 
-def order_kernel(n, meta, *refs):
-    outs = refs[n:]
-    width = outs[0].shape[2]
-    for piece, index in views(meta, refs[:n]):
-        for part, out in enumerate(outs):
-            out[:, start_of(index, piece.shape[1]), :] = piece[:, :, part * width : (part + 1) * width]
-
-
-def order(meta, pieces, parts, after=()):
+def order_kernel(meta, *refs):
+    out = refs[-1]
+    for piece, index in views(meta, refs[:-1]):
+        out[:, start_of(index, piece.shape[1]), :] = piece[...]
+
+
+def order(meta, pieces, after=()):
     _, rows, width = pieces[0].shape
     n = len(pieces)
-    shape = jax.ShapeDtypeStruct((2, n * rows, width // parts), jnp.bfloat16)
-    return pl.pallas_call(
-        behind(functools.partial(order_kernel, n), len(after)),
-        out_shape=[shape] * parts,
+    return pl.pallas_call(
+        behind(order_kernel, len(after)),
+        out_shape=jax.ShapeDtypeStruct((2, n * rows, width), jnp.bfloat16),
         in_specs=[ANY_SPEC] * len(after) + [SMEM_SPEC] + [VMEM_SPEC] * n,
-        out_specs=[VMEM_SPEC] * parts,
+        out_specs=VMEM_SPEC,
         compiler_params=params(),
         cost_estimate=cost(0, 8 * n * rows * width),
         name="order",
@@ -216,35 +212,44 @@
                 addend = jnp.where(query_block == block, times.astype(jnp.float32), addend)
             addends.append(jnp.where(addend > 0, jnp.log2(jnp.maximum(addend, 1.0)), masked_score))
     window = ((mid, own), (near, near_sum), (far, far_sum))
-    for h in range(heads):
-        lanes = slice(h * HEAD_SIZE, (h + 1) * HEAD_SIZE)
-        query, grad = query_s[:, lanes], grad_s[:, lanes]
-        scores = []
-        for i, part in enumerate((mid, near, far)):
-            score = dot(part[0, :, lanes], query, ((1,), (1,))) * (SCALE * math.log2(math.e))
+    def lanes_of(h):
+        return slice(h * HEAD_SIZE, (h + 1) * HEAD_SIZE)
+
+    def stage_scores(h):
+        lanes, scores = lanes_of(h), []
+        for i, (part, _) in enumerate(window):
+            score = dot(part[0, :, lanes], query_s[:, lanes], ((1,), (1,))) * (SCALE * math.log2(math.e))
             for b in range(nblk):
                 block = score[b * BLOCK_TOKENS : (b + 1) * BLOCK_TOKENS]
                 scores.append(block + addends[i * nblk + b])
+        return scores
+
+    def stage_grad(h):
+        lanes = lanes_of(h)
+        return [dot(part[1, :, lanes], grad_s[:, lanes], ((1,), (1,))) for part, _ in window]
+
+    def stage_soft(scores):
         top = functools.reduce(jnp.maximum, [jnp.max(s, axis=0, keepdims=True) for s in scores])
         raised = [jnp.exp2(s - top) for s in scores]
-        total = sum(jnp.sum(r, axis=0, keepdims=True) for r in raised)
-        scaling = 1.0 / total
-        delta = jnp.zeros((1, length), jnp.float32)
+        scaling = 1.0 / sum(jnp.sum(r, axis=0, keepdims=True) for r in raised)
+        return [jnp.concatenate(raised[i * nblk : (i + 1) * nblk], axis=0) * scaling for i in range(3)]
+
+    def stage_out(h, chances):
+        lanes = lanes_of(h)
         out = jnp.zeros((HEAD_SIZE, length), jnp.float32)
-        chances, grad_chances = [], []
-        for i, (part, sums) in enumerate(window):
-            chance = jnp.concatenate(raised[i * nblk : (i + 1) * nblk], axis=0) * scaling
+        for (part, sums), chance in zip(window, chances):
             weights = chance.astype(jnp.bfloat16)
-            sums[1, :, lanes] = dot(weights, grad, ((1,), (0,))).astype(sums.dtype)
+            sums[1, :, lanes] = dot(weights, grad_s[:, lanes], ((1,), (0,))).astype(sums.dtype)
             out += dot(part[1, :, lanes], weights, ((0,), (0,)))
-            grad_chance = dot(part[1, :, lanes], grad, ((1,), (1,)))
-            delta += jnp.sum(chance * grad_chance, axis=0, keepdims=True)
-            chances.append(chance)
-            grad_chances.append(grad_chance)
+        out_s[:, lanes] = out.T.astype(jnp.bfloat16)
+
+    def stage_back(h, chances, grad_chances):
+        lanes = lanes_of(h)
+        delta = sum(jnp.sum(c * g, axis=0, keepdims=True) for c, g in zip(chances, grad_chances))
         back = jnp.zeros((HEAD_SIZE, length), jnp.float32)
-        for i, (part, sums) in enumerate(window):
-            grad_score = (chances[i] * (grad_chances[i] - delta) * SCALE).astype(jnp.bfloat16)
-            sums[0, :, lanes] = dot(grad_score, query, ((1,), (0,))).astype(sums.dtype)
+        for (part, sums), c, g in zip(window, chances, grad_chances):
+            grad_score = (c * (g - delta) * SCALE).astype(jnp.bfloat16)
+            sums[0, :, lanes] = dot(grad_score, query_s[:, lanes], ((1,), (0,))).astype(sums.dtype)
             back += dot(part[0, :, lanes], grad_score, ((0,), (0,)))
         low, high = back[:HALF], back[HALF:]
         back = jnp.concatenate(
@@ -254,41 +259,39 @@
             ],
             axis=0,
         )
-        out_s[:, lanes] = out.T.astype(jnp.bfloat16)
         back_s[:, lanes] = back.T.astype(jnp.bfloat16)
+
+    scores = stage_scores(0)
+    for h in range(heads):
+        grad_chances = stage_grad(h)
+        chances = stage_soft(scores)
+        if h + 1 < heads:
+            scores = stage_scores(h + 1)
+        stage_out(h, chances)
+        stage_back(h, chances, grad_chances)
     for result, index in results:
         place = start_of(index, result.shape[1])
         result[0] = out_s[place, :]
         result[1] = back_s[place, :]
 
 
-def attend(meta, listed, half_cosine, half_sine, mid, near, far, inputs, part, parts, before):
+def attend(meta, listed, half_cosine, half_sine, mid, near, far, inputs, heads):
     n = len(inputs)
     _, length, width = mid.shape
-    rows, whole = length // n, width * parts
-    window = pl.BlockSpec(mid.shape, lambda i: (0, 0, 0))
-    sums = pl.BlockSpec(mid.shape, lambda i: (0, 0, part))
-    source = pl.BlockSpec((2, rows, width), lambda i: (0, 0, 0))
-    target = pl.BlockSpec((2, rows, width), lambda i: (0, 0, part))
-    table = pl.BlockSpec(half_cosine.shape, lambda i: (0, 0))
+    rows, lanes = length // n, heads * HEAD_SIZE
     results = pl.pallas_call(
-        behind(functools.partial(attend_kernel, n, width // HEAD_SIZE), len(before)),
-        grid=(1,),
-        out_shape=[jax.ShapeDtypeStruct((2, rows, whole), jnp.bfloat16)] * n
-        + [jax.ShapeDtypeStruct((2, length, whole), jnp.float32)]
-        + [jax.ShapeDtypeStruct((2, length, whole), jnp.bfloat16)] * 2,
-        in_specs=[ANY_SPEC] * len(before)
-        + [SMEM_SPEC, SMEM_SPEC, table, table]
-        + [window] * 3
-        + [source] * n,
-        out_specs=[target] * n + [sums] * 3,
-        scratch_shapes=[pltpu.VMEM((length, width), jnp.bfloat16)] * 4,
-        input_output_aliases={t: t for t in range(len(before))},
+        functools.partial(attend_kernel, n, heads),
+        out_shape=[jax.ShapeDtypeStruct((2, rows, width), jnp.bfloat16)] * n
+        + [jax.ShapeDtypeStruct(mid.shape, jnp.float32)]
+        + [jax.ShapeDtypeStruct(mid.shape, jnp.bfloat16)] * 2,
+        in_specs=[SMEM_SPEC] * 2 + [VMEM_SPEC] * (5 + n),
+        out_specs=[VMEM_SPEC] * (n + 3),
+        scratch_shapes=[pltpu.VMEM((length, lanes), jnp.bfloat16)] * 4,
         compiler_params=params(),
         cost_estimate=cost(36 * length * length * width, 40 * length * width),
         name="attend",
-    )(*before, meta, listed, half_cosine, half_sine, mid, near, far, *inputs)
-    return results
+    )(meta, listed, half_cosine, half_sine, mid, near, far, *inputs)
+    return results[:n], *results[n:]
 
 
 def combine_kernel(meta, cosine, sine, own, from_near, from_far, *pieces):
@@ -317,7 +320,7 @@
         compiler_params=params(),
         cost_estimate=cost(0, 20 * length * width),
         name="combine",
-    )(meta, cosine, sine, own, from_near, from_far)
+    )(meta, cosine, sine, own, from_far, from_near)
 
 
 def join_kernel(n, meta, *refs):
@@ -369,32 +372,16 @@
     length = queries.shape[0] * n
     meta = jnp.stack([lax.axis_index("head"), lax.axis_index("seq")]).astype(jnp.int32)
     key_value = swap(cut(meta, chain_lengths, keys, values, n, WIDE_LIMIT))
-    laters = [
-        cut(meta, chain_lengths, queries, out_grad, n, VMEM_LIMIT, part, PARTS, [key_value[1]])
-        for part in range(PARTS)
-    ]
-    inputs = [swap(later) for later in laters]
-    mids = order(meta, key_value, PARTS, [later[0] for later in laters])
-    nears, fars = [trade(mid, 0) for mid in mids], [trade(mid, 1) for mid in mids]
-    cosine, sine, half_cosine, half_sine = tables(meta, chain_lengths, length, [inputs[0][1]])
-    sums = []
-    for part in range(PARTS):
-        sums = attend(
-            meta,
-            block_pairs,
-            half_cosine,
-            half_sine,
-            mids[part],
-            nears[part],
-            fars[part],
-            inputs[part],
-            part,
-            PARTS,
-            sums,
-        )
-    results, (own, near_sum, far_sum) = sums[:n], sums[n:]
+    later = cut(meta, chain_lengths, queries, out_grad, n, VMEM_LIMIT, [key_value[1]])
+    inputs = swap(later)
+    mid = order(meta, key_value, [later[0]])
+    near, far = trade(mid, 0), trade(mid, 1)
+    cosine, sine, half_cosine, half_sine = tables(meta, chain_lengths, length, [inputs[1]])
+    results, own, near_sum, far_sum = attend(
+        meta, block_pairs, half_cosine, half_sine, mid, near, far, inputs, HEADS_A_STEP
+    )
     attn_out, query_grad = join(meta, swap(results))
-    from_near, from_far = trade(near_sum, 0), trade(far_sum, 1)
+    from_far, from_near = trade(far_sum, 1), trade(near_sum, 0)
     back = swap(combine(meta, cosine, sine, own, from_near, from_far, n))
     key_grad, value_grad = join(meta, back)
     return attn_out, query_grad, key_grad, value_grad

time: 154 us -> 149 us (0.968)
  Pallas kernels: 25.1 us -> 21.8 us
    pallas_call x4, Pallas kernels: 18.7 us -> 15.4 us  [the longest x1 8.99 us: attend(): pl.pallas_call(functools.partial(attend_kernel, n, heads), out_shape=[jax...]
where the time goes in v2:
time: 149 us; the launch traced here: 148 us
  waiting for transfers between devices  105 us (70%)
  Pallas kernels  21.8 us (15%)
  starting transfers between devices  20.3 us (14%)
    ppermute x12, waiting for transfers between devices, swap(): lax.ppermute(pieces[k], 'head', [(i, i ^ k) for i in range(n)])  78.5 us
    ppermute x4, waiting for transfers between devices, trade(): return lax.ppermute(block, 'seq', route)  26.3 us
    ppermute x12, starting transfers between devices, swap(): lax.ppermute(pieces[k], 'head', [(i, i ^ k) for i in range(n)])  10.8 us
    ppermute x4, starting transfers between devices, trade(): return lax.ppermute(block, 'seq', route)  9.52 us
    pallas_call x1, Pallas kernels, attend(): pl.pallas_call(functools.partial(attend_kernel, n, heads), out_shape=[jax...  8.99 us
    pallas_call x2, Pallas kernels, cut(): pl.pallas_call(functools.partial(cut_kernel, n), out_shape=[jax.ShapeDtyp...  5.79 us
    pallas_call x2, Pallas kernels, join(): pl.pallas_call(functools.partial(join_kernel, n), out_shape=[jax.ShapeDty...  3.32 us
  transfers between devices with their start and end apart: 16, of which 10 were waited for; matrix products, arithmetic and copies ran while one was open for 0% of the time, Pallas kernels for 5%

profile of v2, /device:TPU:11, one launch (start us, length us, event | category | flops | bytes accessed | tf_op | source)
XLA Modules:
  0.0 148.5 jit_solution(8404593029887711359)
XLA Ops:
  0.6 0.0 copy-start.4
  0.6 0.0 copy-start.1
  0.7 0.0 copy-start
  0.7 0.7 pad_add_fusion.meta.refs_1_
  1.3 3.2 %cut.2 = (bf16[2,64,1280]{2,1,0:T(8,128)(2,1)}, bf16[2,64,1280]{2,1,0:T(8,128)(2,1)}, bf16[2,64,1280]{2,1,0:T(8,128)(2,1)}, bf16[2,64,1280]{2,1,0:T(8,128)(2,1)}) custom-call(s32[2]{0:T(128)} %pad_add_fusion.meta.refs_1_, s32[16]{0:T(128)} %refs_2_.1, bf16[64,5120]{1,0:T(8,128)(2,1)} %turned.2, bf16[64,5120]{1,0:T(8,128)(2,1)} %plain.2), custom_call_target="tpu_custom_call" | custom-call | bytes 2621440 | tf_op jit(solution)/shard_map/cut/pallas_call | solution.py:130
  4.6 0.0 copy-start.2
  4.6 0.2 collective-permute-start
  4.8 2.3 %collective-permute-start.2 = (bf16[2,64,1280]{2,1,0:T(8,128)(2,1)}, bf16[2,64,1280]{2,1,0:T(8,128)(2,1)S(1)}, u32[]{:S(2)}, u32[]{:S(2)}) collective-permute-start(bf16[2,64,1280]{2,1,0:T(8,128)(2,1)} %get-tuple-element.37), channel_id=1, source_target_pairs={{0,2},{1,3},{2,0},{3,1},{4,6},{5,7},{6,4},{7,5},{8,10},{9,11},{10,... | collective-permute-start | bytes 983048 | tf_op jit(solution)/shard_map/ppermute | solution.py:359
  7.1 0.2 collective-permute-start.3
  7.3 10.5 %collective-permute-done.refs_0_.refs_3_ = bf16[2,64,1280]{2,1,0:T(8,128)(2,1)S(1)} collective-permute-done((bf16[2,64,1280]{2,1,0:T(8,128)(2,1)}, bf16[2,64,1280]{2,1,0:T(8,128)(2,1)S(1)}, u32[]{:S(2)}, u32[]{:S(2)}) %collective-permute-start) | collective-permute-done | bytes 327712 | tf_op jit(solution)/shard_map/ppermute | solution.py:359
  17.8 0.0 copy-done.4
  17.8 0.0 copy-done.1
  17.8 2.5 %cut.3 = (bf16[2,64,1280]{2,1,0:T(8,128)(2,1)S(1)}, bf16[2,64,1280]{2,1,0:T(8,128)(2,1)}, bf16[2,64,1280]{2,1,0:T(8,128)(2,1)}, bf16[2,64,1280]{2,1,0:T(8,128)(2,1)}) custom-call(s32[2]{0:T(128)S(1)} %copy-done.3, s32[16]{0:T(128)S(1)} %copy-done.4, bf16[64,5120]{1,0:T(8,128)(2,1)S(1)} %copy-done, bf16[64,5120]{1,0:T(8,128)(2,1)S(1)} %copy-done.1, ...), custom_call_target="tpu_custom_call" | custom-call | bytes 2621440 | tf_op jit(solution)/shard_map/cut/pallas_call | solution.py:130
  20.3 1.2 collective-permute-done.2.refs_4_
  21.5 13.9 %collective-permute-done.3.refs_5_ = bf16[2,64,1280]{2,1,0:T(8,128)(2,1)S(1)} collective-permute-done((bf16[2,64,1280]{2,1,0:T(8,128)(2,1)}, bf16[2,64,1280]{2,1,0:T(8,128)(2,1)S(1)}, u32[]{:S(2)}, u32[]{:S(2)}) %collective-permute-start.3) | collective-permute-done | bytes 327712 | tf_op jit(solution)/shard_map/ppermute | solution.py:359
  35.5 0.6 order.1.mid
  36.1 4.8 %collective-permute-start.5 = (bf16[2,256,1280]{2,1,0:T(8,128)(2,1)S(1)}, bf16[2,256,1280]{2,1,0:T(8,128)(2,1)S(1)}, u32[]{:S(2)}, u32[]{:S(2)}) collective-permute-start(bf16[2,256,1280]{2,1,0:T(8,128)(2,1)S(1)} %order.1.mid), channel_id=1, source_target_pairs={{4,8},{8,4},{12,16},{16,12},{20,24},{24,20},{5,9},{9,5},{13,17},{1... | collective-permute-start | bytes 3932168 | tf_op jit(solution)/shard_map/ppermute | solution.py:367
  41.0 0.1 collective-permute-start.4
  41.0 0.1 collective-permute-start.1
  41.1 2.5 %collective-permute-start.6 = (bf16[2,64,1280]{2,1,0:T(8,128)(2,1)}, bf16[2,64,1280]{2,1,0:T(8,128)(2,1)}, u32[]{:S(2)}, u32[]{:S(2)}) collective-permute-start(bf16[2,64,1280]{2,1,0:T(8,128)(2,1)} %get-tuple-element.39), channel_id=1, source_target_pairs={{0,2},{1,3},{2,0},{3,1},{4,6},{5,7},{6,4},{7,5},{8,10},{9,11},{10,... | collective-permute-start | bytes 983048 | tf_op jit(solution)/shard_map/ppermute | solution.py:359
  43.6 0.2 collective-permute-start.7
  43.8 0.1 copy.10.listed
  43.8 11.0 %collective-permute-done.1.refs_0_.refs_1_ = bf16[2,64,1280]{2,1,0:T(8,128)(2,1)S(1)} collective-permute-done((bf16[2,64,1280]{2,1,0:T(8,128)(2,1)}, bf16[2,64,1280]{2,1,0:T(8,128)(2,1)S(1)}, u32[]{:S(2)}, u32[]{:S(2)}) %collective-permute-start.1) | collective-permute-done | bytes 327712 | tf_op jit(solution)/shard_map/ppermute | solution.py:359
  54.8 1.8 %tables.1 = (f32[256,128]{1,0:T(8,128)S(1)}, f32[256,128]{1,0:T(8,128)S(1)}, f32[64,256]{1,0:T(8,128)S(1)}, f32[64,256]{1,0:T(8,128)S(1)}) custom-call(bf16[2,64,1280]{2,1,0:T(8,128)(2,1)S(1)} %collective-permute-done.1.refs_0_.refs_1_, s32[2]{0:T(128)S(1)} %copy-done.3, s32[16]{0:T(128)S(1)} %copy-done.4), custom_call_target="tpu_custom_call" | custom-call | bytes 262144 | tf_op jit(solution)/shard_map/tables/pallas_call | solution.py:156
  56.6 1.7 %collective-permute-done.6.refs_2_ = bf16[2,64,1280]{2,1,0:T(8,128)(2,1)} collective-permute-done((bf16[2,64,1280]{2,1,0:T(8,128)(2,1)}, bf16[2,64,1280]{2,1,0:T(8,128)(2,1)}, u32[]{:S(2)}, u32[]{:S(2)}) %collective-permute-start.6) | collective-permute-done | bytes 327712 | tf_op jit(solution)/shard_map/ppermute | solution.py:359
  58.3 14.0 %collective-permute-done.7.refs_3_ = bf16[2,64,1280]{2,1,0:T(8,128)(2,1)} collective-permute-done((bf16[2,64,1280]{2,1,0:T(8,128)(2,1)}, bf16[2,64,1280]{2,1,0:T(8,128)(2,1)}, u32[]{:S(2)}, u32[]{:S(2)}) %collective-permute-start.7) | collective-permute-done | bytes 327712 | tf_op jit(solution)/shard_map/ppermute | solution.py:359
  72.3 0.0 collective-permute-done.5.far
  72.3 0.0 collective-permute-done.4.near
  72.3 9.0 %attend.1 = (bf16[2,64,1280]{2,1,0:T(8,128)(2,1)S(1)}, bf16[2,64,1280]{2,1,0:T(8,128)(2,1)S(1)}, bf16[2,64,1280]{2,1,0:T(8,128)(2,1)S(1)}, bf16[2,64,1280]{2,1,0...) custom-call(s32[2]{0:T(128)S(1)} %copy-done.3, ...), custom_call_target="tpu_custom_call" | custom-call | flops 3019898880 | bytes 13107200 | tf_op jit(solution)/shard_map/attend/pallas_call | solution.py:282
  81.3 4.5 %collective-permute-start.11 = (bf16[2,256,1280]{2,1,0:T(8,128)(2,1)S(1)}, bf16[2,256,1280]{2,1,0:T(8,128)(2,1)S(1)}, u32[]{:S(2)}, u32[]{:S(2)}) collective-permute-start(bf16[2,256,1280]{2,1,0:T(8,128)(2,1)S(1)} %get-tuple-element.50), channel_id=1, source_target_pairs={{4,8},{8,4},{12,16},{16,12},{20,24},{24,20},{5,9},{9,5},{13,17},{1... | collective-permute-start | bytes 3932168 | tf_op jit(solution)/shard_map/ppermute | solution.py:367
  85.9 0.1 collective-permute-start.12
  85.9 0.1 collective-permute-start.8
  86.0 2.5 %collective-permute-start.9 = (bf16[2,64,1280]{2,1,0:T(8,128)(2,1)S(1)}, bf16[2,64,1280]{2,1,0:T(8,128)(2,1)S(1)}, u32[]{:S(2)}, u32[]{:S(2)}) collective-permute-start(bf16[2,64,1280]{2,1,0:T(8,128)(2,1)S(1)} %get-tuple-element.43), channel_id=1, source_target_pairs={{0,2},{1,3},{2,0},{3,1},{4,6},{5,7},{6,4},{7,5},{8,10},{9,11},{10,... | collective-permute-start | bytes 983048 | tf_op jit(solution)/shard_map/ppermute | solution.py:359
  88.5 0.2 collective-permute-start.10
  88.7 26.3 %collective-permute-done.11.from_near = bf16[2,256,1280]{2,1,0:T(8,128)(2,1)S(1)} collective-permute-done((bf16[2,256,1280]{2,1,0:T(8,128)(2,1)S(1)}, bf16[2,256,1280]{2,1,0:T(8,128)(2,1)S(1)}, u32[]{:S(2)}, u32[]{:S(2)}) %collective-permute-start.11) | collective-permute-done | bytes 1310752 | tf_op jit(solution)/shard_map/ppermute | solution.py:367
  114.9 0.0 collective-permute-done.12.from_far
  114.9 1.2 combine.1
  116.2 0.1 collective-permute-start.13
  116.3 2.5 %collective-permute-start.14 = (bf16[2,64,1280]{2,1,0:T(8,128)(2,1)S(1)}, bf16[2,64,1280]{2,1,0:T(8,128)(2,1)S(1)}, u32[]{:S(2)}, u32[]{:S(2)}) collective-permute-start(bf16[2,64,1280]{2,1,0:T(8,128)(2,1)S(1)} %get-tuple-element.54), channel_id=1, source_target_pairs={{0,2},{1,3},{2,0},{3,1},{4,6},{5,7},{6,4},{7,5},{8,10},{9,11},{10,... | collective-permute-start | bytes 983048 | tf_op jit(solution)/shard_map/ppermute | solution.py:359
  118.7 0.0 collective-permute-done.8.refs_1_
  118.7 0.2 collective-permute-start.15
  118.9 0.0 collective-permute-done.9.refs_2_
  118.9 0.0 collective-permute-done.10.refs_3_
  118.9 1.7 %join.2 = (bf16[64,5120]{1,0:T(8,128)(2,1)}, bf16[64,5120]{1,0:T(8,128)(2,1)}) custom-call(s32[2]{0:T(128)S(1)} %copy-done.3, bf16[2,64,1280]{2,1,0:T(8,128)(2,1)S(1)} %get-tuple-element.41.refs_0_, bf16[2,64,1280]{2,1,0:T(8,128)(2,1)S(1)} %collective-permute-done.8.refs_1_, bf16[2,64,1280]{2,1,0:T(8,128)(2,1)S(1)} %collective-permute-done.9.refs_2_, ...), custom_call_target="tpu_custom_call" | custom-call | bytes 2621440 | tf_op jit(solution)/shard_map/join/pallas_call | solution.py:342
  120.6 7.7 %collective-permute-done.13.refs_1_ = bf16[2,64,1280]{2,1,0:T(8,128)(2,1)S(1)} collective-permute-done((bf16[2,64,1280]{2,1,0:T(8,128)(2,1)S(1)}, bf16[2,64,1280]{2,1,0:T(8,128)(2,1)S(1)}, u32[]{:S(2)}, u32[]{:S(2)}) %collective-permute-start.13) | collective-permute-done | bytes 327712 | tf_op jit(solution)/shard_map/ppermute | solution.py:359
  128.3 12.0 %collective-permute-done.14.refs_2_ = bf16[2,64,1280]{2,1,0:T(8,128)(2,1)S(1)} collective-permute-done((bf16[2,64,1280]{2,1,0:T(8,128)(2,1)S(1)}, bf16[2,64,1280]{2,1,0:T(8,128)(2,1)S(1)}, u32[]{:S(2)}, u32[]{:S(2)}) %collective-permute-start.14) | collective-permute-done | bytes 327712 | tf_op jit(solution)/shard_map/ppermute | solution.py:359
  140.3 6.5 %collective-permute-done.15.refs_3_ = bf16[2,64,1280]{2,1,0:T(8,128)(2,1)S(1)} collective-permute-done((bf16[2,64,1280]{2,1,0:T(8,128)(2,1)S(1)}, bf16[2,64,1280]{2,1,0:T(8,128)(2,1)S(1)}, u32[]{:S(2)}, u32[]{:S(2)}) %collective-permute-start.15) | collective-permute-done | bytes 327712 | tf_op jit(solution)/shard_map/ppermute | solution.py:359
  146.8 1.7 %join.3 = (bf16[64,5120]{1,0:T(8,128)(2,1)}, bf16[64,5120]{1,0:T(8,128)(2,1)}) custom-call(s32[2]{0:T(128)S(1)} %copy-done.3, bf16[2,64,1280]{2,1,0:T(8,128)(2,1)S(1)} %get-tuple-element.52.refs_0_, bf16[2,64,1280]{2,1,0:T(8,128)(2,1)S(1)} %collective-permute-done.13.refs_1_, bf16[2,64,1280]{2,1,0:T(8,128)(2,1)S(1)} %collective-permute-done.14.refs_2_, ...), custom_call_target="tpu_custom_call" | custom-call | bytes 2621440 | tf_op jit(solution)/shard_map/join/pallas_call | solution.py:342
  (6 shorter events, 0.0 us)
Async XLA Ops:
  0.6 17.2 %copy-start.4 = (s32[16]{0:T(128)S(1)}, s32[16]{0:T(128)}, u32[]{:S(2)}) copy-start(s32[16]{0:T(128)} %refs_2_.1) | copy-start | bytes 196
  0.6 17.1 %copy-start.1 = (bf16[64,5120]{1,0:T(8,128)(2,1)S(1)}, bf16[64,5120]{1,0:T(8,128)(2,1)}, u32[]{:S(2)}) copy-start(bf16[64,5120]{1,0:T(8,128)(2,1)} %plain.3) | copy-start | bytes 1966084
  0.7 17.1 %copy-start = (bf16[64,5120]{1,0:T(8,128)(2,1)S(1)}, bf16[64,5120]{1,0:T(8,128)(2,1)}, u32[]{:S(2)}) copy-start(bf16[64,5120]{1,0:T(8,128)(2,1)} %turned.3) | copy-start | bytes 1966084
  1.3 16.5 %copy-start.3 = (s32[2]{0:T(128)S(1)}, s32[2]{0:T(128)}, u32[]{:S(2)}) copy-start(s32[2]{0:T(128)} %pad_add_fusion.meta.refs_1_) | copy-start | bytes 28
  4.6 30.9 %copy-start.2 = (bf16[2,64,1280]{2,1,0:T(8,128)(2,1)S(1)}, bf16[2,64,1280]{2,1,0:T(8,128)(2,1)}, u32[]{:S(2)}) copy-start(bf16[2,64,1280]{2,1,0:T(8,128)(2,1)} %get-tuple-element.36.refs_2_) | copy-start | bytes 983044
  4.6 13.2 %collective-permute-start = (bf16[2,64,1280]{2,1,0:T(8,128)(2,1)}, bf16[2,64,1280]{2,1,0:T(8,128)(2,1)S(1)}, u32[]{:S(2)}, u32[]{:S(2)}) collective-permute-start(bf16[2,64,1280]{2,1,0:T(8,128)(2,1)} %get-tuple-element.31), channel_id=1, source_target_pairs={{0,1},{1,0},{2,3},{3,2},{4,5},{5,4},{6,7},{7,6},{8,9},{9,8},{10,11... | collective-permute-start | bytes 983048 | tf_op jit(solution)/shard_map/ppermute | solution.py:359
  4.8 16.7 %collective-permute-start.2 = (bf16[2,64,1280]{2,1,0:T(8,128)(2,1)}, bf16[2,64,1280]{2,1,0:T(8,128)(2,1)S(1)}, u32[]{:S(2)}, u32[]{:S(2)}) collective-permute-start(bf16[2,64,1280]{2,1,0:T(8,128)(2,1)} %get-tuple-element.37), channel_id=1, source_target_pairs={{0,2},{1,3},{2,0},{3,1},{4,6},{5,7},{6,4},{7,5},{8,10},{9,11},{10,... | collective-permute-start | bytes 983048 | tf_op jit(solution)/shard_map/ppermute | solution.py:359
  7.1 28.3 %collective-permute-start.3 = (bf16[2,64,1280]{2,1,0:T(8,128)(2,1)}, bf16[2,64,1280]{2,1,0:T(8,128)(2,1)S(1)}, u32[]{:S(2)}, u32[]{:S(2)}) collective-permute-start(bf16[2,64,1280]{2,1,0:T(8,128)(2,1)} %get-tuple-element.38), channel_id=1, source_target_pairs={{0,3},{1,2},{2,1},{3,0},{4,7},{5,6},{6,5},{7,4},{8,11},{9,10},{10,... | collective-permute-start | bytes 983048 | tf_op jit(solution)/shard_map/ppermute | solution.py:359
  35.5 8.3 %copy-start.5 = (s32[16,4]{0,1:T(4,128)S(1)}, s32[16,4]{0,1:T(4,128)}, u32[]{:S(2)}) copy-start(s32[16,4]{0,1:T(4,128)} %param.11) | copy-start | bytes 772
  36.1 36.2 %collective-permute-start.5 = (bf16[2,256,1280]{2,1,0:T(8,128)(2,1)S(1)}, bf16[2,256,1280]{2,1,0:T(8,128)(2,1)S(1)}, u32[]{:S(2)}, u32[]{:S(2)}) collective-permute-start(bf16[2,256,1280]{2,1,0:T(8,128)(2,1)S(1)} %order.1.mid), channel_id=1, source_target_pairs={{4,8},{8,4},{12,16},{16,12},{20,24},{24,20},{5,9},{9,5},{13,17},{1... | collective-permute-start | bytes 3932168 | tf_op jit(solution)/shard_map/ppermute | solution.py:367
  41.0 31.3 %collective-permute-start.4 = (bf16[2,256,1280]{2,1,0:T(8,128)(2,1)S(1)}, bf16[2,256,1280]{2,1,0:T(8,128)(2,1)}, u32[]{:S(2)}, u32[]{:S(2)}) collective-permute-start(bf16[2,256,1280]{2,1,0:T(8,128)(2,1)S(1)} %order.1.mid), channel_id=1, source_target_pairs={{0,4},{4,0},{8,12},{12,8},{16,20},{20,16},{24,28},{28,24},{1,5},{5... | collective-permute-start | bytes 3932168 | tf_op jit(solution)/shard_map/ppermute | solution.py:367
  41.0 13.8 %collective-permute-start.1 = (bf16[2,64,1280]{2,1,0:T(8,128)(2,1)}, bf16[2,64,1280]{2,1,0:T(8,128)(2,1)S(1)}, u32[]{:S(2)}, u32[]{:S(2)}) collective-permute-start(bf16[2,64,1280]{2,1,0:T(8,128)(2,1)} %get-tuple-element.32), channel_id=1, source_target_pairs={{0,1},{1,0},{2,3},{3,2},{4,5},{5,4},{6,7},{7,6},{8,9},{9,8},{10,11... | collective-permute-start | bytes 983048 | tf_op jit(solution)/shard_map/ppermute | solution.py:359
  41.1 17.2 %collective-permute-start.6 = (bf16[2,64,1280]{2,1,0:T(8,128)(2,1)}, bf16[2,64,1280]{2,1,0:T(8,128)(2,1)}, u32[]{:S(2)}, u32[]{:S(2)}) collective-permute-start(bf16[2,64,1280]{2,1,0:T(8,128)(2,1)} %get-tuple-element.39), channel_id=1, source_target_pairs={{0,2},{1,3},{2,0},{3,1},{4,6},{5,7},{6,4},{7,5},{8,10},{9,11},{10,... | collective-permute-start | bytes 983048 | tf_op jit(solution)/shard_map/ppermute | solution.py:359
  43.6 28.7 %collective-permute-start.7 = (bf16[2,64,1280]{2,1,0:T(8,128)(2,1)}, bf16[2,64,1280]{2,1,0:T(8,128)(2,1)}, u32[]{:S(2)}, u32[]{:S(2)}) collective-permute-start(bf16[2,64,1280]{2,1,0:T(8,128)(2,1)} %get-tuple-element.40), channel_id=1, source_target_pairs={{0,3},{1,2},{2,1},{3,0},{4,7},{5,6},{6,5},{7,4},{8,11},{9,10},{10,... | collective-permute-start | bytes 983048 | tf_op jit(solution)/shard_map/ppermute | solution.py:359
  81.3 33.6 %collective-permute-start.11 = (bf16[2,256,1280]{2,1,0:T(8,128)(2,1)S(1)}, bf16[2,256,1280]{2,1,0:T(8,128)(2,1)S(1)}, u32[]{:S(2)}, u32[]{:S(2)}) collective-permute-start(bf16[2,256,1280]{2,1,0:T(8,128)(2,1)S(1)} %get-tuple-element.50), channel_id=1, source_target_pairs={{4,8},{8,4},{12,16},{16,12},{20,24},{24,20},{5,9},{9,5},{13,17},{1... | collective-permute-start | bytes 3932168 | tf_op jit(solution)/shard_map/ppermute | solution.py:367
  85.9 29.1 %collective-permute-start.12 = (bf16[2,256,1280]{2,1,0:T(8,128)(2,1)S(1)}, bf16[2,256,1280]{2,1,0:T(8,128)(2,1)S(1)}, u32[]{:S(2)}, u32[]{:S(2)}) collective-permute-start(bf16[2,256,1280]{2,1,0:T(8,128)(2,1)S(1)} %get-tuple-element.51), channel_id=1, source_target_pairs={{0,4},{4,0},{8,12},{12,8},{16,20},{20,16},{24,28},{28,24},{1,5},{5... | collective-permute-start | bytes 3932168 | tf_op jit(solution)/shard_map/ppermute | solution.py:367
  85.9 32.8 %collective-permute-start.8 = (bf16[2,64,1280]{2,1,0:T(8,128)(2,1)S(1)}, bf16[2,64,1280]{2,1,0:T(8,128)(2,1)S(1)}, u32[]{:S(2)}, u32[]{:S(2)}) collective-permute-start(bf16[2,64,1280]{2,1,0:T(8,128)(2,1)S(1)} %get-tuple-element.42), channel_id=1, source_target_pairs={{0,1},{1,0},{2,3},{3,2},{4,5},{5,4},{6,7},{7,6},{8,9},{9,8},{10,11... | collective-permute-start | bytes 983048 | tf_op jit(solution)/shard_map/ppermute | solution.py:359
  86.0 32.9 %collective-permute-start.9 = (bf16[2,64,1280]{2,1,0:T(8,128)(2,1)S(1)}, bf16[2,64,1280]{2,1,0:T(8,128)(2,1)S(1)}, u32[]{:S(2)}, u32[]{:S(2)}) collective-permute-start(bf16[2,64,1280]{2,1,0:T(8,128)(2,1)S(1)} %get-tuple-element.43), channel_id=1, source_target_pairs={{0,2},{1,3},{2,0},{3,1},{4,6},{5,7},{6,4},{7,5},{8,10},{9,11},{10,... | collective-permute-start | bytes 983048 | tf_op jit(solution)/shard_map/ppermute | solution.py:359
  88.5 30.4 %collective-permute-start.10 = (bf16[2,64,1280]{2,1,0:T(8,128)(2,1)S(1)}, bf16[2,64,1280]{2,1,0:T(8,128)(2,1)S(1)}, u32[]{:S(2)}, u32[]{:S(2)}) collective-permute-start(bf16[2,64,1280]{2,1,0:T(8,128)(2,1)S(1)} %get-tuple-element.44), channel_id=1, source_target_pairs={{0,3},{1,2},{2,1},{3,0},{4,7},{5,6},{6,5},{7,4},{8,11},{9,10},{10,... | collective-permute-start | bytes 983048 | tf_op jit(solution)/shard_map/ppermute | solution.py:359
  116.2 12.1 %collective-permute-start.13 = (bf16[2,64,1280]{2,1,0:T(8,128)(2,1)S(1)}, bf16[2,64,1280]{2,1,0:T(8,128)(2,1)S(1)}, u32[]{:S(2)}, u32[]{:S(2)}) collective-permute-start(bf16[2,64,1280]{2,1,0:T(8,128)(2,1)S(1)} %get-tuple-element.53), channel_id=1, source_target_pairs={{0,1},{1,0},{2,3},{3,2},{4,5},{5,4},{6,7},{7,6},{8,9},{9,8},{10,11... | collective-permute-start | bytes 983048 | tf_op jit(solution)/shard_map/ppermute | solution.py:359
  116.3 24.0 %collective-permute-start.14 = (bf16[2,64,1280]{2,1,0:T(8,128)(2,1)S(1)}, bf16[2,64,1280]{2,1,0:T(8,128)(2,1)S(1)}, u32[]{:S(2)}, u32[]{:S(2)}) collective-permute-start(bf16[2,64,1280]{2,1,0:T(8,128)(2,1)S(1)} %get-tuple-element.54), channel_id=1, source_target_pairs={{0,2},{1,3},{2,0},{3,1},{4,6},{5,7},{6,4},{7,5},{8,10},{9,11},{10,... | collective-permute-start | bytes 983048 | tf_op jit(solution)/shard_map/ppermute | solution.py:359
  118.7 28.1 %collective-permute-start.15 = (bf16[2,64,1280]{2,1,0:T(8,128)(2,1)S(1)}, bf16[2,64,1280]{2,1,0:T(8,128)(2,1)S(1)}, u32[]{:S(2)}, u32[]{:S(2)}) collective-permute-start(bf16[2,64,1280]{2,1,0:T(8,128)(2,1)S(1)} %get-tuple-element.55), channel_id=1, source_target_pairs={{0,3},{1,2},{2,1},{3,0},{4,7},{5,6},{6,5},{7,4},{8,11},{9,10},{10,... | collective-permute-start | bytes 983048 | tf_op jit(solution)/shard_map/ppermute | solution.py:359

commit v3 on v2

--- a/solution.py
+++ b/solution.py
@@ -93,6 +93,22 @@
     if joined:
         return [pl.BlockSpec((n,) + shape, lambda *i: (0,) + index_map(*i))]
     return [pl.BlockSpec(shape, index_map)] * n
+
+
+def again_kernel(value, out):
+    out[...] = value[...]
+
+
+def again(value, after):
+    return pl.pallas_call(
+        behind(again_kernel, len(after)),
+        out_shape=jax.ShapeDtypeStruct(value.shape, value.dtype),
+        in_specs=[ANY_SPEC] * len(after) + [VMEM_SPEC],
+        out_specs=VMEM_SPEC,
+        compiler_params=params(),
+        cost_estimate=cost(0, 2 * value.size),
+        name="again",
+    )(*after, value)
 
 
 def dot(a, b, contract):
@@ -375,12 +391,13 @@
     later = cut(meta, chain_lengths, queries, out_grad, n, VMEM_LIMIT, [key_value[1]])
     inputs = swap(later)
     mid = order(meta, key_value, [later[0]])
-    near, far = trade(mid, 0), trade(mid, 1)
+    far, near = trade(mid, 1), trade(again(mid, [inputs[1]]), 0)
     cosine, sine, half_cosine, half_sine = tables(meta, chain_lengths, length, [inputs[1]])
     results, own, near_sum, far_sum = attend(
         meta, block_pairs, half_cosine, half_sine, mid, near, far, inputs, HEADS_A_STEP
     )
-    attn_out, query_grad = join(meta, swap(results))
+    back_out = swap(results)
+    attn_out, query_grad = join(meta, back_out)
     from_far, from_near = trade(far_sum, 1), trade(near_sum, 0)
     back = swap(combine(meta, cosine, sine, own, from_near, from_far, n))
     key_grad, value_grad = join(meta, back)

time: 149 us -> 148 us (level)
  waiting for transfers between devices: 105 us -> 103 us
    ppermute x12, waiting for transfers between devices: 78.5 us -> 76.9 us  [swap(): lax.ppermute(pieces[k], 'head', [(i, i ^ k) for i in range(n)])]
  transfers between devices with their start and end apart: 16 -> 16, of which waited for: 10 -> 8; matrix products, arithmetic and copies ran while one was open for 0% -> 0% of each run, Pallas kernels for 5% -> 5%
where the time goes in v3:
time: 148 us
  waiting for transfers between devices  103 us (70%)
  Pallas kernels  22.2 us (15%)
  starting transfers between devices  20.7 us (14%)
    ppermute x12, waiting for transfers between devices, swap(): lax.ppermute(pieces[k], 'head', [(i, i ^ k) for i in range(n)])  76.9 us
    ppermute x4, waiting for transfers between devices, trade(): return lax.ppermute(block, 'seq', route)  26.3 us
    ppermute x12, starting transfers between devices, swap(): lax.ppermute(pieces[k], 'head', [(i, i ^ k) for i in range(n)])  11.7 us
    pallas_call x1, Pallas kernels, attend(): pl.pallas_call(functools.partial(attend_kernel, n, heads), out_shape=[jax...  9.42 us
    ppermute x4, starting transfers between devices, trade(): return lax.ppermute(block, 'seq', route)  8.93 us
    pallas_call x2, Pallas kernels, cut(): pl.pallas_call(functools.partial(cut_kernel, n), out_shape=[jax.ShapeDtyp...  5.67 us
    pallas_call x2, Pallas kernels, join(): pl.pallas_call(functools.partial(join_kernel, n), out_shape=[jax.ShapeDty...  3.32 us
  transfers between devices with their start and end apart: 16, of which 8 were waited for; matrix products, arithmetic and copies ran while one was open for 0% of the time, Pallas kernels for 5%

profile of v3, /device:TPU:11, one launch (start us, length us, event | category | flops | bytes accessed | tf_op | source)
XLA Modules:
  0.0 147.7 jit_solution(7933445605261451985)
XLA Ops:
  0.6 0.0 copy-start.4
  0.7 0.7 pad_add_fusion.meta.refs_1_
  1.3 3.2 %cut.2 = (bf16[2,64,1280]{2,1,0:T(8,128)(2,1)}, bf16[2,64,1280]{2,1,0:T(8,128)(2,1)}, bf16[2,64,1280]{2,1,0:T(8,128)(2,1)}, bf16[2,64,1280]{2,1,0:T(8,128)(2,1)}) custom-call(s32[2]{0:T(128)} %pad_add_fusion.meta.refs_1_, s32[16]{0:T(128)} %refs_2_.1, bf16[64,5120]{1,0:T(8,128)(2,1)} %turned.2, bf16[64,5120]{1,0:T(8,128)(2,1)} %plain.2), custom_call_target="tpu_custom_call" | custom-call | bytes 2621440 | tf_op jit(solution)/shard_map/cut/pallas_call | solution.py:146
  4.6 0.0 copy-start.2
  4.6 0.2 collective-permute-start
  4.8 2.3 %collective-permute-start.2 = (bf16[2,64,1280]{2,1,0:T(8,128)(2,1)}, bf16[2,64,1280]{2,1,0:T(8,128)(2,1)S(1)}, u32[]{:S(2)}, u32[]{:S(2)}) collective-permute-start(bf16[2,64,1280]{2,1,0:T(8,128)(2,1)} %get-tuple-element.37), channel_id=1, source_target_pairs={{0,2},{1,3},{2,0},{3,1},{4,6},{5,7},{6,4},{7,5},{8,10},{9,11},{10,... | collective-permute-start | bytes 983048 | tf_op jit(solution)/shard_map/ppermute | solution.py:375
  7.1 0.2 collective-permute-start.3
  7.3 10.5 %collective-permute-done.refs_0_.refs_3_ = bf16[2,64,1280]{2,1,0:T(8,128)(2,1)S(1)} collective-permute-done((bf16[2,64,1280]{2,1,0:T(8,128)(2,1)}, bf16[2,64,1280]{2,1,0:T(8,128)(2,1)S(1)}, u32[]{:S(2)}, u32[]{:S(2)}) %collective-permute-start) | collective-permute-done | bytes 327712 | tf_op jit(solution)/shard_map/ppermute | solution.py:375
  17.8 0.0 copy-done.4
  17.8 2.4 %cut.3 = (bf16[2,64,1280]{2,1,0:T(8,128)(2,1)S(1)}, bf16[2,64,1280]{2,1,0:T(8,128)(2,1)S(1)}, bf16[2,64,1280]{2,1,0:T(8,128)(2,1)}, bf16[2,64,1280]{2,1,0:T(8,128)(2,1)}) custom-call(s32[2]{0:T(128)S(1)} %copy-done.3, s32[16]{0:T(128)S(1)} %copy-done.4, bf16[64,5120]{1,0:T(8,128)(2,1)S(1)} %copy-done, bf16[64,5120]{1,0:T(8,128)(2,1)S(1)} %copy-done.1, ...), custom_call_target="tpu_custom_call" | custom-call | bytes 2621440 | tf_op jit(solution)/shard_map/cut/pallas_call | solution.py:146
  20.2 2.2 %collective-permute-start.1 = (bf16[2,64,1280]{2,1,0:T(8,128)(2,1)S(1)}, bf16[2,64,1280]{2,1,0:T(8,128)(2,1)S(1)}, u32[]{:S(2)}, u32[]{:S(2)}) collective-permute-start(bf16[2,64,1280]{2,1,0:T(8,128)(2,1)S(1)} %get-tuple-element.32), channel_id=1, source_target_pairs={{0,1},{1,0},{2,3},{3,2},{4,5},{5,4},{6,7},{7,6},{8,9},{9,8},{10,11... | collective-permute-start | bytes 983048 | tf_op jit(solution)/shard_map/ppermute | solution.py:375
  22.4 0.0 collective-permute-done.2.refs_4_
  22.4 13.1 %collective-permute-done.3.refs_5_ = bf16[2,64,1280]{2,1,0:T(8,128)(2,1)S(1)} collective-permute-done((bf16[2,64,1280]{2,1,0:T(8,128)(2,1)}, bf16[2,64,1280]{2,1,0:T(8,128)(2,1)S(1)}, u32[]{:S(2)}, u32[]{:S(2)}) %collective-permute-start.3) | collective-permute-done | bytes 327712 | tf_op jit(solution)/shard_map/ppermute | solution.py:375
  35.5 0.0 copy-done.2
  35.5 0.6 order.1.refs_1_.mid
  36.2 0.0 copy-start.5
  36.2 4.8 %collective-permute-start.5 = (bf16[2,256,1280]{2,1,0:T(8,128)(2,1)S(1)}, bf16[2,256,1280]{2,1,0:T(8,128)(2,1)}, u32[]{:S(2)}, u32[]{:S(2)}) collective-permute-start(bf16[2,256,1280]{2,1,0:T(8,128)(2,1)S(1)} %order.1.refs_1_.mid), channel_id=1, source_target_pairs={{4,8},{8,4},{12,16},{16,12},{20,24},{24,20},{5,9},{9,5},{13,17},{1... | collective-permute-start | bytes 3932168 | tf_op jit(solution)/shard_map/ppermute | solution.py:383
  41.0 0.0 collective-permute-done.1.refs_0_.refs_1_
  41.0 0.1 again.1
  41.1 0.1 collective-permute-start.4
  41.2 0.1 collective-permute-start.6
  41.3 1.4 collective-permute-start.7
  42.6 0.1 copy.10.listed
  42.7 1.8 %tables.1 = (f32[256,128]{1,0:T(8,128)S(1)}, f32[256,128]{1,0:T(8,128)S(1)}, f32[64,256]{1,0:T(8,128)S(1)}, f32[64,256]{1,0:T(8,128)S(1)}) custom-call(bf16[2,64,1280]{2,1,0:T(8,128)(2,1)S(1)} %collective-permute-done.1.refs_0_.refs_1_, s32[2]{0:T(128)S(1)} %copy-done.3, s32[16]{0:T(128)S(1)} %copy-done.4), custom_call_target="tpu_custom_call" | custom-call | bytes 262144 | tf_op jit(solution)/shard_map/tables/pallas_call | solution.py:172
  44.6 18.0 %collective-permute-done.6.refs_2_ = bf16[2,64,1280]{2,1,0:T(8,128)(2,1)} collective-permute-done((bf16[2,64,1280]{2,1,0:T(8,128)(2,1)}, bf16[2,64,1280]{2,1,0:T(8,128)(2,1)}, u32[]{:S(2)}, u32[]{:S(2)}) %collective-permute-start.6) | collective-permute-done | bytes 327712 | tf_op jit(solution)/shard_map/ppermute | solution.py:375
  62.6 9.1 %collective-permute-done.7.refs_3_ = bf16[2,64,1280]{2,1,0:T(8,128)(2,1)} collective-permute-done((bf16[2,64,1280]{2,1,0:T(8,128)(2,1)}, bf16[2,64,1280]{2,1,0:T(8,128)(2,1)}, u32[]{:S(2)}, u32[]{:S(2)}) %collective-permute-start.7) | collective-permute-done | bytes 327712 | tf_op jit(solution)/shard_map/ppermute | solution.py:375
  71.7 0.0 collective-permute-done.5.far
  71.7 0.0 collective-permute-done.4.near
  71.7 9.4 %attend.1 = (bf16[2,64,1280]{2,1,0:T(8,128)(2,1)S(1)}, bf16[2,64,1280]{2,1,0:T(8,128)(2,1)S(1)}, bf16[2,64,1280]{2,1,0:T(8,128)(2,1)S(1)}, bf16[2,64,1280]{2,1,0...) custom-call(s32[2]{0:T(128)S(1)} %copy-done.3, ...), custom_call_target="tpu_custom_call" | custom-call | flops 3019898880 | bytes 13107200 | tf_op jit(solution)/shard_map/attend/pallas_call | solution.py:298
  81.1 4.0 %collective-permute-start.11 = (bf16[2,256,1280]{2,1,0:T(8,128)(2,1)S(1)}, bf16[2,256,1280]{2,1,0:T(8,128)(2,1)S(1)}, u32[]{:S(2)}, u32[]{:S(2)}) collective-permute-start(bf16[2,256,1280]{2,1,0:T(8,128)(2,1)S(1)} %get-tuple-element.50), channel_id=1, source_target_pairs={{4,8},{8,4},{12,16},{16,12},{20,24},{24,20},{5,9},{9,5},{13,17},{1... | collective-permute-start | bytes 3932168 | tf_op jit(solution)/shard_map/ppermute | solution.py:383
  85.1 0.1 collective-permute-start.12
  85.1 0.1 collective-permute-start.8
  85.2 1.3 collective-permute-start.9
  86.5 1.3 collective-permute-start.10
  87.8 26.3 %collective-permute-done.11.from_near = bf16[2,256,1280]{2,1,0:T(8,128)(2,1)S(1)} collective-permute-done((bf16[2,256,1280]{2,1,0:T(8,128)(2,1)S(1)}, bf16[2,256,1280]{2,1,0:T(8,128)(2,1)S(1)}, u32[]{:S(2)}, u32[]{:S(2)}) %collective-permute-start.11) | collective-permute-done | bytes 1310752 | tf_op jit(solution)/shard_map/ppermute | solution.py:383
  114.1 0.0 collective-permute-done.12.from_far
  114.1 1.2 combine.1
  115.4 0.1 collective-permute-start.13
  115.4 1.3 collective-permute-start.14
  116.8 0.0 collective-permute-done.8.refs_1_
  116.8 1.3 collective-permute-start.15
  118.1 0.0 collective-permute-done.9.refs_2_
  118.1 0.0 collective-permute-done.10.refs_3_
  118.1 1.7 %join.2 = (bf16[64,5120]{1,0:T(8,128)(2,1)}, bf16[64,5120]{1,0:T(8,128)(2,1)}) custom-call(s32[2]{0:T(128)S(1)} %copy-done.3, bf16[2,64,1280]{2,1,0:T(8,128)(2,1)S(1)} %get-tuple-element.41.refs_0_, bf16[2,64,1280]{2,1,0:T(8,128)(2,1)S(1)} %collective-permute-done.8.refs_1_, bf16[2,64,1280]{2,1,0:T(8,128)(2,1)S(1)} %collective-permute-done.9.refs_2_, ...), custom_call_target="tpu_custom_call" | custom-call | bytes 2621440 | tf_op jit(solution)/shard_map/join/pallas_call | solution.py:358
  119.8 7.0 %collective-permute-done.13.refs_1_ = bf16[2,64,1280]{2,1,0:T(8,128)(2,1)S(1)} collective-permute-done((bf16[2,64,1280]{2,1,0:T(8,128)(2,1)S(1)}, bf16[2,64,1280]{2,1,0:T(8,128)(2,1)S(1)}, u32[]{:S(2)}, u32[]{:S(2)}) %collective-permute-start.13) | collective-permute-done | bytes 327712 | tf_op jit(solution)/shard_map/ppermute | solution.py:375
  126.8 11.6 %collective-permute-done.14.refs_2_ = bf16[2,64,1280]{2,1,0:T(8,128)(2,1)S(1)} collective-permute-done((bf16[2,64,1280]{2,1,0:T(8,128)(2,1)S(1)}, bf16[2,64,1280]{2,1,0:T(8,128)(2,1)S(1)}, u32[]{:S(2)}, u32[]{:S(2)}) %collective-permute-start.14) | collective-permute-done | bytes 327712 | tf_op jit(solution)/shard_map/ppermute | solution.py:375
  138.4 7.6 %collective-permute-done.15.refs_3_ = bf16[2,64,1280]{2,1,0:T(8,128)(2,1)S(1)} collective-permute-done((bf16[2,64,1280]{2,1,0:T(8,128)(2,1)S(1)}, bf16[2,64,1280]{2,1,0:T(8,128)(2,1)S(1)}, u32[]{:S(2)}, u32[]{:S(2)}) %collective-permute-start.15) | collective-permute-done | bytes 327712 | tf_op jit(solution)/shard_map/ppermute | solution.py:375
  146.0 1.7 %join.3 = (bf16[64,5120]{1,0:T(8,128)(2,1)}, bf16[64,5120]{1,0:T(8,128)(2,1)}) custom-call(s32[2]{0:T(128)S(1)} %copy-done.3, bf16[2,64,1280]{2,1,0:T(8,128)(2,1)S(1)} %get-tuple-element.52.refs_0_, bf16[2,64,1280]{2,1,0:T(8,128)(2,1)S(1)} %collective-permute-done.13.refs_1_, bf16[2,64,1280]{2,1,0:T(8,128)(2,1)S(1)} %collective-permute-done.14.refs_2_, ...), custom_call_target="tpu_custom_call" | custom-call | bytes 2621440 | tf_op jit(solution)/shard_map/join/pallas_call | solution.py:358
  (7 shorter events, 0.0 us)
Async XLA Ops:
  0.6 17.2 %copy-start.4 = (s32[16]{0:T(128)S(1)}, s32[16]{0:T(128)}, u32[]{:S(2)}) copy-start(s32[16]{0:T(128)} %refs_2_.1) | copy-start | bytes 196
  0.6 17.1 %copy-start.1 = (bf16[64,5120]{1,0:T(8,128)(2,1)S(1)}, bf16[64,5120]{1,0:T(8,128)(2,1)}, u32[]{:S(2)}) copy-start(bf16[64,5120]{1,0:T(8,128)(2,1)} %plain.3) | copy-start | bytes 1966084
  0.7 17.1 %copy-start = (bf16[64,5120]{1,0:T(8,128)(2,1)S(1)}, bf16[64,5120]{1,0:T(8,128)(2,1)}, u32[]{:S(2)}) copy-start(bf16[64,5120]{1,0:T(8,128)(2,1)} %turned.3) | copy-start | bytes 1966084
  1.3 16.5 %copy-start.3 = (s32[2]{0:T(128)S(1)}, s32[2]{0:T(128)}, u32[]{:S(2)}) copy-start(s32[2]{0:T(128)} %pad_add_fusion.meta.refs_1_) | copy-start | bytes 28
  4.6 30.9 %copy-start.2 = (bf16[2,64,1280]{2,1,0:T(8,128)(2,1)S(1)}, bf16[2,64,1280]{2,1,0:T(8,128)(2,1)}, u32[]{:S(2)}) copy-start(bf16[2,64,1280]{2,1,0:T(8,128)(2,1)} %get-tuple-element.36.refs_2_) | copy-start | bytes 983044
  4.6 13.2 %collective-permute-start = (bf16[2,64,1280]{2,1,0:T(8,128)(2,1)}, bf16[2,64,1280]{2,1,0:T(8,128)(2,1)S(1)}, u32[]{:S(2)}, u32[]{:S(2)}) collective-permute-start(bf16[2,64,1280]{2,1,0:T(8,128)(2,1)} %get-tuple-element.31), channel_id=1, source_target_pairs={{0,1},{1,0},{2,3},{3,2},{4,5},{5,4},{6,7},{7,6},{8,9},{9,8},{10,11... | collective-permute-start | bytes 983048 | tf_op jit(solution)/shard_map/ppermute | solution.py:375
  4.8 17.6 %collective-permute-start.2 = (bf16[2,64,1280]{2,1,0:T(8,128)(2,1)}, bf16[2,64,1280]{2,1,0:T(8,128)(2,1)S(1)}, u32[]{:S(2)}, u32[]{:S(2)}) collective-permute-start(bf16[2,64,1280]{2,1,0:T(8,128)(2,1)} %get-tuple-element.37), channel_id=1, source_target_pairs={{0,2},{1,3},{2,0},{3,1},{4,6},{5,7},{6,4},{7,5},{8,10},{9,11},{10,... | collective-permute-start | bytes 983048 | tf_op jit(solution)/shard_map/ppermute | solution.py:375
  7.1 28.4 %collective-permute-start.3 = (bf16[2,64,1280]{2,1,0:T(8,128)(2,1)}, bf16[2,64,1280]{2,1,0:T(8,128)(2,1)S(1)}, u32[]{:S(2)}, u32[]{:S(2)}) collective-permute-start(bf16[2,64,1280]{2,1,0:T(8,128)(2,1)} %get-tuple-element.38), channel_id=1, source_target_pairs={{0,3},{1,2},{2,1},{3,0},{4,7},{5,6},{6,5},{7,4},{8,11},{9,10},{10,... | collective-permute-start | bytes 983048 | tf_op jit(solution)/shard_map/ppermute | solution.py:375
  20.2 20.8 %collective-permute-start.1 = (bf16[2,64,1280]{2,1,0:T(8,128)(2,1)S(1)}, bf16[2,64,1280]{2,1,0:T(8,128)(2,1)S(1)}, u32[]{:S(2)}, u32[]{:S(2)}) collective-permute-start(bf16[2,64,1280]{2,1,0:T(8,128)(2,1)S(1)} %get-tuple-element.32), channel_id=1, source_target_pairs={{0,1},{1,0},{2,3},{3,2},{4,5},{5,4},{6,7},{7,6},{8,9},{9,8},{10,11... | collective-permute-start | bytes 983048 | tf_op jit(solution)/shard_map/ppermute | solution.py:375
  36.2 6.5 %copy-start.5 = (s32[16,4]{0,1:T(4,128)S(1)}, s32[16,4]{0,1:T(4,128)}, u32[]{:S(2)}) copy-start(s32[16,4]{0,1:T(4,128)} %param.11) | copy-start | bytes 772
  36.2 35.5 %collective-permute-start.5 = (bf16[2,256,1280]{2,1,0:T(8,128)(2,1)S(1)}, bf16[2,256,1280]{2,1,0:T(8,128)(2,1)}, u32[]{:S(2)}, u32[]{:S(2)}) collective-permute-start(bf16[2,256,1280]{2,1,0:T(8,128)(2,1)S(1)} %order.1.refs_1_.mid), channel_id=1, source_target_pairs={{4,8},{8,4},{12,16},{16,12},{20,24},{24,20},{5,9},{9,5},{13,17},{1... | collective-permute-start | bytes 3932168 | tf_op jit(solution)/shard_map/ppermute | solution.py:383
  41.1 30.6 %collective-permute-start.4 = (bf16[2,256,1280]{2,1,0:T(8,128)(2,1)S(1)}, bf16[2,256,1280]{2,1,0:T(8,128)(2,1)}, u32[]{:S(2)}, u32[]{:S(2)}) collective-permute-start(bf16[2,256,1280]{2,1,0:T(8,128)(2,1)S(1)} %again.1), channel_id=1, source_target_pairs={{0,4},{4,0},{8,12},{12,8},{16,20},{20,16},{24,28},{28,24},{1,5},{5... | collective-permute-start | bytes 3932168 | tf_op jit(solution)/shard_map/ppermute | solution.py:383
  41.2 21.4 %collective-permute-start.6 = (bf16[2,64,1280]{2,1,0:T(8,128)(2,1)}, bf16[2,64,1280]{2,1,0:T(8,128)(2,1)}, u32[]{:S(2)}, u32[]{:S(2)}) collective-permute-start(bf16[2,64,1280]{2,1,0:T(8,128)(2,1)} %get-tuple-element.39), channel_id=1, source_target_pairs={{0,2},{1,3},{2,0},{3,1},{4,6},{5,7},{6,4},{7,5},{8,10},{9,11},{10,... | collective-permute-start | bytes 983048 | tf_op jit(solution)/shard_map/ppermute | solution.py:375
  41.3 30.4 %collective-permute-start.7 = (bf16[2,64,1280]{2,1,0:T(8,128)(2,1)}, bf16[2,64,1280]{2,1,0:T(8,128)(2,1)}, u32[]{:S(2)}, u32[]{:S(2)}) collective-permute-start(bf16[2,64,1280]{2,1,0:T(8,128)(2,1)} %get-tuple-element.40), channel_id=1, source_target_pairs={{0,3},{1,2},{2,1},{3,0},{4,7},{5,6},{6,5},{7,4},{8,11},{9,10},{10,... | collective-permute-start | bytes 983048 | tf_op jit(solution)/shard_map/ppermute | solution.py:375
  81.1 33.0 %collective-permute-start.11 = (bf16[2,256,1280]{2,1,0:T(8,128)(2,1)S(1)}, bf16[2,256,1280]{2,1,0:T(8,128)(2,1)S(1)}, u32[]{:S(2)}, u32[]{:S(2)}) collective-permute-start(bf16[2,256,1280]{2,1,0:T(8,128)(2,1)S(1)} %get-tuple-element.50), channel_id=1, source_target_pairs={{4,8},{8,4},{12,16},{16,12},{20,24},{24,20},{5,9},{9,5},{13,17},{1... | collective-permute-start | bytes 3932168 | tf_op jit(solution)/shard_map/ppermute | solution.py:383
  85.1 29.1 %collective-permute-start.12 = (bf16[2,256,1280]{2,1,0:T(8,128)(2,1)S(1)}, bf16[2,256,1280]{2,1,0:T(8,128)(2,1)S(1)}, u32[]{:S(2)}, u32[]{:S(2)}) collective-permute-start(bf16[2,256,1280]{2,1,0:T(8,128)(2,1)S(1)} %get-tuple-element.51), channel_id=1, source_target_pairs={{0,4},{4,0},{8,12},{12,8},{16,20},{20,16},{24,28},{28,24},{1,5},{5... | collective-permute-start | bytes 3932168 | tf_op jit(solution)/shard_map/ppermute | solution.py:383
  85.1 31.7 %collective-permute-start.8 = (bf16[2,64,1280]{2,1,0:T(8,128)(2,1)S(1)}, bf16[2,64,1280]{2,1,0:T(8,128)(2,1)S(1)}, u32[]{:S(2)}, u32[]{:S(2)}) collective-permute-start(bf16[2,64,1280]{2,1,0:T(8,128)(2,1)S(1)} %get-tuple-element.42), channel_id=1, source_target_pairs={{0,1},{1,0},{2,3},{3,2},{4,5},{5,4},{6,7},{7,6},{8,9},{9,8},{10,11... | collective-permute-start | bytes 983048 | tf_op jit(solution)/shard_map/ppermute | solution.py:375
  85.2 32.9 %collective-permute-start.9 = (bf16[2,64,1280]{2,1,0:T(8,128)(2,1)S(1)}, bf16[2,64,1280]{2,1,0:T(8,128)(2,1)S(1)}, u32[]{:S(2)}, u32[]{:S(2)}) collective-permute-start(bf16[2,64,1280]{2,1,0:T(8,128)(2,1)S(1)} %get-tuple-element.43), channel_id=1, source_target_pairs={{0,2},{1,3},{2,0},{3,1},{4,6},{5,7},{6,4},{7,5},{8,10},{9,11},{10,... | collective-permute-start | bytes 983048 | tf_op jit(solution)/shard_map/ppermute | solution.py:375
  86.5 31.5 %collective-permute-start.10 = (bf16[2,64,1280]{2,1,0:T(8,128)(2,1)S(1)}, bf16[2,64,1280]{2,1,0:T(8,128)(2,1)S(1)}, u32[]{:S(2)}, u32[]{:S(2)}) collective-permute-start(bf16[2,64,1280]{2,1,0:T(8,128)(2,1)S(1)} %get-tuple-element.44), channel_id=1, source_target_pairs={{0,3},{1,2},{2,1},{3,0},{4,7},{5,6},{6,5},{7,4},{8,11},{9,10},{10,... | collective-permute-start | bytes 983048 | tf_op jit(solution)/shard_map/ppermute | solution.py:375
  115.4 11.4 %collective-permute-start.13 = (bf16[2,64,1280]{2,1,0:T(8,128)(2,1)S(1)}, bf16[2,64,1280]{2,1,0:T(8,128)(2,1)S(1)}, u32[]{:S(2)}, u32[]{:S(2)}) collective-permute-start(bf16[2,64,1280]{2,1,0:T(8,128)(2,1)S(1)} %get-tuple-element.53), channel_id=1, source_target_pairs={{0,1},{1,0},{2,3},{3,2},{4,5},{5,4},{6,7},{7,6},{8,9},{9,8},{10,11... | collective-permute-start | bytes 983048 | tf_op jit(solution)/shard_map/ppermute | solution.py:375
  115.4 22.9 %collective-permute-start.14 = (bf16[2,64,1280]{2,1,0:T(8,128)(2,1)S(1)}, bf16[2,64,1280]{2,1,0:T(8,128)(2,1)S(1)}, u32[]{:S(2)}, u32[]{:S(2)}) collective-permute-start(bf16[2,64,1280]{2,1,0:T(8,128)(2,1)S(1)} %get-tuple-element.54), channel_id=1, source_target_pairs={{0,2},{1,3},{2,0},{3,1},{4,6},{5,7},{6,4},{7,5},{8,10},{9,11},{10,... | collective-permute-start | bytes 983048 | tf_op jit(solution)/shard_map/ppermute | solution.py:375
  116.8 29.2 %collective-permute-start.15 = (bf16[2,64,1280]{2,1,0:T(8,128)(2,1)S(1)}, bf16[2,64,1280]{2,1,0:T(8,128)(2,1)S(1)}, u32[]{:S(2)}, u32[]{:S(2)}) collective-permute-start(bf16[2,64,1280]{2,1,0:T(8,128)(2,1)S(1)} %get-tuple-element.55), channel_id=1, source_target_pairs={{0,3},{1,2},{2,1},{3,0},{4,7},{5,6},{6,5},{7,4},{8,11},{9,10},{10,... | collective-permute-start | bytes 983048 | tf_op jit(solution)/shard_map/ppermute | solution.py:375

commit v4 on v3

--- a/solution.py
+++ b/solution.py
@@ -115,7 +115,8 @@
     return lax.dot_general(a, b, (contract, ((), ())), preferred_element_type=jnp.float32)
 
 
-def cut_kernel(n, meta, lengths, turned, plain, *refs):
+def cut_kernel(n, lengths, turned, plain, *refs):
+    meta = lax.axis_index("head"), lax.axis_index("seq")
     pieces, (held, cosine, sine, sems) = refs[-4 - n : -4], refs[-4:]
     rows, width = turned.shape[0], held.shape[2]
     copies = []
@@ -141,12 +142,12 @@
         copies[step][1].wait()
 
 
-def cut(meta, lengths, turned, plain, n, limit, after=()):
+def cut(lengths, turned, plain, n, limit, after=()):
     rows, width = turned.shape[0], turned.shape[1] // n
     return pl.pallas_call(
         functools.partial(cut_kernel, n),
         out_shape=[jax.ShapeDtypeStruct((2, rows, width), jnp.bfloat16)] * n,
-        in_specs=[SMEM_SPEC] * 2 + [HBM_SPEC] * 2 + [ANY_SPEC] * len(after),
+        in_specs=[SMEM_SPEC] + [HBM_SPEC] * 2 + [ANY_SPEC] * len(after),
         out_specs=[VMEM_SPEC] * n,
         scratch_shapes=[
             pltpu.VMEM((n, rows, width), jnp.bfloat16),
@@ -157,7 +158,7 @@
         compiler_params=params(limit),
         cost_estimate=cost(0, 8 * n * rows * width),
         name="cut",
-    )(meta, lengths, turned, plain, *after)
+    )(lengths, turned, plain, *after)
 
 
 def tables_kernel(meta, lengths, cosine, sine, half_cosine, half_sine):
@@ -257,7 +258,7 @@
             weights = chance.astype(jnp.bfloat16)
             sums[1, :, lanes] = dot(weights, grad_s[:, lanes], ((1,), (0,))).astype(sums.dtype)
             out += dot(part[1, :, lanes], weights, ((0,), (0,)))
-        out_s[:, lanes] = out.T.astype(jnp.bfloat16)
+        out_s[:, lanes] = out.astype(jnp.bfloat16).T
 
     def stage_back(h, chances, grad_chances):
         lanes = lanes_of(h)
@@ -275,16 +276,17 @@
             ],
             axis=0,
         )
-        back_s[:, lanes] = back.T.astype(jnp.bfloat16)
-
-    scores = stage_scores(0)
+        back_s[:, lanes] = back.astype(jnp.bfloat16).T
+
+    scores, grad_chances = stage_scores(0), stage_grad(0)
     for h in range(heads):
-        grad_chances = stage_grad(h)
         chances = stage_soft(scores)
         if h + 1 < heads:
             scores = stage_scores(h + 1)
+        stage_back(h, chances, grad_chances)
+        if h + 1 < heads:
+            grad_chances = stage_grad(h + 1)
         stage_out(h, chances)
-        stage_back(h, chances, grad_chances)
     for result, index in results:
         place = start_of(index, result.shape[1])
         result[0] = out_s[place, :]
@@ -387,8 +389,8 @@
     n = lax.axis_size("head")
     length = queries.shape[0] * n
     meta = jnp.stack([lax.axis_index("head"), lax.axis_index("seq")]).astype(jnp.int32)
-    key_value = swap(cut(meta, chain_lengths, keys, values, n, WIDE_LIMIT))
-    later = cut(meta, chain_lengths, queries, out_grad, n, VMEM_LIMIT, [key_value[1]])
+    key_value = swap(cut(chain_lengths, keys, values, n, WIDE_LIMIT))
+    later = cut(chain_lengths, queries, out_grad, n, VMEM_LIMIT, [key_value[1]])
     inputs = swap(later)
     mid = order(meta, key_value, [later[0]])
     far, near = trade(mid, 1), trade(again(mid, [inputs[1]]), 0)

time: 148 us -> 147 us (level)
  no operation moved by 1% of the time
where the time goes in v4:
time: 147 us
  waiting for transfers between devices  103 us (70%)
  Pallas kernels  22.1 us (15%)
  starting transfers between devices  20.7 us (14%)
    ppermute x12, waiting for transfers between devices, swap(): lax.ppermute(pieces[k], 'head', [(i, i ^ k) for i in range(n)])  76.8 us
    ppermute x4, waiting for transfers between devices, trade(): return lax.ppermute(block, 'seq', route)  26.3 us
    ppermute x12, starting transfers between devices, swap(): lax.ppermute(pieces[k], 'head', [(i, i ^ k) for i in range(n)])  11.7 us
    pallas_call x1, Pallas kernels, attend(): pl.pallas_call(functools.partial(attend_kernel, n, heads), out_shape=[jax...  9.19 us
    ppermute x4, starting transfers between devices, trade(): return lax.ppermute(block, 'seq', route)  8.93 us
    pallas_call x2, Pallas kernels, cut(): pl.pallas_call(functools.partial(cut_kernel, n), out_shape=[jax.ShapeDtyp...  5.82 us
    pallas_call x2, Pallas kernels, join(): pl.pallas_call(functools.partial(join_kernel, n), out_shape=[jax.ShapeDty...  3.32 us
  transfers between devices with their start and end apart: 16, of which 8 were waited for; matrix products, arithmetic and copies ran while one was open for 0% of the time, Pallas kernels for 5%

profile of v4, /device:TPU:11, one launch (start us, length us, event | category | flops | bytes accessed | tf_op | source)
XLA Modules:
  0.0 146.8 jit_solution(12366512436427729587)
XLA Ops:
  0.6 0.0 copy-start.3
  0.6 0.0 copy-start.1
  0.7 3.3 %cut.2 = (bf16[2,64,1280]{2,1,0:T(8,128)(2,1)}, bf16[2,64,1280]{2,1,0:T(8,128)(2,1)}, bf16[2,64,1280]{2,1,0:T(8,128)(2,1)}, bf16[2,64,1280]{2,1,0:T(8,128)(2,1)}) custom-call(s32[16]{0:T(128)} %refs_2_.1, bf16[64,5120]{1,0:T(8,128)(2,1)} %turned.2, bf16[64,5120]{1,0:T(8,128)(2,1)} %plain.2), custom_call_target="tpu_custom_call" | custom-call | bytes 2621440 | tf_op jit(solution)/shard_map/cut/pallas_call | solution.py:147
  4.0 0.0 copy-start.2
  4.0 0.2 collective-permute-start
  4.2 2.3 %collective-permute-start.2 = (bf16[2,64,1280]{2,1,0:T(8,128)(2,1)}, bf16[2,64,1280]{2,1,0:T(8,128)(2,1)S(1)}, u32[]{:S(2)}, u32[]{:S(2)}) collective-permute-start(bf16[2,64,1280]{2,1,0:T(8,128)(2,1)} %get-tuple-element.37), channel_id=1, source_target_pairs={{0,2},{1,3},{2,0},{3,1},{4,6},{5,7},{6,4},{7,5},{8,10},{9,11},{10,... | collective-permute-start | bytes 983048 | tf_op jit(solution)/shard_map/ppermute | solution.py:377
  6.5 0.2 collective-permute-start.3
  6.7 10.5 %collective-permute-done.refs_0_.refs_3_ = bf16[2,64,1280]{2,1,0:T(8,128)(2,1)S(1)} collective-permute-done((bf16[2,64,1280]{2,1,0:T(8,128)(2,1)}, bf16[2,64,1280]{2,1,0:T(8,128)(2,1)S(1)}, u32[]{:S(2)}, u32[]{:S(2)}) %collective-permute-start) | collective-permute-done | bytes 327712 | tf_op jit(solution)/shard_map/ppermute | solution.py:377
  17.2 0.0 copy-done.1
  17.2 2.5 %cut.3 = (bf16[2,64,1280]{2,1,0:T(8,128)(2,1)S(1)}, bf16[2,64,1280]{2,1,0:T(8,128)(2,1)}, bf16[2,64,1280]{2,1,0:T(8,128)(2,1)}, bf16[2,64,1280]{2,1,0:T(8,128)(2,1)}) custom-call(s32[16]{0:T(128)S(1)} %copy-done.3, bf16[64,5120]{1,0:T(8,128)(2,1)S(1)} %copy-done, bf16[64,5120]{1,0:T(8,128)(2,1)S(1)} %copy-done.1, ...), custom_call_target="tpu_custom_call" | custom-call | bytes 2621440 | tf_op jit(solution)/shard_map/cut/pallas_call | solution.py:147
  19.7 2.2 %collective-permute-start.1 = (bf16[2,64,1280]{2,1,0:T(8,128)(2,1)}, bf16[2,64,1280]{2,1,0:T(8,128)(2,1)S(1)}, u32[]{:S(2)}, u32[]{:S(2)}) collective-permute-start(bf16[2,64,1280]{2,1,0:T(8,128)(2,1)} %get-tuple-element.32), channel_id=1, source_target_pairs={{0,1},{1,0},{2,3},{3,2},{4,5},{5,4},{6,7},{7,6},{8,9},{9,8},{10,11... | collective-permute-start | bytes 983048 | tf_op jit(solution)/shard_map/ppermute | solution.py:377
  21.9 0.1 pad_add_fusion.refs_1_.meta
  21.9 0.0 collective-permute-done.2.refs_4_
  21.9 13.0 %collective-permute-done.3.refs_5_ = bf16[2,64,1280]{2,1,0:T(8,128)(2,1)S(1)} collective-permute-done((bf16[2,64,1280]{2,1,0:T(8,128)(2,1)}, bf16[2,64,1280]{2,1,0:T(8,128)(2,1)S(1)}, u32[]{:S(2)}, u32[]{:S(2)}) %collective-permute-start.3) | collective-permute-done | bytes 327712 | tf_op jit(solution)/shard_map/ppermute | solution.py:377
  34.9 0.6 order.1.refs_1_.mid
  35.5 0.0 copy-start.4
  35.6 4.8 %collective-permute-start.5 = (bf16[2,256,1280]{2,1,0:T(8,128)(2,1)S(1)}, bf16[2,256,1280]{2,1,0:T(8,128)(2,1)}, u32[]{:S(2)}, u32[]{:S(2)}) collective-permute-start(bf16[2,256,1280]{2,1,0:T(8,128)(2,1)S(1)} %order.1.refs_1_.mid), channel_id=1, source_target_pairs={{4,8},{8,4},{12,16},{16,12},{20,24},{24,20},{5,9},{9,5},{13,17},{1... | collective-permute-start | bytes 3932168 | tf_op jit(solution)/shard_map/ppermute | solution.py:385
  40.4 0.0 collective-permute-done.1.refs_0_.refs_1_
  40.4 0.1 again.1
  40.5 0.1 collective-permute-start.4
  40.6 0.1 collective-permute-start.6
  40.7 1.4 collective-permute-start.7
  42.0 0.1 copy.10.listed
  42.1 1.8 %tables.1 = (f32[256,128]{1,0:T(8,128)S(1)}, f32[256,128]{1,0:T(8,128)S(1)}, f32[64,256]{1,0:T(8,128)S(1)}, f32[64,256]{1,0:T(8,128)S(1)}) custom-call(bf16[2,64,1280]{2,1,0:T(8,128)(2,1)S(1)} %collective-permute-done.1.refs_0_.refs_1_, s32[2]{0:T(128)S(1)} %pad_add_fusion.refs_1_.meta, s32[16]{0:T(128)S(1)} %copy-done.3), custom_call_target="tpu_custom_call" | custom-call | bytes 262144 | tf_op jit(solution)/shard_map/tables/pallas_call | solution.py:173
  44.0 18.0 %collective-permute-done.6.refs_2_ = bf16[2,64,1280]{2,1,0:T(8,128)(2,1)} collective-permute-done((bf16[2,64,1280]{2,1,0:T(8,128)(2,1)}, bf16[2,64,1280]{2,1,0:T(8,128)(2,1)}, u32[]{:S(2)}, u32[]{:S(2)}) %collective-permute-start.6) | collective-permute-done | bytes 327712 | tf_op jit(solution)/shard_map/ppermute | solution.py:377
  62.0 9.1 %collective-permute-done.7.refs_3_ = bf16[2,64,1280]{2,1,0:T(8,128)(2,1)} collective-permute-done((bf16[2,64,1280]{2,1,0:T(8,128)(2,1)}, bf16[2,64,1280]{2,1,0:T(8,128)(2,1)}, u32[]{:S(2)}, u32[]{:S(2)}) %collective-permute-start.7) | collective-permute-done | bytes 327712 | tf_op jit(solution)/shard_map/ppermute | solution.py:377
  71.0 0.0 collective-permute-done.5.far
  71.0 0.0 collective-permute-done.4.near
  71.1 9.2 %attend.1 = (bf16[2,64,1280]{2,1,0:T(8,128)(2,1)S(1)}, bf16[2,64,1280]{2,1,0:T(8,128)(2,1)S(1)}, bf16[2,64,1280]{2,1,0:T(8,128)(2,1)S(1)}, bf16[2,64,1280]{2,1,0...) custom-call(s32[2]{0:T(128)S(1)} %pad_add_fusion.refs_1_.meta, ...), custom_call_target="tpu_custom_call" | custom-call | flops 3019898880 | bytes 13107200 | tf_op jit(solution)/shard_map/attend/pallas_call | solution.py:300
  80.2 4.0 %collective-permute-start.11 = (bf16[2,256,1280]{2,1,0:T(8,128)(2,1)S(1)}, bf16[2,256,1280]{2,1,0:T(8,128)(2,1)S(1)}, u32[]{:S(2)}, u32[]{:S(2)}) collective-permute-start(bf16[2,256,1280]{2,1,0:T(8,128)(2,1)S(1)} %get-tuple-element.50), channel_id=1, source_target_pairs={{4,8},{8,4},{12,16},{16,12},{20,24},{24,20},{5,9},{9,5},{13,17},{1... | collective-permute-start | bytes 3932168 | tf_op jit(solution)/shard_map/ppermute | solution.py:385
  84.2 0.1 collective-permute-start.12
  84.3 0.1 collective-permute-start.8
  84.4 1.3 collective-permute-start.9
  85.7 1.3 collective-permute-start.10
  87.0 26.3 %collective-permute-done.11.from_near = bf16[2,256,1280]{2,1,0:T(8,128)(2,1)S(1)} collective-permute-done((bf16[2,256,1280]{2,1,0:T(8,128)(2,1)S(1)}, bf16[2,256,1280]{2,1,0:T(8,128)(2,1)S(1)}, u32[]{:S(2)}, u32[]{:S(2)}) %collective-permute-start.11) | collective-permute-done | bytes 1310752 | tf_op jit(solution)/shard_map/ppermute | solution.py:385
  113.3 0.0 collective-permute-done.12.from_far
  113.3 1.2 combine.1
  114.5 0.1 collective-permute-start.13
  114.6 1.3 collective-permute-start.14
  115.9 0.0 collective-permute-done.8.refs_1_
  115.9 1.3 collective-permute-start.15
  117.2 0.0 collective-permute-done.9.refs_2_
  117.2 0.0 collective-permute-done.10.refs_3_
  117.2 1.7 %join.2 = (bf16[64,5120]{1,0:T(8,128)(2,1)}, bf16[64,5120]{1,0:T(8,128)(2,1)}) custom-call(s32[2]{0:T(128)S(1)} %pad_add_fusion.refs_1_.meta, bf16[2,64,1280]{2,1,0:T(8,128)(2,1)S(1)} %get-tuple-element.41.refs_0_, bf16[2,64,1280]{2,1,0:T(8,128)(2,1)S(1)} %collective-permute-done.8.refs_1_, bf16[2,64,1280]{2,1,0:T(8,128)(2,1)S(1)} %collective-permute-done.9.refs_2_, ...), custom_call_target="tpu_custom_call" | custom-call | bytes 2621440 | tf_op jit(solution)/shard_map/join/pallas_call | solution.py:360
  118.9 7.0 %collective-permute-done.13.refs_1_ = bf16[2,64,1280]{2,1,0:T(8,128)(2,1)S(1)} collective-permute-done((bf16[2,64,1280]{2,1,0:T(8,128)(2,1)S(1)}, bf16[2,64,1280]{2,1,0:T(8,128)(2,1)S(1)}, u32[]{:S(2)}, u32[]{:S(2)}) %collective-permute-start.13) | collective-permute-done | bytes 327712 | tf_op jit(solution)/shard_map/ppermute | solution.py:377
  125.9 11.6 %collective-permute-done.14.refs_2_ = bf16[2,64,1280]{2,1,0:T(8,128)(2,1)S(1)} collective-permute-done((bf16[2,64,1280]{2,1,0:T(8,128)(2,1)S(1)}, bf16[2,64,1280]{2,1,0:T(8,128)(2,1)S(1)}, u32[]{:S(2)}, u32[]{:S(2)}) %collective-permute-start.14) | collective-permute-done | bytes 327712 | tf_op jit(solution)/shard_map/ppermute | solution.py:377
  137.5 7.6 %collective-permute-done.15.refs_3_ = bf16[2,64,1280]{2,1,0:T(8,128)(2,1)S(1)} collective-permute-done((bf16[2,64,1280]{2,1,0:T(8,128)(2,1)S(1)}, bf16[2,64,1280]{2,1,0:T(8,128)(2,1)S(1)}, u32[]{:S(2)}, u32[]{:S(2)}) %collective-permute-start.15) | collective-permute-done | bytes 327712 | tf_op jit(solution)/shard_map/ppermute | solution.py:377
  145.2 1.7 %join.3 = (bf16[64,5120]{1,0:T(8,128)(2,1)}, bf16[64,5120]{1,0:T(8,128)(2,1)}) custom-call(s32[2]{0:T(128)S(1)} %pad_add_fusion.refs_1_.meta, bf16[2,64,1280]{2,1,0:T(8,128)(2,1)S(1)} %get-tuple-element.52.refs_0_, bf16[2,64,1280]{2,1,0:T(8,128)(2,1)S(1)} %collective-permute-done.13.refs_1_, bf16[2,64,1280]{2,1,0:T(8,128)(2,1)S(1)} %collective-permute-done.14.refs_2_, ...), custom_call_target="tpu_custom_call" | custom-call | bytes 2621440 | tf_op jit(solution)/shard_map/join/pallas_call | solution.py:360
  (5 shorter events, 0.0 us)
Async XLA Ops:
  0.6 16.5 %copy-start.3 = (s32[16]{0:T(128)S(1)}, s32[16]{0:T(128)}, u32[]{:S(2)}) copy-start(s32[16]{0:T(128)} %refs_2_.1) | copy-start | bytes 196
  0.6 16.5 %copy-start.1 = (bf16[64,5120]{1,0:T(8,128)(2,1)S(1)}, bf16[64,5120]{1,0:T(8,128)(2,1)}, u32[]{:S(2)}) copy-start(bf16[64,5120]{1,0:T(8,128)(2,1)} %plain.3) | copy-start | bytes 1966084
  0.7 16.5 %copy-start = (bf16[64,5120]{1,0:T(8,128)(2,1)S(1)}, bf16[64,5120]{1,0:T(8,128)(2,1)}, u32[]{:S(2)}) copy-start(bf16[64,5120]{1,0:T(8,128)(2,1)} %turned.3) | copy-start | bytes 1966084
  4.0 30.9 %copy-start.2 = (bf16[2,64,1280]{2,1,0:T(8,128)(2,1)S(1)}, bf16[2,64,1280]{2,1,0:T(8,128)(2,1)}, u32[]{:S(2)}) copy-start(bf16[2,64,1280]{2,1,0:T(8,128)(2,1)} %get-tuple-element.36.refs_2_) | copy-start | bytes 983044
  4.0 13.2 %collective-permute-start = (bf16[2,64,1280]{2,1,0:T(8,128)(2,1)}, bf16[2,64,1280]{2,1,0:T(8,128)(2,1)S(1)}, u32[]{:S(2)}, u32[]{:S(2)}) collective-permute-start(bf16[2,64,1280]{2,1,0:T(8,128)(2,1)} %get-tuple-element.31), channel_id=1, source_target_pairs={{0,1},{1,0},{2,3},{3,2},{4,5},{5,4},{6,7},{7,6},{8,9},{9,8},{10,11... | collective-permute-start | bytes 983048 | tf_op jit(solution)/shard_map/ppermute | solution.py:377
  4.2 17.7 %collective-permute-start.2 = (bf16[2,64,1280]{2,1,0:T(8,128)(2,1)}, bf16[2,64,1280]{2,1,0:T(8,128)(2,1)S(1)}, u32[]{:S(2)}, u32[]{:S(2)}) collective-permute-start(bf16[2,64,1280]{2,1,0:T(8,128)(2,1)} %get-tuple-element.37), channel_id=1, source_target_pairs={{0,2},{1,3},{2,0},{3,1},{4,6},{5,7},{6,4},{7,5},{8,10},{9,11},{10,... | collective-permute-start | bytes 983048 | tf_op jit(solution)/shard_map/ppermute | solution.py:377
  6.5 28.4 %collective-permute-start.3 = (bf16[2,64,1280]{2,1,0:T(8,128)(2,1)}, bf16[2,64,1280]{2,1,0:T(8,128)(2,1)S(1)}, u32[]{:S(2)}, u32[]{:S(2)}) collective-permute-start(bf16[2,64,1280]{2,1,0:T(8,128)(2,1)} %get-tuple-element.38), channel_id=1, source_target_pairs={{0,3},{1,2},{2,1},{3,0},{4,7},{5,6},{6,5},{7,4},{8,11},{9,10},{10,... | collective-permute-start | bytes 983048 | tf_op jit(solution)/shard_map/ppermute | solution.py:377
  19.7 20.7 %collective-permute-start.1 = (bf16[2,64,1280]{2,1,0:T(8,128)(2,1)}, bf16[2,64,1280]{2,1,0:T(8,128)(2,1)S(1)}, u32[]{:S(2)}, u32[]{:S(2)}) collective-permute-start(bf16[2,64,1280]{2,1,0:T(8,128)(2,1)} %get-tuple-element.32), channel_id=1, source_target_pairs={{0,1},{1,0},{2,3},{3,2},{4,5},{5,4},{6,7},{7,6},{8,9},{9,8},{10,11... | collective-permute-start | bytes 983048 | tf_op jit(solution)/shard_map/ppermute | solution.py:377
  35.5 6.5 %copy-start.4 = (s32[16,4]{0,1:T(4,128)S(1)}, s32[16,4]{0,1:T(4,128)}, u32[]{:S(2)}) copy-start(s32[16,4]{0,1:T(4,128)} %param.11) | copy-start | bytes 772
  35.6 35.5 %collective-permute-start.5 = (bf16[2,256,1280]{2,1,0:T(8,128)(2,1)S(1)}, bf16[2,256,1280]{2,1,0:T(8,128)(2,1)}, u32[]{:S(2)}, u32[]{:S(2)}) collective-permute-start(bf16[2,256,1280]{2,1,0:T(8,128)(2,1)S(1)} %order.1.refs_1_.mid), channel_id=1, source_target_pairs={{4,8},{8,4},{12,16},{16,12},{20,24},{24,20},{5,9},{9,5},{13,17},{1... | collective-permute-start | bytes 3932168 | tf_op jit(solution)/shard_map/ppermute | solution.py:385
  40.5 30.5 %collective-permute-start.4 = (bf16[2,256,1280]{2,1,0:T(8,128)(2,1)S(1)}, bf16[2,256,1280]{2,1,0:T(8,128)(2,1)}, u32[]{:S(2)}, u32[]{:S(2)}) collective-permute-start(bf16[2,256,1280]{2,1,0:T(8,128)(2,1)S(1)} %again.1), channel_id=1, source_target_pairs={{0,4},{4,0},{8,12},{12,8},{16,20},{20,16},{24,28},{28,24},{1,5},{5... | collective-permute-start | bytes 3932168 | tf_op jit(solution)/shard_map/ppermute | solution.py:385
  40.6 21.4 %collective-permute-start.6 = (bf16[2,64,1280]{2,1,0:T(8,128)(2,1)}, bf16[2,64,1280]{2,1,0:T(8,128)(2,1)}, u32[]{:S(2)}, u32[]{:S(2)}) collective-permute-start(bf16[2,64,1280]{2,1,0:T(8,128)(2,1)} %get-tuple-element.39), channel_id=1, source_target_pairs={{0,2},{1,3},{2,0},{3,1},{4,6},{5,7},{6,4},{7,5},{8,10},{9,11},{10,... | collective-permute-start | bytes 983048 | tf_op jit(solution)/shard_map/ppermute | solution.py:377
  40.7 30.4 %collective-permute-start.7 = (bf16[2,64,1280]{2,1,0:T(8,128)(2,1)}, bf16[2,64,1280]{2,1,0:T(8,128)(2,1)}, u32[]{:S(2)}, u32[]{:S(2)}) collective-permute-start(bf16[2,64,1280]{2,1,0:T(8,128)(2,1)} %get-tuple-element.40), channel_id=1, source_target_pairs={{0,3},{1,2},{2,1},{3,0},{4,7},{5,6},{6,5},{7,4},{8,11},{9,10},{10,... | collective-permute-start | bytes 983048 | tf_op jit(solution)/shard_map/ppermute | solution.py:377
  80.2 33.0 %collective-permute-start.11 = (bf16[2,256,1280]{2,1,0:T(8,128)(2,1)S(1)}, bf16[2,256,1280]{2,1,0:T(8,128)(2,1)S(1)}, u32[]{:S(2)}, u32[]{:S(2)}) collective-permute-start(bf16[2,256,1280]{2,1,0:T(8,128)(2,1)S(1)} %get-tuple-element.50), channel_id=1, source_target_pairs={{4,8},{8,4},{12,16},{16,12},{20,24},{24,20},{5,9},{9,5},{13,17},{1... | collective-permute-start | bytes 3932168 | tf_op jit(solution)/shard_map/ppermute | solution.py:385
  84.2 29.1 %collective-permute-start.12 = (bf16[2,256,1280]{2,1,0:T(8,128)(2,1)S(1)}, bf16[2,256,1280]{2,1,0:T(8,128)(2,1)S(1)}, u32[]{:S(2)}, u32[]{:S(2)}) collective-permute-start(bf16[2,256,1280]{2,1,0:T(8,128)(2,1)S(1)} %get-tuple-element.51), channel_id=1, source_target_pairs={{0,4},{4,0},{8,12},{12,8},{16,20},{20,16},{24,28},{28,24},{1,5},{5... | collective-permute-start | bytes 3932168 | tf_op jit(solution)/shard_map/ppermute | solution.py:385
  84.3 31.7 %collective-permute-start.8 = (bf16[2,64,1280]{2,1,0:T(8,128)(2,1)S(1)}, bf16[2,64,1280]{2,1,0:T(8,128)(2,1)S(1)}, u32[]{:S(2)}, u32[]{:S(2)}) collective-permute-start(bf16[2,64,1280]{2,1,0:T(8,128)(2,1)S(1)} %get-tuple-element.42), channel_id=1, source_target_pairs={{0,1},{1,0},{2,3},{3,2},{4,5},{5,4},{6,7},{7,6},{8,9},{9,8},{10,11... | collective-permute-start | bytes 983048 | tf_op jit(solution)/shard_map/ppermute | solution.py:377
  84.4 32.9 %collective-permute-start.9 = (bf16[2,64,1280]{2,1,0:T(8,128)(2,1)S(1)}, bf16[2,64,1280]{2,1,0:T(8,128)(2,1)S(1)}, u32[]{:S(2)}, u32[]{:S(2)}) collective-permute-start(bf16[2,64,1280]{2,1,0:T(8,128)(2,1)S(1)} %get-tuple-element.43), channel_id=1, source_target_pairs={{0,2},{1,3},{2,0},{3,1},{4,6},{5,7},{6,4},{7,5},{8,10},{9,11},{10,... | collective-permute-start | bytes 983048 | tf_op jit(solution)/shard_map/ppermute | solution.py:377
  85.7 31.5 %collective-permute-start.10 = (bf16[2,64,1280]{2,1,0:T(8,128)(2,1)S(1)}, bf16[2,64,1280]{2,1,0:T(8,128)(2,1)S(1)}, u32[]{:S(2)}, u32[]{:S(2)}) collective-permute-start(bf16[2,64,1280]{2,1,0:T(8,128)(2,1)S(1)} %get-tuple-element.44), channel_id=1, source_target_pairs={{0,3},{1,2},{2,1},{3,0},{4,7},{5,6},{6,5},{7,4},{8,11},{9,10},{10,... | collective-permute-start | bytes 983048 | tf_op jit(solution)/shard_map/ppermute | solution.py:377
  114.5 11.4 %collective-permute-start.13 = (bf16[2,64,1280]{2,1,0:T(8,128)(2,1)S(1)}, bf16[2,64,1280]{2,1,0:T(8,128)(2,1)S(1)}, u32[]{:S(2)}, u32[]{:S(2)}) collective-permute-start(bf16[2,64,1280]{2,1,0:T(8,128)(2,1)S(1)} %get-tuple-element.53), channel_id=1, source_target_pairs={{0,1},{1,0},{2,3},{3,2},{4,5},{5,4},{6,7},{7,6},{8,9},{9,8},{10,11... | collective-permute-start | bytes 983048 | tf_op jit(solution)/shard_map/ppermute | solution.py:377
  114.6 22.9 %collective-permute-start.14 = (bf16[2,64,1280]{2,1,0:T(8,128)(2,1)S(1)}, bf16[2,64,1280]{2,1,0:T(8,128)(2,1)S(1)}, u32[]{:S(2)}, u32[]{:S(2)}) collective-permute-start(bf16[2,64,1280]{2,1,0:T(8,128)(2,1)S(1)} %get-tuple-element.54), channel_id=1, source_target_pairs={{0,2},{1,3},{2,0},{3,1},{4,6},{5,7},{6,4},{7,5},{8,10},{9,11},{10,... | collective-permute-start | bytes 983048 | tf_op jit(solution)/shard_map/ppermute | solution.py:377
  115.9 29.2 %collective-permute-start.15 = (bf16[2,64,1280]{2,1,0:T(8,128)(2,1)S(1)}, bf16[2,64,1280]{2,1,0:T(8,128)(2,1)S(1)}, u32[]{:S(2)}, u32[]{:S(2)}) collective-permute-start(bf16[2,64,1280]{2,1,0:T(8,128)(2,1)S(1)} %get-tuple-element.55), channel_id=1, source_target_pairs={{0,3},{1,2},{2,1},{3,0},{4,7},{5,6},{6,5},{7,4},{8,11},{9,10},{10,... | collective-permute-start | bytes 983048 | tf_op jit(solution)/shard_map/ppermute | solution.py:377

commit v5 on v4

--- a/solution.py
+++ b/solution.py
@@ -341,32 +341,34 @@
     )(meta, cosine, sine, own, from_far, from_near)
 
 
-def join_kernel(n, meta, *refs):
-    pieces, outs, sems = refs[:n], refs[n:-1], refs[-1]
+def join_kernel(steps, meta, *refs):
+    pieces, outs, sems = refs[: len(steps)], refs[-3:-1], refs[-1]
     copies = []
-    for step, piece in enumerate(pieces):
+    for i, (step, piece) in enumerate(zip(steps, pieces)):
         lanes = start_of(jnp.bitwise_xor(meta[0], step), piece.shape[2])
         for t, out in enumerate(outs):
-            copies.append(pltpu.make_async_copy(piece.at[t], out.at[:, lanes], sems.at[step, t]))
+            copies.append(pltpu.make_async_copy(piece.at[t], out.at[:, lanes], sems.at[i, t]))
     for copy in copies:
         copy.start()
     for copy in copies:
         copy.wait()
 
 
-def join(meta, pieces):
+def join(meta, pieces, steps, outs=()):
     n = len(pieces)
     count, rows, width = pieces[0].shape
-    return pl.pallas_call(
-        functools.partial(join_kernel, n),
+    chosen = [pieces[step] for step in steps]
+    return pl.pallas_call(
+        functools.partial(join_kernel, steps),
         out_shape=[jax.ShapeDtypeStruct((rows, n * width), jnp.bfloat16)] * count,
-        in_specs=[SMEM_SPEC] + [ANY_SPEC] * n,
+        in_specs=[SMEM_SPEC] + [ANY_SPEC] * len(steps) + [HBM_SPEC] * len(outs),
         out_specs=[HBM_SPEC] * count,
-        scratch_shapes=[pltpu.SemaphoreType.DMA((n, count))],
-        compiler_params=params(),
-        cost_estimate=cost(0, 4 * n * count * rows * width),
+        scratch_shapes=[pltpu.SemaphoreType.DMA((len(steps), count))],
+        input_output_aliases={1 + len(steps) + t: t for t in range(len(outs))},
+        compiler_params=params(),
+        cost_estimate=cost(0, 4 * len(steps) * count * rows * width),
         name="join",
-    )(meta, *pieces)
+    )(meta, *chosen, *outs)
 
 
 def swap(pieces):
@@ -399,10 +401,11 @@
         meta, block_pairs, half_cosine, half_sine, mid, near, far, inputs, HEADS_A_STEP
     )
     back_out = swap(results)
-    attn_out, query_grad = join(meta, back_out)
+    attn_out, query_grad = join(meta, back_out, tuple(range(n)))
     from_far, from_near = trade(far_sum, 1), trade(near_sum, 0)
     back = swap(combine(meta, cosine, sine, own, from_near, from_far, n))
-    key_grad, value_grad = join(meta, back)
+    key_grad, value_grad = join(meta, back, (0, 1))
+    key_grad, value_grad = join(meta, back, tuple(range(2, n)), (key_grad, value_grad))
     return attn_out, query_grad, key_grad, value_grad
 
 

time: 147 us -> 147 us (level)
    pallas_call x2 -> x3, Pallas kernels: 3.32 us -> 4.47 us  [join(): pl.pallas_call(functools.partial(join_kernel, steps), out_shape=[jax.Shap...]
  transfers between devices with their start and end apart: 16 -> 16, of which waited for: 8 -> 8; matrix products, arithmetic and copies ran while one was open for 0% -> 0% of each run, Pallas kernels for 5% -> 6%
where the time goes in v5:
time: 147 us
  waiting for transfers between devices  102 us (69%)
  Pallas kernels  23.3 us (16%)
  starting transfers between devices  20.7 us (14%)
    ppermute x12, waiting for transfers between devices, swap(): lax.ppermute(pieces[k], 'head', [(i, i ^ k) for i in range(n)])  75.4 us
    ppermute x4, waiting for transfers between devices, trade(): return lax.ppermute(block, 'seq', route)  26.3 us
    ppermute x12, starting transfers between devices, swap(): lax.ppermute(pieces[k], 'head', [(i, i ^ k) for i in range(n)])  11.7 us
    pallas_call x1, Pallas kernels, attend(): pl.pallas_call(functools.partial(attend_kernel, n, heads), out_shape=[jax...  9.19 us
    ppermute x4, starting transfers between devices, trade(): return lax.ppermute(block, 'seq', route)  8.93 us
    pallas_call x2, Pallas kernels, cut(): pl.pallas_call(functools.partial(cut_kernel, n), out_shape=[jax.ShapeDtyp...  5.82 us
    pallas_call x3, Pallas kernels, join(): pl.pallas_call(functools.partial(join_kernel, steps), out_shape=[jax.Shap...  4.47 us
  transfers between devices with their start and end apart: 16, of which 8 were waited for; matrix products, arithmetic and copies ran while one was open for 0% of the time, Pallas kernels for 6%

profile of v5, /device:TPU:11, one launch (start us, length us, event | category | flops | bytes accessed | tf_op | source)
XLA Modules:
  0.0 146.6 jit_solution(12181392901730489109)
XLA Ops:
  0.6 0.0 copy-start.3
  0.7 3.3 %cut.2 = (bf16[2,64,1280]{2,1,0:T(8,128)(2,1)}, bf16[2,64,1280]{2,1,0:T(8,128)(2,1)}, bf16[2,64,1280]{2,1,0:T(8,128)(2,1)}, bf16[2,64,1280]{2,1,0:T(8,128)(2,1)}) custom-call(s32[16]{0:T(128)} %refs_2_.1, bf16[64,5120]{1,0:T(8,128)(2,1)} %turned.2, bf16[64,5120]{1,0:T(8,128)(2,1)} %plain.2), custom_call_target="tpu_custom_call" | custom-call | bytes 2621440 | tf_op jit(solution)/shard_map/cut/pallas_call | solution.py:147
  4.0 0.0 copy-start.2
  4.0 0.2 collective-permute-start
  4.2 2.3 %collective-permute-start.2 = (bf16[2,64,1280]{2,1,0:T(8,128)(2,1)}, bf16[2,64,1280]{2,1,0:T(8,128)(2,1)S(1)}, u32[]{:S(2)}, u32[]{:S(2)}) collective-permute-start(bf16[2,64,1280]{2,1,0:T(8,128)(2,1)} %get-tuple-element.39), channel_id=1, source_target_pairs={{0,2},{1,3},{2,0},{3,1},{4,6},{5,7},{6,4},{7,5},{8,10},{9,11},{10,... | collective-permute-start | bytes 983048 | tf_op jit(solution)/shard_map/ppermute | solution.py:379
  6.5 0.2 collective-permute-start.3
  6.7 10.5 %collective-permute-done.refs_0_.refs_3_ = bf16[2,64,1280]{2,1,0:T(8,128)(2,1)S(1)} collective-permute-done((bf16[2,64,1280]{2,1,0:T(8,128)(2,1)}, bf16[2,64,1280]{2,1,0:T(8,128)(2,1)S(1)}, u32[]{:S(2)}, u32[]{:S(2)}) %collective-permute-start) | collective-permute-done | bytes 327712 | tf_op jit(solution)/shard_map/ppermute | solution.py:379
  17.2 0.0 copy-done.1
  17.2 2.5 %cut.3 = (bf16[2,64,1280]{2,1,0:T(8,128)(2,1)S(1)}, bf16[2,64,1280]{2,1,0:T(8,128)(2,1)}, bf16[2,64,1280]{2,1,0:T(8,128)(2,1)}, bf16[2,64,1280]{2,1,0:T(8,128)(2,1)}) custom-call(s32[16]{0:T(128)S(1)} %copy-done.3, bf16[64,5120]{1,0:T(8,128)(2,1)S(1)} %copy-done, bf16[64,5120]{1,0:T(8,128)(2,1)S(1)} %copy-done.1, ...), custom_call_target="tpu_custom_call" | custom-call | bytes 2621440 | tf_op jit(solution)/shard_map/cut/pallas_call | solution.py:147
  19.7 2.2 %collective-permute-start.1 = (bf16[2,64,1280]{2,1,0:T(8,128)(2,1)}, bf16[2,64,1280]{2,1,0:T(8,128)(2,1)S(1)}, u32[]{:S(2)}, u32[]{:S(2)}) collective-permute-start(bf16[2,64,1280]{2,1,0:T(8,128)(2,1)} %get-tuple-element.34), channel_id=1, source_target_pairs={{0,1},{1,0},{2,3},{3,2},{4,5},{5,4},{6,7},{7,6},{8,9},{9,8},{10,11... | collective-permute-start | bytes 983048 | tf_op jit(solution)/shard_map/ppermute | solution.py:379
  21.9 0.1 pad_add_fusion.refs_1_.meta
  21.9 0.0 collective-permute-done.2.refs_4_
  21.9 13.0 %collective-permute-done.3.refs_5_ = bf16[2,64,1280]{2,1,0:T(8,128)(2,1)S(1)} collective-permute-done((bf16[2,64,1280]{2,1,0:T(8,128)(2,1)}, bf16[2,64,1280]{2,1,0:T(8,128)(2,1)S(1)}, u32[]{:S(2)}, u32[]{:S(2)}) %collective-permute-start.3) | collective-permute-done | bytes 327712 | tf_op jit(solution)/shard_map/ppermute | solution.py:379
  34.9 0.6 order.1.refs_1_.mid
  35.5 0.0 copy-start.4
  35.6 4.8 %collective-permute-start.5 = (bf16[2,256,1280]{2,1,0:T(8,128)(2,1)S(1)}, bf16[2,256,1280]{2,1,0:T(8,128)(2,1)}, u32[]{:S(2)}, u32[]{:S(2)}) collective-permute-start(bf16[2,256,1280]{2,1,0:T(8,128)(2,1)S(1)} %order.1.refs_1_.mid), channel_id=1, source_target_pairs={{4,8},{8,4},{12,16},{16,12},{20,24},{24,20},{5,9},{9,5},{13,17},{1... | collective-permute-start | bytes 3932168 | tf_op jit(solution)/shard_map/ppermute | solution.py:387
  40.4 0.0 collective-permute-done.1.refs_0_.refs_1_
  40.4 0.1 again.1
  40.5 0.1 collective-permute-start.4
  40.6 0.1 collective-permute-start.6
  40.7 1.4 collective-permute-start.7
  42.0 0.1 copy.12.listed
  42.1 1.8 %tables.1 = (f32[256,128]{1,0:T(8,128)S(1)}, f32[256,128]{1,0:T(8,128)S(1)}, f32[64,256]{1,0:T(8,128)S(1)}, f32[64,256]{1,0:T(8,128)S(1)}) custom-call(bf16[2,64,1280]{2,1,0:T(8,128)(2,1)S(1)} %collective-permute-done.1.refs_0_.refs_1_, s32[2]{0:T(128)S(1)} %pad_add_fusion.refs_1_.meta, s32[16]{0:T(128)S(1)} %copy-done.3), custom_call_target="tpu_custom_call" | custom-call | bytes 262144 | tf_op jit(solution)/shard_map/tables/pallas_call | solution.py:173
  44.0 18.0 %collective-permute-done.6.refs_2_ = bf16[2,64,1280]{2,1,0:T(8,128)(2,1)} collective-permute-done((bf16[2,64,1280]{2,1,0:T(8,128)(2,1)}, bf16[2,64,1280]{2,1,0:T(8,128)(2,1)}, u32[]{:S(2)}, u32[]{:S(2)}) %collective-permute-start.6) | collective-permute-done | bytes 327712 | tf_op jit(solution)/shard_map/ppermute | solution.py:379
  62.0 9.1 %collective-permute-done.7.refs_3_ = bf16[2,64,1280]{2,1,0:T(8,128)(2,1)} collective-permute-done((bf16[2,64,1280]{2,1,0:T(8,128)(2,1)}, bf16[2,64,1280]{2,1,0:T(8,128)(2,1)}, u32[]{:S(2)}, u32[]{:S(2)}) %collective-permute-start.7) | collective-permute-done | bytes 327712 | tf_op jit(solution)/shard_map/ppermute | solution.py:379
  71.0 0.0 collective-permute-done.5.far
  71.0 0.0 collective-permute-done.4.near
  71.1 9.2 %attend.1 = (bf16[2,64,1280]{2,1,0:T(8,128)(2,1)S(1)}, bf16[2,64,1280]{2,1,0:T(8,128)(2,1)S(1)}, bf16[2,64,1280]{2,1,0:T(8,128)(2,1)S(1)}, bf16[2,64,1280]{2,1,0...) custom-call(s32[2]{0:T(128)S(1)} %pad_add_fusion.refs_1_.meta, ...), custom_call_target="tpu_custom_call" | custom-call | flops 3019898880 | bytes 13107200 | tf_op jit(solution)/shard_map/attend/pallas_call | solution.py:300
  80.2 4.0 %collective-permute-start.11 = (bf16[2,256,1280]{2,1,0:T(8,128)(2,1)S(1)}, bf16[2,256,1280]{2,1,0:T(8,128)(2,1)S(1)}, u32[]{:S(2)}, u32[]{:S(2)}) collective-permute-start(bf16[2,256,1280]{2,1,0:T(8,128)(2,1)S(1)} %get-tuple-element.52), channel_id=1, source_target_pairs={{4,8},{8,4},{12,16},{16,12},{20,24},{24,20},{5,9},{9,5},{13,17},{1... | collective-permute-start | bytes 3932168 | tf_op jit(solution)/shard_map/ppermute | solution.py:387
  84.2 0.1 collective-permute-start.12
  84.3 0.1 collective-permute-start.8
  84.4 1.3 collective-permute-start.9
  85.7 1.3 collective-permute-start.10
  87.0 26.3 %collective-permute-done.11.from_near = bf16[2,256,1280]{2,1,0:T(8,128)(2,1)S(1)} collective-permute-done((bf16[2,256,1280]{2,1,0:T(8,128)(2,1)S(1)}, bf16[2,256,1280]{2,1,0:T(8,128)(2,1)S(1)}, u32[]{:S(2)}, u32[]{:S(2)}) %collective-permute-start.11) | collective-permute-done | bytes 1310752 | tf_op jit(solution)/shard_map/ppermute | solution.py:387
  113.3 0.0 collective-permute-done.12.from_far
  113.3 1.2 combine.1
  114.5 0.1 collective-permute-start.15
  114.6 1.3 collective-permute-start.13
  115.9 0.0 collective-permute-done.8.refs_1_
  115.9 1.3 collective-permute-start.14
  117.2 0.0 collective-permute-done.9.refs_2_
  117.2 0.0 collective-permute-done.10.refs_3_
  117.2 1.7 %join.3 = (bf16[64,5120]{1,0:T(8,128)(2,1)}, bf16[64,5120]{1,0:T(8,128)(2,1)}) custom-call(s32[2]{0:T(128)S(1)} %pad_add_fusion.refs_1_.meta, bf16[2,64,1280]{2,1,0:T(8,128)(2,1)S(1)} %get-tuple-element.43.refs_0_, bf16[2,64,1280]{2,1,0:T(8,128)(2,1)S(1)} %collective-permute-done.8.refs_1_, bf16[2,64,1280]{2,1,0:T(8,128)(2,1)S(1)} %collective-permute-done.9.refs_2_, ...), custom_call_target="tpu_custom_call" | custom-call | bytes 2621440 | tf_op jit(solution)/shard_map/join/pallas_call | solution.py:361
  118.9 7.0 %collective-permute-done.15.refs_1_ = bf16[2,64,1280]{2,1,0:T(8,128)(2,1)S(1)} collective-permute-done((bf16[2,64,1280]{2,1,0:T(8,128)(2,1)S(1)}, bf16[2,64,1280]{2,1,0:T(8,128)(2,1)S(1)}, u32[]{:S(2)}, u32[]{:S(2)}) %collective-permute-start.15) | collective-permute-done | bytes 327712 | tf_op jit(solution)/shard_map/ppermute | solution.py:379
  125.9 1.4 join.4
  127.3 10.2 %collective-permute-done.13.refs_0_ = bf16[2,64,1280]{2,1,0:T(8,128)(2,1)S(1)} collective-permute-done((bf16[2,64,1280]{2,1,0:T(8,128)(2,1)S(1)}, bf16[2,64,1280]{2,1,0:T(8,128)(2,1)S(1)}, u32[]{:S(2)}, u32[]{:S(2)}) %collective-permute-start.13) | collective-permute-done | bytes 327712 | tf_op jit(solution)/shard_map/ppermute | solution.py:379
  137.5 7.6 %collective-permute-done.14.refs_1_ = bf16[2,64,1280]{2,1,0:T(8,128)(2,1)S(1)} collective-permute-done((bf16[2,64,1280]{2,1,0:T(8,128)(2,1)S(1)}, bf16[2,64,1280]{2,1,0:T(8,128)(2,1)S(1)}, u32[]{:S(2)}, u32[]{:S(2)}) %collective-permute-start.14) | collective-permute-done | bytes 327712 | tf_op jit(solution)/shard_map/ppermute | solution.py:379
  145.2 1.4 join.5
  (6 shorter events, 0.0 us)
Async XLA Ops:
  0.6 16.5 %copy-start.3 = (s32[16]{0:T(128)S(1)}, s32[16]{0:T(128)}, u32[]{:S(2)}) copy-start(s32[16]{0:T(128)} %refs_2_.1) | copy-start | bytes 196
  0.6 16.5 %copy-start.1 = (bf16[64,5120]{1,0:T(8,128)(2,1)S(1)}, bf16[64,5120]{1,0:T(8,128)(2,1)}, u32[]{:S(2)}) copy-start(bf16[64,5120]{1,0:T(8,128)(2,1)} %plain.3) | copy-start | bytes 1966084
  0.7 16.5 %copy-start = (bf16[64,5120]{1,0:T(8,128)(2,1)S(1)}, bf16[64,5120]{1,0:T(8,128)(2,1)}, u32[]{:S(2)}) copy-start(bf16[64,5120]{1,0:T(8,128)(2,1)} %turned.3) | copy-start | bytes 1966084
  4.0 30.9 %copy-start.2 = (bf16[2,64,1280]{2,1,0:T(8,128)(2,1)S(1)}, bf16[2,64,1280]{2,1,0:T(8,128)(2,1)}, u32[]{:S(2)}) copy-start(bf16[2,64,1280]{2,1,0:T(8,128)(2,1)} %get-tuple-element.38.refs_2_) | copy-start | bytes 983044
  4.0 13.2 %collective-permute-start = (bf16[2,64,1280]{2,1,0:T(8,128)(2,1)}, bf16[2,64,1280]{2,1,0:T(8,128)(2,1)S(1)}, u32[]{:S(2)}, u32[]{:S(2)}) collective-permute-start(bf16[2,64,1280]{2,1,0:T(8,128)(2,1)} %get-tuple-element.33), channel_id=1, source_target_pairs={{0,1},{1,0},{2,3},{3,2},{4,5},{5,4},{6,7},{7,6},{8,9},{9,8},{10,11... | collective-permute-start | bytes 983048 | tf_op jit(solution)/shard_map/ppermute | solution.py:379
  4.2 17.7 %collective-permute-start.2 = (bf16[2,64,1280]{2,1,0:T(8,128)(2,1)}, bf16[2,64,1280]{2,1,0:T(8,128)(2,1)S(1)}, u32[]{:S(2)}, u32[]{:S(2)}) collective-permute-start(bf16[2,64,1280]{2,1,0:T(8,128)(2,1)} %get-tuple-element.39), channel_id=1, source_target_pairs={{0,2},{1,3},{2,0},{3,1},{4,6},{5,7},{6,4},{7,5},{8,10},{9,11},{10,... | collective-permute-start | bytes 983048 | tf_op jit(solution)/shard_map/ppermute | solution.py:379
  6.5 28.4 %collective-permute-start.3 = (bf16[2,64,1280]{2,1,0:T(8,128)(2,1)}, bf16[2,64,1280]{2,1,0:T(8,128)(2,1)S(1)}, u32[]{:S(2)}, u32[]{:S(2)}) collective-permute-start(bf16[2,64,1280]{2,1,0:T(8,128)(2,1)} %get-tuple-element.40), channel_id=1, source_target_pairs={{0,3},{1,2},{2,1},{3,0},{4,7},{5,6},{6,5},{7,4},{8,11},{9,10},{10,... | collective-permute-start | bytes 983048 | tf_op jit(solution)/shard_map/ppermute | solution.py:379
  19.7 20.7 %collective-permute-start.1 = (bf16[2,64,1280]{2,1,0:T(8,128)(2,1)}, bf16[2,64,1280]{2,1,0:T(8,128)(2,1)S(1)}, u32[]{:S(2)}, u32[]{:S(2)}) collective-permute-start(bf16[2,64,1280]{2,1,0:T(8,128)(2,1)} %get-tuple-element.34), channel_id=1, source_target_pairs={{0,1},{1,0},{2,3},{3,2},{4,5},{5,4},{6,7},{7,6},{8,9},{9,8},{10,11... | collective-permute-start | bytes 983048 | tf_op jit(solution)/shard_map/ppermute | solution.py:379
  35.5 6.5 %copy-start.4 = (s32[16,4]{0,1:T(4,128)S(1)}, s32[16,4]{0,1:T(4,128)}, u32[]{:S(2)}) copy-start(s32[16,4]{0,1:T(4,128)} %param.11) | copy-start | bytes 772
  35.6 35.5 %collective-permute-start.5 = (bf16[2,256,1280]{2,1,0:T(8,128)(2,1)S(1)}, bf16[2,256,1280]{2,1,0:T(8,128)(2,1)}, u32[]{:S(2)}, u32[]{:S(2)}) collective-permute-start(bf16[2,256,1280]{2,1,0:T(8,128)(2,1)S(1)} %order.1.refs_1_.mid), channel_id=1, source_target_pairs={{4,8},{8,4},{12,16},{16,12},{20,24},{24,20},{5,9},{9,5},{13,17},{1... | collective-permute-start | bytes 3932168 | tf_op jit(solution)/shard_map/ppermute | solution.py:387
  40.5 30.5 %collective-permute-start.4 = (bf16[2,256,1280]{2,1,0:T(8,128)(2,1)S(1)}, bf16[2,256,1280]{2,1,0:T(8,128)(2,1)}, u32[]{:S(2)}, u32[]{:S(2)}) collective-permute-start(bf16[2,256,1280]{2,1,0:T(8,128)(2,1)S(1)} %again.1), channel_id=1, source_target_pairs={{0,4},{4,0},{8,12},{12,8},{16,20},{20,16},{24,28},{28,24},{1,5},{5... | collective-permute-start | bytes 3932168 | tf_op jit(solution)/shard_map/ppermute | solution.py:387
  40.6 21.4 %collective-permute-start.6 = (bf16[2,64,1280]{2,1,0:T(8,128)(2,1)}, bf16[2,64,1280]{2,1,0:T(8,128)(2,1)}, u32[]{:S(2)}, u32[]{:S(2)}) collective-permute-start(bf16[2,64,1280]{2,1,0:T(8,128)(2,1)} %get-tuple-element.41), channel_id=1, source_target_pairs={{0,2},{1,3},{2,0},{3,1},{4,6},{5,7},{6,4},{7,5},{8,10},{9,11},{10,... | collective-permute-start | bytes 983048 | tf_op jit(solution)/shard_map/ppermute | solution.py:379
  40.7 30.4 %collective-permute-start.7 = (bf16[2,64,1280]{2,1,0:T(8,128)(2,1)}, bf16[2,64,1280]{2,1,0:T(8,128)(2,1)}, u32[]{:S(2)}, u32[]{:S(2)}) collective-permute-start(bf16[2,64,1280]{2,1,0:T(8,128)(2,1)} %get-tuple-element.42), channel_id=1, source_target_pairs={{0,3},{1,2},{2,1},{3,0},{4,7},{5,6},{6,5},{7,4},{8,11},{9,10},{10,... | collective-permute-start | bytes 983048 | tf_op jit(solution)/shard_map/ppermute | solution.py:379
  80.2 33.0 %collective-permute-start.11 = (bf16[2,256,1280]{2,1,0:T(8,128)(2,1)S(1)}, bf16[2,256,1280]{2,1,0:T(8,128)(2,1)S(1)}, u32[]{:S(2)}, u32[]{:S(2)}) collective-permute-start(bf16[2,256,1280]{2,1,0:T(8,128)(2,1)S(1)} %get-tuple-element.52), channel_id=1, source_target_pairs={{4,8},{8,4},{12,16},{16,12},{20,24},{24,20},{5,9},{9,5},{13,17},{1... | collective-permute-start | bytes 3932168 | tf_op jit(solution)/shard_map/ppermute | solution.py:387
  84.2 29.1 %collective-permute-start.12 = (bf16[2,256,1280]{2,1,0:T(8,128)(2,1)S(1)}, bf16[2,256,1280]{2,1,0:T(8,128)(2,1)S(1)}, u32[]{:S(2)}, u32[]{:S(2)}) collective-permute-start(bf16[2,256,1280]{2,1,0:T(8,128)(2,1)S(1)} %get-tuple-element.53), channel_id=1, source_target_pairs={{0,4},{4,0},{8,12},{12,8},{16,20},{20,16},{24,28},{28,24},{1,5},{5... | collective-permute-start | bytes 3932168 | tf_op jit(solution)/shard_map/ppermute | solution.py:387
  84.3 31.6 %collective-permute-start.8 = (bf16[2,64,1280]{2,1,0:T(8,128)(2,1)S(1)}, bf16[2,64,1280]{2,1,0:T(8,128)(2,1)S(1)}, u32[]{:S(2)}, u32[]{:S(2)}) collective-permute-start(bf16[2,64,1280]{2,1,0:T(8,128)(2,1)S(1)} %get-tuple-element.44), channel_id=1, source_target_pairs={{0,1},{1,0},{2,3},{3,2},{4,5},{5,4},{6,7},{7,6},{8,9},{9,8},{10,11... | collective-permute-start | bytes 983048 | tf_op jit(solution)/shard_map/ppermute | solution.py:379
  84.4 32.9 %collective-permute-start.9 = (bf16[2,64,1280]{2,1,0:T(8,128)(2,1)S(1)}, bf16[2,64,1280]{2,1,0:T(8,128)(2,1)S(1)}, u32[]{:S(2)}, u32[]{:S(2)}) collective-permute-start(bf16[2,64,1280]{2,1,0:T(8,128)(2,1)S(1)} %get-tuple-element.45), channel_id=1, source_target_pairs={{0,2},{1,3},{2,0},{3,1},{4,6},{5,7},{6,4},{7,5},{8,10},{9,11},{10,... | collective-permute-start | bytes 983048 | tf_op jit(solution)/shard_map/ppermute | solution.py:379
  85.7 31.5 %collective-permute-start.10 = (bf16[2,64,1280]{2,1,0:T(8,128)(2,1)S(1)}, bf16[2,64,1280]{2,1,0:T(8,128)(2,1)S(1)}, u32[]{:S(2)}, u32[]{:S(2)}) collective-permute-start(bf16[2,64,1280]{2,1,0:T(8,128)(2,1)S(1)} %get-tuple-element.46), channel_id=1, source_target_pairs={{0,3},{1,2},{2,1},{3,0},{4,7},{5,6},{6,5},{7,4},{8,11},{9,10},{10,... | collective-permute-start | bytes 983048 | tf_op jit(solution)/shard_map/ppermute | solution.py:379
  114.5 11.4 %collective-permute-start.15 = (bf16[2,64,1280]{2,1,0:T(8,128)(2,1)S(1)}, bf16[2,64,1280]{2,1,0:T(8,128)(2,1)S(1)}, u32[]{:S(2)}, u32[]{:S(2)}) collective-permute-start(bf16[2,64,1280]{2,1,0:T(8,128)(2,1)S(1)} %get-tuple-element.57), channel_id=1, source_target_pairs={{0,1},{1,0},{2,3},{3,2},{4,5},{5,4},{6,7},{7,6},{8,9},{9,8},{10,11... | collective-permute-start | bytes 983048 | tf_op jit(solution)/shard_map/ppermute | solution.py:379
  114.6 22.9 %collective-permute-start.13 = (bf16[2,64,1280]{2,1,0:T(8,128)(2,1)S(1)}, bf16[2,64,1280]{2,1,0:T(8,128)(2,1)S(1)}, u32[]{:S(2)}, u32[]{:S(2)}) collective-permute-start(bf16[2,64,1280]{2,1,0:T(8,128)(2,1)S(1)} %get-tuple-element.54), channel_id=1, source_target_pairs={{0,2},{1,3},{2,0},{3,1},{4,6},{5,7},{6,4},{7,5},{8,10},{9,11},{10,... | collective-permute-start | bytes 983048 | tf_op jit(solution)/shard_map/ppermute | solution.py:379
  115.9 29.2 %collective-permute-start.14 = (bf16[2,64,1280]{2,1,0:T(8,128)(2,1)S(1)}, bf16[2,64,1280]{2,1,0:T(8,128)(2,1)S(1)}, u32[]{:S(2)}, u32[]{:S(2)}) collective-permute-start(bf16[2,64,1280]{2,1,0:T(8,128)(2,1)S(1)} %get-tuple-element.55), channel_id=1, source_target_pairs={{0,3},{1,2},{2,1},{3,0},{4,7},{5,6},{6,5},{7,4},{8,11},{9,10},{10,... | collective-permute-start | bytes 983048 | tf_op jit(solution)/shard_map/ppermute | solution.py:379
